TPU v7x, 32 devices: a whole 2x2x4 slice. The times are simulated.
32 devices in a mesh: dp: 4 (over y, x), fsdp: 8 (over z, core).
Axes of the slice: x: 2, y: 2, z: 4, core: 2. Of those that a mesh axis runs over, the one named last changes fastest.
Arguments:
- frames: bfloat16 [32768, 768], P(('dp', 'fsdp')), may hold values from -6 to 6
- cotangent: bfloat16 [32768, 768], P(('dp', 'fsdp')), may hold values from -6 to 6
- lengths: int32 [32, 7], P(('dp', 'fsdp')), may hold values from 0 to 780, as said below
- qkv_master: float32 [3, 768, 768], P(None, ('dp', 'fsdp')), may hold values from -0.21875 to 0.21875
- out_master: float32 [768, 768], P(('dp', 'fsdp')), may hold values from -1.5 to 1.5
- up_master: float32 [768, 3072], P(('dp', 'fsdp')), may hold values from -0.21875 to 0.21875
- down_master: float32 [3072, 768], P(('dp', 'fsdp')), may hold values from -0.109375 to 0.109375
- vector_master: float32 [9216], P(('dp', 'fsdp')), may hold values from -2 to 2, as said below
- qkv_first: float32 [3, 768, 768], P(None, ('dp', 'fsdp')), may hold values from -80 to 80
- qkv_second: float32 [3, 768, 768], P(None, ('dp', 'fsdp')), may hold values from 128.3457 to 2053.5312
- out_first: float32 [768, 768], P(('dp', 'fsdp')), may hold values from -14 to 14
- out_second: float32 [768, 768], P(('dp', 'fsdp')), may hold values from 4.5121536 to 72.19446
- up_first: float32 [768, 3072], P(('dp', 'fsdp')), may hold values from -56 to 56
- up_second: float32 [768, 3072], P(('dp', 'fsdp')), may hold values from 72.19446 to 1155.1113
- down_first: float32 [3072, 768], P(('dp', 'fsdp')), may hold values from -56 to 56
- down_second: float32 [3072, 768], P(('dp', 'fsdp')), may hold values from 72.19446 to 1155.1113
- vector_first: float32 [9216], P(('dp', 'fsdp')), may hold values from -96 to 96
- vector_second: float32 [9216], P(('dp', 'fsdp')), may hold values from 200.54016 to 3208.6426
Outputs:
- layer_output: bfloat16 [32768, 768], P(('dp', 'fsdp'))
- frames_grad: bfloat16 [32768, 768], P(('dp', 'fsdp'))
- layer_rms: float32 [4], replicated
- qkv_first_new: float32 [3, 768, 768], P(None, ('dp', 'fsdp'))
- qkv_second_new: float32 [3, 768, 768], P(None, ('dp', 'fsdp'))
- qkv_master_new: float32 [3, 768, 768], P(None, ('dp', 'fsdp'))
- qkv_weight_low: bfloat16 [3, 768, 768], P(None, ('dp', 'fsdp'))
- out_first_new: float32 [768, 768], P(('dp', 'fsdp'))
- out_second_new: float32 [768, 768], P(('dp', 'fsdp'))
- out_master_new: float32 [768, 768], P(('dp', 'fsdp'))
- out_weight_low: bfloat16 [768, 768], P(('dp', 'fsdp'))
- up_first_new: float32 [768, 3072], P(('dp', 'fsdp'))
- up_second_new: float32 [768, 3072], P(('dp', 'fsdp'))
- up_master_new: float32 [768, 3072], P(('dp', 'fsdp'))
- up_weight_low: bfloat16 [768, 3072], P(('dp', 'fsdp'))
- down_first_new: float32 [3072, 768], P(('dp', 'fsdp'))
- down_second_new: float32 [3072, 768], P(('dp', 'fsdp'))
- down_master_new: float32 [3072, 768], P(('dp', 'fsdp'))
- down_weight_low: bfloat16 [3072, 768], P(('dp', 'fsdp'))
- vector_first_new: float32 [9216], P(('dp', 'fsdp'))
- vector_second_new: float32 [9216], P(('dp', 'fsdp'))
- vector_master_new: float32 [9216], P(('dp', 'fsdp'))
- vector_weight_low: bfloat16 [9216], P(('dp', 'fsdp'))
Inputs may be any that keep to these rules, and one draw needn't show every extreme that they name: Each row holds 780 or 0 in its first slot, then some entries 150, then zeros; it has at least one clip, and its lengths sum to at most 900, which some row reaches. `vector_master`: the gain entries (g_1, g_2) lie between 0.5 and 1.5.
All inputs are finite; a program needn't handle non-finite values.
Results may differ from a plain program's by a relative error of at most 0.015.
The roundings to bfloat16 on the way count: a program that leaves them out, or rounds other values in their place, can miss the bound.
Values may be sent and summed in bfloat16 or wider, within the bound.
No kernel may reach another device: no remote copies, remote signals or barrier semaphores. Data moves between devices by JAX's collectives and lax.ppermute only.
A program may use at most 256 MiB of HBM per device.

v0:
```python
from functools import partial

import jax
import jax.numpy as jnp
from jax import lax
from jax.sharding import PartitionSpec as P

HEADS = 12
QBLK = 512
STEP = 10


NEGATIVE = -1e30
NORM_EPS = 1e-05
SCORE_SCALE = 0.125
BETA_FIRST = 0.9
BETA_SECOND = 0.98
ADAM_EPS = 1e-06
MATRIX_RATE = 0.05
VECTOR_RATE = 0.3
WEIGHT_DECAY = 0.01


def clip_segments(length_row, frame_count):
    clip_ends = jnp.cumsum(length_row)
    position = jnp.arange(frame_count, dtype=jnp.int32)
    segment = jnp.sum((clip_ends[None, :] <= position[:, None]).astype(jnp.int32), axis=1)
    valid_rows = (position < clip_ends[-1]).astype(jnp.float32)
    return (segment, valid_rows)


def split_vector(vector, model_width, hidden_width):
    pieces = [
        vector[piece_index * model_width : (piece_index + 1) * model_width]
        for piece_index in range(8)
    ]
    return (pieces, vector[8 * model_width : 8 * model_width + hidden_width])


def normalize(hidden):
    row_mean = jnp.mean(hidden, axis=-1, keepdims=True)
    centred = hidden - row_mean
    variance = jnp.mean(centred * centred, axis=-1, keepdims=True)
    inverse = lax.rsqrt(variance + NORM_EPS)
    return (centred * inverse, inverse)


def norm_backward(grad_output, normal_hat, inverse, norm_gain):
    scaled = grad_output * norm_gain
    return inverse * (
        scaled
        - jnp.mean(scaled, axis=-1, keepdims=True)
        - normal_hat * jnp.mean(scaled * normal_hat, axis=-1, keepdims=True)
    )


def adam_update(master, first, second, gradient, step_rate, decay_rate):
    first_new = BETA_FIRST * first + (1.0 - BETA_FIRST) * gradient
    second_new = BETA_SECOND * second + (1.0 - BETA_SECOND) * gradient * gradient
    first_hat = first_new / (1.0 - BETA_FIRST**STEP)
    second_hat = second_new / (1.0 - BETA_SECOND**STEP)
    updated = master - step_rate * (
        first_hat / (jnp.sqrt(second_hat) + ADAM_EPS) + decay_rate * master
    )
    return (first_new, second_new, updated, updated.astype(jnp.bfloat16))


def shards(
    frames,
    cotangent,
    lengths,
    qkv_master,
    out_master,
    up_master,
    down_master,
    vector_master,
    qkv_first,
    qkv_second,
    out_first,
    out_second,
    up_first,
    up_second,
    down_first,
    down_second,
    vector_first,
    vector_second,
):
    frame_count = frames.shape[0]
    model_width = frames.shape[1]
    head_size = model_width // HEADS
    segment, valid_rows = clip_segments(lengths[0], frame_count)
    low_shards = (
        qkv_master.astype(jnp.bfloat16),
        out_master.astype(jnp.bfloat16),
        up_master.astype(jnp.bfloat16),
        down_master.astype(jnp.bfloat16),
        vector_master.astype(jnp.bfloat16),
    )
    gathered = (
        lax.all_gather(low_shards[0], ("dp", "fsdp"), axis=1, tiled=True),
        lax.all_gather(low_shards[1], ("dp", "fsdp"), axis=0, tiled=True),
        lax.all_gather(low_shards[2], ("dp", "fsdp"), axis=0, tiled=True),
        lax.all_gather(low_shards[3], ("dp", "fsdp"), axis=0, tiled=True),
        lax.all_gather(low_shards[4], ("dp", "fsdp"), axis=0, tiled=True),
    )
    qkv_full, out_full, up_full, down_full, vector_full = gathered
    hidden_width = up_full.shape[1]
    pieces, bias_up = split_vector(vector_full.astype(jnp.float32), model_width, hidden_width)
    (
        bias_query,
        bias_value,
        bias_out,
        bias_down,
        gain_first,
        shift_first,
        gain_second,
        shift_second,
    ) = pieces
    projected = jnp.einsum("fd,cde->cfe", frames, qkv_full, preferred_element_type=jnp.float32)
    queries = (
        (projected[0] + bias_query).astype(jnp.bfloat16).reshape(frame_count, HEADS, head_size)
    )
    keys_heads = projected[1].astype(jnp.bfloat16).reshape(frame_count, HEADS, head_size)
    values_heads = (
        (projected[2] + bias_value).astype(jnp.bfloat16).reshape(frame_count, HEADS, head_size)
    )
    block_rows = QBLK
    block_count = frame_count // block_rows
    query_blocks = queries.reshape(block_count, block_rows, HEADS, head_size)
    segment_blocks = segment.reshape(block_count, block_rows)

    def masked_scores(query_block, segment_block):
        scores = (
            jnp.einsum("qhd,khd->hqk", query_block, keys_heads, preferred_element_type=jnp.float32)
            * SCORE_SCALE
        )
        allowed = segment_block[None, :, None] == segment[None, None, :]
        return jnp.where(allowed, scores, NEGATIVE)

    def forward_block(inputs):
        query_block, segment_block = inputs
        scores = masked_scores(query_block, segment_block)
        maximum = jnp.max(scores, axis=-1, keepdims=True)
        raised = jnp.exp(scores - maximum)
        row_total = jnp.sum(raised, axis=-1, keepdims=True)
        weights_low = (raised / row_total).astype(jnp.bfloat16)
        context_block = jnp.einsum(
            "hqk,khd->qhd", weights_low, values_heads, preferred_element_type=jnp.float32
        )
        return (context_block, (maximum + jnp.log(row_total))[..., 0])

    context_blocks, log_totals = lax.map(forward_block, (query_blocks, segment_blocks))
    context = context_blocks.reshape(frame_count, model_width).astype(jnp.bfloat16)
    attended = jnp.dot(context, out_full, preferred_element_type=jnp.float32) + bias_out
    first_sum = frames.astype(jnp.float32) + attended
    first_hat, first_inverse = normalize(first_sum)
    normed = (first_hat * gain_first + shift_first).astype(jnp.bfloat16)
    up_pre = jnp.dot(normed, up_full, preferred_element_type=jnp.float32) + bias_up
    activated = jax.nn.gelu(up_pre, approximate=False).astype(jnp.bfloat16)
    down_out = jnp.dot(activated, down_full, preferred_element_type=jnp.float32) + bias_down
    second_sum = normed.astype(jnp.float32) + down_out
    second_hat, second_inverse = normalize(second_sum)
    result = (second_hat * gain_second + shift_second).astype(jnp.bfloat16)
    valid_column = valid_rows[:, None]
    squares = jnp.stack(
        [
            jnp.sum(valid_column * attended * attended),
            jnp.sum(valid_column * first_sum * first_sum),
            jnp.sum(valid_column * down_out * down_out),
            jnp.sum(valid_column * second_sum * second_sum),
        ]
    )
    counted = jnp.sum(valid_rows) * model_width
    square_total, count_total = lax.psum((squares, counted), ("dp", "fsdp"))
    layer_rms = jnp.sqrt(square_total / count_total)
    back_full = (
        lax.all_gather(low_shards[0], ("dp", "fsdp"), axis=1, tiled=True),
        lax.all_gather(low_shards[1], ("dp", "fsdp"), axis=0, tiled=True),
        lax.all_gather(low_shards[2], ("dp", "fsdp"), axis=0, tiled=True),
        lax.all_gather(low_shards[3], ("dp", "fsdp"), axis=0, tiled=True),
        lax.all_gather(low_shards[4], ("dp", "fsdp"), axis=0, tiled=True),
    )
    qkv_back, out_back, up_back, down_back, vector_back = back_full
    back_pieces, unused = split_vector(vector_back.astype(jnp.float32), model_width, hidden_width)
    gain_first_back = back_pieces[4]
    gain_second_back = back_pieces[6]
    grad_result = cotangent.astype(jnp.float32) * valid_column
    grad_second = norm_backward(grad_result, second_hat, second_inverse, gain_second_back)
    grad_gain_second = jnp.sum(grad_result * second_hat, axis=0)
    grad_shift_second = jnp.sum(grad_result, axis=0)
    grad_down_out = grad_second.astype(jnp.bfloat16)
    grad_down_weight = jnp.einsum(
        "fh,fd->hd", activated, grad_down_out, preferred_element_type=jnp.float32
    )
    grad_bias_down = jnp.sum(grad_down_out.astype(jnp.float32), axis=0)
    grad_activated = jnp.einsum(
        "fd,hd->fh", grad_down_out, down_back, preferred_element_type=jnp.float32
    )
    ignored, gelu_pull = jax.vjp(partial(jax.nn.gelu, approximate=False), up_pre)
    grad_up_pre = gelu_pull(grad_activated)[0].astype(jnp.bfloat16)
    grad_up_weight = jnp.einsum(
        "fd,fh->dh", normed, grad_up_pre, preferred_element_type=jnp.float32
    )
    grad_bias_up = jnp.sum(grad_up_pre.astype(jnp.float32), axis=0)
    grad_normed = grad_second + jnp.einsum(
        "fh,dh->fd", grad_up_pre, up_back, preferred_element_type=jnp.float32
    )
    grad_first = norm_backward(grad_normed, first_hat, first_inverse, gain_first_back)
    grad_gain_first = jnp.sum(grad_normed * first_hat, axis=0)
    grad_shift_first = jnp.sum(grad_normed, axis=0)
    grad_attended = grad_first.astype(jnp.bfloat16)
    grad_out_weight = jnp.einsum(
        "fe,fd->ed", context, grad_attended, preferred_element_type=jnp.float32
    )
    grad_bias_out = jnp.sum(grad_attended.astype(jnp.float32), axis=0)
    grad_context = jnp.einsum(
        "fd,ed->fe", grad_attended, out_back, preferred_element_type=jnp.float32
    )
    grad_context = grad_context.astype(jnp.bfloat16).reshape(
        block_count, block_rows, HEADS, head_size
    )

    def backward_block(running, inputs):
        key_sum, value_sum = running
        query_block, segment_block, log_block, grad_block = inputs
        scores = masked_scores(query_block, segment_block)
        probabilities = jnp.exp(scores - log_block[..., None])
        probabilities_low = probabilities.astype(jnp.bfloat16)
        grad_probabilities = jnp.einsum(
            "qhd,khd->hqk", grad_block, values_heads, preferred_element_type=jnp.float32
        )
        row_inner = jnp.sum(probabilities * grad_probabilities, axis=-1, keepdims=True)
        grad_scores = (probabilities * (grad_probabilities - row_inner)).astype(jnp.bfloat16)
        grad_query = (
            jnp.einsum("hqk,khd->qhd", grad_scores, keys_heads, preferred_element_type=jnp.float32)
            * SCORE_SCALE
        )
        key_sum = (
            key_sum
            + jnp.einsum(
                "hqk,qhd->khd", grad_scores, query_block, preferred_element_type=jnp.float32
            )
            * SCORE_SCALE
        )
        value_sum = value_sum + jnp.einsum(
            "hqk,qhd->khd", probabilities_low, grad_block, preferred_element_type=jnp.float32
        )
        return ((key_sum, value_sum), grad_query)

    zero_heads = jnp.zeros((frame_count, HEADS, head_size), jnp.float32)
    (grad_keys, grad_values), grad_query_blocks = lax.scan(
        backward_block,
        (zero_heads, zero_heads),
        (query_blocks, segment_blocks, log_totals, grad_context),
    )
    grad_projected = jnp.stack(
        [
            grad_query_blocks.reshape(frame_count, model_width),
            grad_keys.reshape(frame_count, model_width),
            grad_values.reshape(frame_count, model_width),
        ]
    ).astype(jnp.bfloat16)
    grad_qkv_weight = jnp.einsum(
        "fd,cfe->cde", frames, grad_projected, preferred_element_type=jnp.float32
    )
    grad_bias_query = jnp.sum(grad_projected[0].astype(jnp.float32), axis=0)
    grad_bias_value = jnp.sum(grad_projected[2].astype(jnp.float32), axis=0)
    frames_grad = (
        grad_first
        + jnp.einsum("cfe,cde->fd", grad_projected, qkv_back, preferred_element_type=jnp.float32)
    ).astype(jnp.bfloat16)
    grad_vector = jnp.concatenate(
        [
            grad_bias_query,
            grad_bias_value,
            grad_bias_out,
            grad_bias_down,
            grad_gain_first,
            grad_shift_first,
            grad_gain_second,
            grad_shift_second,
            grad_bias_up,
        ]
    )
    shares = (
        lax.psum_scatter(grad_qkv_weight, ("dp", "fsdp"), scatter_dimension=1, tiled=True),
        lax.psum_scatter(grad_out_weight, ("dp", "fsdp"), scatter_dimension=0, tiled=True),
        lax.psum_scatter(grad_up_weight, ("dp", "fsdp"), scatter_dimension=0, tiled=True),
        lax.psum_scatter(grad_down_weight, ("dp", "fsdp"), scatter_dimension=0, tiled=True),
        lax.psum_scatter(grad_vector, ("dp", "fsdp"), scatter_dimension=0, tiled=True),
    )
    qkv_new = adam_update(qkv_master, qkv_first, qkv_second, shares[0], MATRIX_RATE, WEIGHT_DECAY)
    out_new = adam_update(out_master, out_first, out_second, shares[1], MATRIX_RATE, WEIGHT_DECAY)
    up_new = adam_update(up_master, up_first, up_second, shares[2], MATRIX_RATE, WEIGHT_DECAY)
    down_new = adam_update(
        down_master, down_first, down_second, shares[3], MATRIX_RATE, WEIGHT_DECAY
    )
    vector_new = adam_update(
        vector_master, vector_first, vector_second, shares[4], VECTOR_RATE, 0.0
    )
    return (
        result,
        frames_grad,
        layer_rms,
        qkv_new[0],
        qkv_new[1],
        qkv_new[2],
        qkv_new[3],
        out_new[0],
        out_new[1],
        out_new[2],
        out_new[3],
        up_new[0],
        up_new[1],
        up_new[2],
        up_new[3],
        down_new[0],
        down_new[1],
        down_new[2],
        down_new[3],
        vector_new[0],
        vector_new[1],
        vector_new[2],
        vector_new[3],
    )


def solution(mesh):
    return jax.shard_map(
        shards,
        mesh=mesh,
        in_specs=(
            P(("dp", "fsdp"), None),
            P(("dp", "fsdp"), None),
            P(("dp", "fsdp"), None),
            P(None, ("dp", "fsdp"), None),
            P(("dp", "fsdp"), None),
            P(("dp", "fsdp"), None),
            P(("dp", "fsdp"), None),
            P(("dp", "fsdp")),
            P(None, ("dp", "fsdp"), None),
            P(None, ("dp", "fsdp"), None),
            P(("dp", "fsdp"), None),
            P(("dp", "fsdp"), None),
            P(("dp", "fsdp"), None),
            P(("dp", "fsdp"), None),
            P(("dp", "fsdp"), None),
            P(("dp", "fsdp"), None),
            P(("dp", "fsdp")),
            P(("dp", "fsdp")),
        ),
        out_specs=(
            P(("dp", "fsdp"), None),
            P(("dp", "fsdp"), None),
            P(),
            P(None, ("dp", "fsdp"), None),
            P(None, ("dp", "fsdp"), None),
            P(None, ("dp", "fsdp"), None),
            P(None, ("dp", "fsdp"), None),
            P(("dp", "fsdp"), None),
            P(("dp", "fsdp"), None),
            P(("dp", "fsdp"), None),
            P(("dp", "fsdp"), None),
            P(("dp", "fsdp"), None),
            P(("dp", "fsdp"), None),
            P(("dp", "fsdp"), None),
            P(("dp", "fsdp"), None),
            P(("dp", "fsdp"), None),
            P(("dp", "fsdp"), None),
            P(("dp", "fsdp"), None),
            P(("dp", "fsdp"), None),
            P(("dp", "fsdp")),
            P(("dp", "fsdp")),
            P(("dp", "fsdp")),
            P(("dp", "fsdp")),
        ),
        check_vma=False,
    )
```

profile of v0, /device:TPU:0, one launch (start us, length us, event | category | flops | bytes accessed | tf_op | source)
XLA Modules:
  0.0 1017.4 jit_solution(6643861059221315501)
XLA Ops:
  14.9 42.4 %all-reduce = bf16[9216]{0:T(1024)(128)(2,1)S(1)} all-reduce(bf16[9216]{0:T(1024)(128)(2,1)S(1)} %dynamic-update-slice), channel_id=1, replica_groups=mesh['dp'=4,'fsdp'=8] {'dp','fsdp'}, use_global_device_ids=true, to_apply=%add | all-reduce | flops 9216 | bytes 36864
  95.7 73.6 %while.27 = (s32[]{:T(128)}, bf16[2,512,12,64]{1,3,2,0:T(8,128)(2,1)}, f32[2,12,512]{2,1,0:T(8,128)S(1)}, s32[2,512]{1,0:T(2,128)S(1)}, s32[1024]{0:T(1024)S(1)}...) while((s32[]{:T(128)}, ...), condition=%wide.region_5.6_spmd, body=%wide.region_2.5_spmd.sunk | while | flops 1686628352 | bytes 183995504 | solution.py:152
  96.5 12.0 %fusion.119 = (f32[12,512]{1,0:T(8,128)S(1)}, f32[12,512,1024]{2,1,0:T(8,128)}) fusion(pred[512,1024]{1,0:T(8,128)(4,1)S(1)} %broadcast_compare_fusion.4, bf16[1024,12,64]{0,2,1:T(8,128)(2,1)S(1)} %get-tuple-element.592, bf16[2,512,12,64]{1,3,2,0:T(8,128)(2,1)} %get-tuple-element.591, s32[]{:T(128)} %get-tuple-element.577), kind=kOutput, calls=%fused_computation.3.clone.1 | convolution fusion | flops 824174592 | bytes 28074496 | tf_op jit(solution)/shard_map/while/body/eval_jaxpr/qhd,khd->hqk/dot_general | solution.py:134
  108.5 12.4 %fusion.120 = f32[12,512]{1,0:T(8,128)S(1)} fusion(f32[12,512,1024]{2,1,0:T(8,128)} %get-tuple-element.553, f32[12,512]{1,0:T(8,128)S(1)} %get-tuple-element.554, pred[512,1024]{1,0:T(8,128)(4,1)S(1)} %broadcast_compare_fusion.4), kind=kLoop, calls=%fused_computation.4.clone.1 | loop fusion | flops 25159680 | bytes 25739264 | tf_op jit(solution)/shard_map/while/body/eval_jaxpr/reduce_sum | solution.py:145
  133.0 12.1 %fusion.119 = (f32[12,512]{1,0:T(8,128)S(1)}, f32[12,512,1024]{2,1,0:T(8,128)}) fusion(pred[512,1024]{1,0:T(8,128)(4,1)S(1)} %broadcast_compare_fusion.4, bf16[1024,12,64]{0,2,1:T(8,128)(2,1)S(1)} %get-tuple-element.592, bf16[2,512,12,64]{1,3,2,0:T(8,128)(2,1)} %get-tuple-element.591, s32[]{:T(128)} %get-tuple-element.577), kind=kOutput, calls=%fused_computation.3.clone.1 | convolution fusion | flops 824174592 | bytes 28074496 | tf_op jit(solution)/shard_map/while/body/eval_jaxpr/qhd,khd->hqk/dot_general | solution.py:134
  145.2 12.3 %fusion.120 = f32[12,512]{1,0:T(8,128)S(1)} fusion(f32[12,512,1024]{2,1,0:T(8,128)} %get-tuple-element.553, f32[12,512]{1,0:T(8,128)S(1)} %get-tuple-element.554, pred[512,1024]{1,0:T(8,128)(4,1)S(1)} %broadcast_compare_fusion.4), kind=kLoop, calls=%fused_computation.4.clone.1 | loop fusion | flops 25159680 | bytes 25739264 | tf_op jit(solution)/shard_map/while/body/eval_jaxpr/reduce_sum | solution.py:145
  181.3 16.6 %all-gather.9.cloned.1.call-done = bf16[768,3072]{1,0:T(8,128)(2,1)} async-done(((bf16[24,3072]{1,0:T(8,128)(2,1)}), bf16[768,3072]{1,0:T(8,128)(2,1)}) %all-gather.9.cloned.1.call-update) | async-done | bytes 4718608 | tf_op jit(solution)/shard_map/all_gather | solution.py:102
  197.8 37.7 %multiply_convert_fusion.1 = (bf16[1024,3072]{1,0:T(8,128)(2,1)}, f32[1024,3072]{1,0:T(8,128)}, f32[1024,3072]{1,0:T(8,128)}) fusion(f32[3072]{0:T(1024)S(1)} %copy-done.54, bf16[768,3072]{1,0:T(8,128)(2,1)} %all-gather.9.cloned.1.call-done, f32[1024,768]{0,1:T(8,128)S(1)} %get-tuple-element.420, f32[768]{0:T(1024)S(1)} %copy-done.56, ...), kind=kOutput, calls=%fused_computation.48 | convolution fusion | flops 5043388416 | bytes 39348224 | tf_op jit(solution)/shard_map/dot_general | solution.py:158
  235.6 28.2 %all-gather.11.cloned.1.call-done = bf16[3072,768]{1,0:T(8,128)(2,1)} async-done(((bf16[96,768]{1,0:T(8,128)(2,1)}), bf16[3072,768]{1,0:T(8,128)(2,1)}) %all-gather.11.cloned.1.call-update) | async-done | bytes 4718608 | tf_op jit(solution)/shard_map/all_gather | solution.py:103
  282.0 18.0 %convert_reduce_fusion = (f32[3072]{0:T(1024)}, bf16[1024,3072]{1,0:T(8,128)(2,1)}) fusion(f32[1024,3072]{1,0:T(8,128)} %get-tuple-element.418, bf16[1024,768]{0,1:T(8,128)(2,1)S(1)} %get-tuple-element.410, bf16[3072,768]{1,0:T(8,128)(2,1)} %all-gather.11.cloned.1.call-done, f32[1024,3072]{1,0:T(8,128)} %get-tuple-element.437, f32[3072]{0:T(1024)S(1)} %copy-done.54), kind=kOutput, calls=%fused_computation.46 | convolution fusion | flops 4885312512 | bytes 37773312 | tf_op jit(solution)/shard_map/fd,hd->fh/dot_general | solution.py:196
  300.0 14.9 %multiply_reduce_fusion.2 = (f32[768]{0:T(1024)}, f32[1024]{0:T(1024)S(1)}, f32[1024]{0:T(1024)S(1)}, f32[768]{0:T(1024)}, f32[]{:T(128)}, /*index=5*/f32[]{:T(128)}, f32[]{:T(128)}, f32[1024,768]{0,1:T(8,128)S(1)}) fusion(f32[1024,768]{0,1:T(8,128)} %copy-done.8, f32[1024]{0:T(1024)S(1)} %add_rsqrt_fusion.1, f32[1024]{0:T(1024)S(1)} %broadcast_multiply_fusion.5, ...), kind=kOutput, calls=%fused_computation.78 | convolution fusion | flops 4855427072 | bytes 28366860 | tf_op jit(solution)/shard_map/fh,dh->fd/dot_general | solution.py:205
  329.2 169.5 %while.28 = (s32[]{:T(128)}, f32[1024,12,64]{0,2,1:T(8,128)}, f32[1024,12,64]{0,2,1:T(8,128)}, bf16[2,512,12,64]{1,3,2,0:T(8,128)(2,1)}, bf16[2,512,12,64]{1,3,2...) while((s32[]{:T(128)}, f32[1024,12,64]{0,2,1:T(8,128)}, ...), condition=%wide.region_16.17_spmd.clone, body=%wide.region_14.16_spmd.clone.sunk | while | flops 4125747200 | bytes 213045904 | solution.py:251
  329.4 11.6 %fusion.130 = f32[12,512,1024]{2,1,0:T(8,128)} fusion(bf16[1024,12,64]{0,2,1:T(8,128)(2,1)S(1)} %get-tuple-element.628, bf16[2,512,12,64]{1,3,2,0:T(8,128)(2,1)} %get-tuple-element.625, s32[]{:T(128)} %get-tuple-element.608), kind=kOutput, calls=%fused_computation.30.clone.1 | convolution fusion | flops 805306368 | bytes 27525632 | tf_op jit(solution)/shard_map/while/body/eval_jaxpr/qhd,khd->hqk/dot_general | solution.py:134
  341.4 18.3 %multiply_reduce_fusion.9 = (f32[12,512]{1,0:T(8,128)S(1)}, f32[12,512,1024]{2,1,0:T(8,128)}) fusion(f32[12,512,1024]{2,1,0:T(8,128)} %fusion.130, f32[12,512]{1,0:T(8,128)S(1)} %dynamic-slice_bitcast_fusion.2, pred[512,1024]{1,0:T(8,128)(4,1)S(1)} %broadcast_compare_fusion.5, bf16[1024,12,64]{0,2,1:T(8,128)(2,1)} %get-tuple-element.631, ...), kind=kOutput, calls=%fused_computation.17.clone.1 | convolution fusion | flops 836757504 | bytes 53264896 | tf_op jit(solution)/shard_map/while/body/eval_jaxpr/qhd,khd->hqk/dot_general | solution.py:229
  359.7 22.1 %multiply_convert_fusion.3 = bf16[12,512,1024]{2,1,0:T(8,128)(2,1)} fusion(f32[12,512,1024]{2,1,0:T(8,128)} %get-tuple-element.566, f32[12,512,1024]{2,1,0:T(8,128)} %fusion.130, f32[12,512]{1,0:T(8,128)S(1)} %get-tuple-element.567, f32[12,512]{1,0:T(8,128)S(1)} %dynamic-slice_bitcast_fusion.2, pred[512,1024]{1,0:T(8,128)(4,1)S(1)} %broadcast_compare_fusion.5), kind=kLoop, calls=%fused_computation.16.clone.1 | loop fusion | flops 37748736 | bytes 63488000 | tf_op jit(solution)/shard_map/while/body/eval_jaxpr/convert_element_type | solution.py:233
  400.1 13.7 %bitcast_add_fusion.6 = f32[1024,12,64]{0,2,1:T(8,128)} fusion(f32[1024,12,64]{0,2,1:T(8,128)} %get-tuple-element.610, f32[12,512,1024]{2,1,0:T(8,128)} %fusion.130, f32[12,512]{1,0:T(8,128)S(1)} %dynamic-slice_bitcast_fusion.2, pred[512,1024]{1,0:T(8,128)(4,1)S(1)} %broadcast_compare_fusion.5, pred[]{:T(512)S(6)} %compare.3, ...), kind=kOutput, calls=%fused_computation.22.clone.1 | convolution fusion | flops 832045056 | bytes 32793088 | tf_op jit(solution)/shard_map/while/body/eval_jaxpr/hqk,qhd->khd/dot_general | solution.py:245
  413.8 11.4 %fusion.130 = f32[12,512,1024]{2,1,0:T(8,128)} fusion(bf16[1024,12,64]{0,2,1:T(8,128)(2,1)S(1)} %get-tuple-element.628, bf16[2,512,12,64]{1,3,2,0:T(8,128)(2,1)} %get-tuple-element.625, s32[]{:T(128)} %get-tuple-element.608), kind=kOutput, calls=%fused_computation.30.clone.1 | convolution fusion | flops 805306368 | bytes 27525632 | tf_op jit(solution)/shard_map/while/body/eval_jaxpr/qhd,khd->hqk/dot_general | solution.py:134
  425.7 18.1 %multiply_reduce_fusion.9 = (f32[12,512]{1,0:T(8,128)S(1)}, f32[12,512,1024]{2,1,0:T(8,128)}) fusion(f32[12,512,1024]{2,1,0:T(8,128)} %fusion.130, f32[12,512]{1,0:T(8,128)S(1)} %dynamic-slice_bitcast_fusion.2, pred[512,1024]{1,0:T(8,128)(4,1)S(1)} %broadcast_compare_fusion.5, bf16[1024,12,64]{0,2,1:T(8,128)(2,1)} %get-tuple-element.631, ...), kind=kOutput, calls=%fused_computation.17.clone.1 | convolution fusion | flops 836757504 | bytes 53264896 | tf_op jit(solution)/shard_map/while/body/eval_jaxpr/qhd,khd->hqk/dot_general | solution.py:229
  443.8 21.2 %multiply_convert_fusion.3 = bf16[12,512,1024]{2,1,0:T(8,128)(2,1)} fusion(f32[12,512,1024]{2,1,0:T(8,128)} %get-tuple-element.566, f32[12,512,1024]{2,1,0:T(8,128)} %fusion.130, f32[12,512]{1,0:T(8,128)S(1)} %get-tuple-element.567, f32[12,512]{1,0:T(8,128)S(1)} %dynamic-slice_bitcast_fusion.2, pred[512,1024]{1,0:T(8,128)(4,1)S(1)} %broadcast_compare_fusion.5), kind=kLoop, calls=%fused_computation.16.clone.1 | loop fusion | flops 37748736 | bytes 63488000 | tf_op jit(solution)/shard_map/while/body/eval_jaxpr/convert_element_type | solution.py:233
  484.1 14.5 %bitcast_add_fusion.6 = f32[1024,12,64]{0,2,1:T(8,128)} fusion(f32[1024,12,64]{0,2,1:T(8,128)} %get-tuple-element.610, f32[12,512,1024]{2,1,0:T(8,128)} %fusion.130, f32[12,512]{1,0:T(8,128)S(1)} %dynamic-slice_bitcast_fusion.2, pred[512,1024]{1,0:T(8,128)(4,1)S(1)} %broadcast_compare_fusion.5, pred[]{:T(512)S(6)} %compare.3, ...), kind=kOutput, calls=%fused_computation.22.clone.1 | convolution fusion | flops 832045056 | bytes 32793088 | tf_op jit(solution)/shard_map/while/body/eval_jaxpr/hqk,qhd->khd/dot_general | solution.py:245
  564.2 42.0 %all-reduce.3 = (f32[4]{0:T(128)S(1)}, f32[]{:T(128)}, f32[9216]{0:T(1024)S(1)}) all-reduce(f32[4]{0:T(128)S(1)} %pad_maximum_fusion.5, f32[]{:T(128)S(6)} %mul.428, f32[9216]{0:T(1024)S(1)} %constant_dynamic-update-slice_fusion), channel_id=1, replica_groups=mesh['dp'=4,'fsdp'=8] {'dp','fsdp'}, use_global_device_ids=true, to_apply=%region_21.22 | all-reduce | flops 9221 | bytes 73768 | tf_op jit(solution)/shard_map/psum | solution.py:174
  623.3 101.9 %all-reduce.6.cloned.1.call-done = f32[3,768,768]{2,0,1:T(4,128)} async-done(((f32[3,768,768]{2,0,1:T(4,128)}), f32[3,768,768]{2,0,1:T(4,128)}) %all-reduce.6.cloned.1.call-update) | async-done | bytes 7077904
  727.2 139.6 %reduce-scatter.8.cloned.1.call-done = f32[96,768]{1,0:T(8,128)} async-done(((f32[3072,768]{1,0:T(8,128)}), f32[96,768]{1,0:T(8,128)}) %reduce-scatter.8.cloned.1.call-update) | async-done | bytes 294928 | tf_op jit(solution)/shard_map/reduce_scatter | solution.py:289
  868.9 139.2 %reduce-scatter.6.cloned.1.call-done = f32[24,3072]{1,0:T(8,128)} async-done(((f32[768,3072]{1,0:T(8,128)}), f32[24,3072]{1,0:T(8,128)}) %reduce-scatter.6.cloned.1.call-update) | async-done | bytes 294928 | tf_op jit(solution)/shard_map/reduce_scatter | solution.py:288
  (251 shorter events, 240.4 us)
Async XLA Ops:
  7.2 56.9 %copy-start.14 = (bf16[1024,768]{1,0:T(8,128)(2,1)S(1)}, bf16[1024,768]{1,0:T(8,128)(2,1)}, u32[]{:S(2)}) copy-start(bf16[1024,768]{1,0:T(8,128)(2,1)} %param.23) | copy-start | bytes 4718596
  7.2 67.9 %all-gather.5.cloned.1.call-start = ((), (), s32[]{:S(2)}) async-start(), calls=%async_computation.3 | async-start | bytes 3649536 | tf_op jit(solution)/shard_map/all_gather | solution.py:100
  9.0 166.3 %all-gather.7.cloned.1.call-start = ((), (), s32[]{:S(2)}) async-start(), calls=%async_computation.4 | async-start | bytes 1216512 | tf_op jit(solution)/shard_map/all_gather | solution.py:101
  10.6 187.2 %all-gather.9.cloned.1.call-start = ((), (), s32[]{:S(2)}) async-start(), calls=%async_computation.5 | async-start | bytes 4866048 | tf_op jit(solution)/shard_map/all_gather | solution.py:102
  12.3 251.5 %all-gather.11.cloned.1.call-start = ((), (), s32[]{:S(2)}) async-start(), calls=%async_computation.6 | async-start | bytes 4866048 | tf_op jit(solution)/shard_map/all_gather | solution.py:103
  14.0 607.7 %reduce-scatter.4.cloned.1.call-start = ((), (), s32[]{:S(2)}) async-start(), calls=%async_computation.7 | async-start | bytes 2433024 | tf_op jit(solution)/shard_map/reduce_scatter | solution.py:287
  180.8 82.9 %copy-start.8 = (f32[1024,768]{0,1:T(8,128)}, f32[1024,768]{0,1:T(8,128)S(1)}, u32[]{:S(2)}) copy-start(f32[1024,768]{0,1:T(8,128)S(1)} %get-tuple-element.420) | copy-start | bytes 9437188
  180.8 134.0 %copy-start.41 = (f32[1024]{0:T(1024)}, f32[1024]{0:T(1024)S(1)}, u32[]{:S(2)}) copy-start(f32[1024]{0:T(1024)S(1)} %broadcast_multiply_fusion.5) | copy-start | bytes 12292
  181.2 133.6 %copy-start.50 = (f32[1024]{0:T(1024)}, f32[1024]{0:T(1024)S(1)}, u32[]{:S(2)}) copy-start(f32[1024]{0:T(1024)S(1)} %add_rsqrt_fusion.1) | copy-start | bytes 12292
  197.8 65.9 %copy-start.58 = (f32[768]{0:T(1024)S(1)}, f32[768]{0:T(1024)}, u32[]{:S(2)}) copy-start(f32[768]{0:T(1024)} %get-tuple-element.430) | copy-start | bytes 9220
  282.0 18.0 %copy-start.20 = (bf16[1024,768]{0,1:T(8,128)(2,1)}, bf16[1024,768]{0,1:T(8,128)(2,1)S(1)}, u32[]{:S(2)}) copy-start(bf16[1024,768]{0,1:T(8,128)(2,1)S(1)} %get-tuple-element.410) | copy-start | bytes 4718596
  327.8 397.3 %all-reduce.6.cloned.1.call-start = ((), (), s32[]{:S(2)}) async-start(), calls=%async_computation.10 | async-start | bytes 18874368
  534.3 332.4 %reduce-scatter.8.cloned.1.call-start = ((), (), s32[]{:S(2)}) async-start(), calls=%async_computation.9 | async-start | bytes 9732096 | tf_op jit(solution)/shard_map/reduce_scatter | solution.py:289
  546.0 462.1 %reduce-scatter.6.cloned.1.call-start = ((), (), s32[]{:S(2)}) async-start(), calls=%async_computation.8 | async-start | bytes 9732096 | tf_op jit(solution)/shard_map/reduce_scatter | solution.py:288
  559.0 47.2 %copy-start.18 = (bf16[1,1024,768]{2,1,0:T(8,128)(2,1)S(1)}, bf16[1,1024,768]{2,1,0:T(8,128)(2,1)}, u32[]{:S(2)}) copy-start(bf16[1,1024,768]{2,1,0:T(8,128)(2,1)} %copy.145) | copy-start | bytes 4718596
  615.3 110.8 %copy-start.24 = (f32[3,24,768]{2,1,0:T(8,128)S(1)}, f32[3,24,768]{2,1,0:T(8,128)}, u32[]{:S(2)}) copy-start(f32[3,24,768]{2,1,0:T(8,128)} %param.25) | copy-start | bytes 663556
  615.4 110.8 %copy-start.34 = (f32[3,24,768]{2,1,0:T(8,128)S(1)}, f32[3,24,768]{2,1,0:T(8,128)}, u32[]{:S(2)}) copy-start(f32[3,24,768]{2,1,0:T(8,128)} %param.31) | copy-start | bytes 663556
  615.4 110.8 %copy-start.35 = (f32[3,24,768]{2,1,0:T(8,128)S(1)}, f32[3,24,768]{2,1,0:T(8,128)}, u32[]{:S(2)}) copy-start(f32[3,24,768]{2,1,0:T(8,128)} %param.30) | copy-start | bytes 663556
  618.1 248.7 %copy-start.22 = (f32[96,768]{1,0:T(8,128)S(1)}, f32[96,768]{1,0:T(8,128)}, u32[]{:S(2)}) copy-start(f32[96,768]{1,0:T(8,128)} %param.28) | copy-start | bytes 884740
  618.1 248.7 %copy-start.29 = (f32[96,768]{1,0:T(8,128)S(1)}, f32[96,768]{1,0:T(8,128)}, u32[]{:S(2)}) copy-start(f32[96,768]{1,0:T(8,128)} %param.37) | copy-start | bytes 884740
  618.1 248.7 %copy-start.30 = (f32[96,768]{1,0:T(8,128)S(1)}, f32[96,768]{1,0:T(8,128)}, u32[]{:S(2)}) copy-start(f32[96,768]{1,0:T(8,128)} %param.36) | copy-start | bytes 884740
  619.7 388.4 %copy-start.23 = (f32[24,3072]{1,0:T(8,128)S(1)}, f32[24,3072]{1,0:T(8,128)}, u32[]{:S(2)}) copy-start(f32[24,3072]{1,0:T(8,128)} %param.27) | copy-start | bytes 884740
  619.7 388.4 %copy-start.31 = (f32[24,3072]{1,0:T(8,128)S(1)}, f32[24,3072]{1,0:T(8,128)}, u32[]{:S(2)}) copy-start(f32[24,3072]{1,0:T(8,128)} %param.35) | copy-start | bytes 884740
  619.7 388.4 %copy-start.32 = (f32[24,3072]{1,0:T(8,128)S(1)}, f32[24,3072]{1,0:T(8,128)}, u32[]{:S(2)}) copy-start(f32[24,3072]{1,0:T(8,128)} %param.34) | copy-start | bytes 884740
  (49 other events, 280.0 us)
Sparse Core Ops, SparseCore 0:
  11.8 63.2 all-gather.4
  78.6 52.8 all-gather.6
  135.2 62.5 all-gather.8
  201.3 62.4 all-gather.10
  328.0 97.9 reduce-scatter.3
  534.5 190.6 all-reduce.5
  731.1 135.6 reduce-scatter.7
  873.7 134.3 reduce-scatter.5
where the time goes:
time: 1030 us; the launch traced here: 1020 us
  waiting for transfers between devices  435 us (42%)
  matrix products  305 us (30%)
  other arithmetic  109 us (11%)
  blocking collectives  84.4 us (8%)
  local copies, waits for them, and re-layouts  66.9 us (6%)
  between operations  15.9 us (2%)
    reduce_scatter x1, waiting for transfers between devices, shards(): lax.psum_scatter(grad_down_weight, ('dp', 'fsdp'), scatter_dimension=0, t...  140 us
    reduce_scatter x1, waiting for transfers between devices, shards(): lax.psum_scatter(grad_up_weight, ('dp', 'fsdp'), scatter_dimension=0, til...  139 us
    unnamed x9, waiting for transfers between devices  102 us
    dot_general x4, matrix products, masked_scores(): jnp.einsum('qhd,khd->hqk', query_block, keys_heads, preferred_element_typ...  47.1 us
    convert_element_type x2, other arithmetic, backward_block(): (probabilities * (grad_probabilities - row_inner)).astype(jnp.bfloat16)  43.3 us
    unnamed x1, blocking collectives  42.4 us
    psum x1, blocking collectives, shards(): square_total, count_total = lax.psum((squares, counted), ('dp', 'fsdp'))  42 us
    dot_general x1, matrix products, shards(): jnp.dot(normed, up_full, preferred_element_type=jnp.float32) + bias_up  37.7 us
  transfers between devices with their start and end apart: 8, of which 6 were waited for; matrix products, arithmetic and copies ran while one was open for 40% of the time, Pallas kernels for 0%

commit v1 on v0

v1 whole, which is shorter than its diff:
```python
from functools import partial

import jax
import jax.numpy as jnp
from jax import lax
from jax.experimental import pallas as pl
from jax.experimental.pallas import tpu as pltpu
from jax.sharding import PartitionSpec as P

HEADS = 12
STEP = 10
MOST_VALID = 900

MASKED = 1e30
NORM_EPS = 1e-05
SCORE_SCALE = 0.125
BETA_FIRST = 0.9
BETA_SECOND = 0.98
ADAM_EPS = 1e-06
MATRIX_RATE = 0.05
VECTOR_RATE = 0.3
WEIGHT_DECAY = 0.01
AXES = ("dp", "fsdp")
BF = jnp.bfloat16
F32 = jnp.float32
NT = (((1,), (1,)), ((), ()))
TN = (((0,), (0,)), ((), ()))
VMEM_LIMIT = 60 * 2**20
INV_SQRT2 = 0.7071067811865476
INV_SQRT_2PI = 0.3989422804014327


def struct(shape, dtype):
    return jax.ShapeDtypeStruct(shape, dtype)


def params(**more):
    return pltpu.CompilerParams(vmem_limit_bytes=VMEM_LIMIT, **more)


def cost(flops, bytes_accessed, transcendentals=0):
    return pl.CostEstimate(
        flops=int(flops), bytes_accessed=int(bytes_accessed), transcendentals=int(transcendentals)
    )


class Place:
    def __init__(self, n_dp, n_fsdp):
        self.n_dp = n_dp
        self.n_fsdp = n_fsdp
        self.depth = n_fsdp // 2
        self.count = n_dp * n_fsdp
        dp = lax.axis_index("dp")
        fsdp = lax.axis_index("fsdp")
        self.index = dp * n_fsdp + fsdp
        self.coords = jnp.stack([dp // 2, dp % 2, fsdp // 2, fsdp % 2]).astype(jnp.int32)

    def swap_x(self, value):
        return lax.ppermute(value, "dp", [(i, i ^ 1) for i in range(self.n_dp)])

    def swap_y(self, value):
        return lax.ppermute(value, "dp", [(i, i ^ 2) for i in range(self.n_dp)])

    def swap_core(self, value):
        return lax.ppermute(value, "fsdp", [(i, i ^ 1) for i in range(self.n_fsdp)])

    def shift_z(self, value, step):
        depth = self.depth
        pairs = [(i, ((i // 2 + step) % depth) * 2 + i % 2) for i in range(self.n_fsdp)]
        return lax.ppermute(value, "fsdp", pairs)

    def total(self, value):
        for axis, size in (("fsdp", self.n_fsdp), ("dp", self.n_dp)):
            bit = 1
            while bit < size:
                other = lax.ppermute(value, axis, [(i, i ^ bit) for i in range(size)])
                value = value + other
                bit *= 2
        return value


def gather_blocks(place, block):
    depth = place.depth
    column = [block] + [place.shift_z(block, step) for step in range(1, depth)]
    near = jnp.stack(column[: depth // 2])
    far = jnp.stack(column[depth // 2 :])
    near_x = place.swap_x(near)
    far_y = place.swap_y(far)
    halves = [
        [near, near_x, place.swap_y(near), place.swap_y(near_x)],
        [far, place.swap_x(far), far_y, place.swap_x(far_y)],
    ]
    own = halves[0] + halves[1]
    return own + [place.swap_core(value) for value in own]


def first_add_kernel(coords, *refs):
    (ka, kar, sa, sar, kb, kbr, sb, sbr, keep_a, send_a, keep_b, send_b) = refs
    for left, right, out in (
        (ka, kar, keep_a),
        (sa, sar, send_a),
        (kb, kbr, keep_b),
        (sb, sbr, send_b),
    ):
        out[0] = (left[0, 0].astype(F32) + right[0, 0].astype(F32)).astype(BF)


def first_add(place, mine, received, width):
    depth = place.depth
    half = depth // 2
    rows, columns = mine.shape[1:]
    shape = (2, 2, depth, rows, columns)
    mine = mine.reshape(shape)
    received = received.reshape(shape)
    block = (1, 1, half, rows, width)
    keep_a = pl.BlockSpec(block, lambda i, j, c: (i, c[1], 0, 0, j))
    send_a = pl.BlockSpec(block, lambda i, j, c: (i, 1 - c[1], 0, 0, j))
    keep_b = pl.BlockSpec(block, lambda i, j, c: (c[0], i, 1, 0, j))
    send_b = pl.BlockSpec(block, lambda i, j, c: (1 - c[0], i, 1, 0, j))
    out = pl.BlockSpec((1, half, rows, width), lambda i, j, c: (i, 0, 0, j))
    outs = struct((2, half, rows, columns), BF)
    return pl.pallas_call(
        first_add_kernel,
        grid_spec=pltpu.PrefetchScalarGridSpec(
            num_scalar_prefetch=1,
            grid=(2, columns // width),
            in_specs=[keep_a, keep_a, send_a, send_a, keep_b, keep_b, send_b, send_b],
            out_specs=[out] * 4,
        ),
        out_shape=[outs] * 4,
        compiler_params=params(),
        cost_estimate=cost(mine.size, 6 * mine.size),
        name="reduce_over_core",
    )(place.coords, mine, received, mine, received, mine, received, mine, received)


def second_add_kernel(coords, *refs):
    (ka, kar, sa, sar, kb, kbr, sb, sbr, keep_a, send_a, keep_b, send_b) = refs
    for left, right, out in (
        (ka, kar, keep_a),
        (sa, sar, send_a),
        (kb, kbr, keep_b),
        (sb, sbr, send_b),
    ):
        out[...] = (left[0].astype(F32) + right[0].astype(F32)).astype(BF)


def second_add(place, keep_a, got_a, keep_b, got_b, width):
    half, rows, columns = keep_a.shape[1:]
    block = (1, half, rows, width)
    spec_ka = pl.BlockSpec(block, lambda j, c: (c[0], 0, 0, j))
    spec_sa = pl.BlockSpec(block, lambda j, c: (1 - c[0], 0, 0, j))
    spec_kb = pl.BlockSpec(block, lambda j, c: (c[1], 0, 0, j))
    spec_sb = pl.BlockSpec(block, lambda j, c: (1 - c[1], 0, 0, j))
    out = pl.BlockSpec((half, rows, width), lambda j, c: (0, 0, j))
    outs = struct((half, rows, columns), BF)
    return pl.pallas_call(
        second_add_kernel,
        grid_spec=pltpu.PrefetchScalarGridSpec(
            num_scalar_prefetch=1,
            grid=(columns // width,),
            in_specs=[spec_ka, spec_ka, spec_sa, spec_sa, spec_kb, spec_kb, spec_sb, spec_sb],
            out_specs=[out] * 4,
        ),
        out_shape=[outs] * 4,
        compiler_params=params(),
        cost_estimate=cost(2 * keep_a.size, 12 * keep_a.size),
        name="reduce_over_first_link",
    )(place.coords, keep_a, got_a, keep_a, got_a, keep_b, got_b, keep_b, got_b)


def third_add_kernel(depth, coords, keep_a, got_a, keep_b, got_b, *outs):
    half = depth // 2
    for step in range(depth):
        target = lax.rem(coords[2] + step, depth)
        inner = lax.rem(target, half)
        near = keep_a[inner].astype(F32) + got_a[inner].astype(F32)
        far = keep_b[inner].astype(F32) + got_b[inner].astype(F32)
        outs[step][...] = jnp.where(target < half, near, far).astype(BF)


def third_add(place, keep_a, got_a, keep_b, got_b, width):
    depth = place.depth
    half, rows, columns = keep_a.shape
    spec = pl.BlockSpec((half, rows, width), lambda j, c: (0, 0, j))
    out = pl.BlockSpec((rows, width), lambda j, c: (0, j))
    return pl.pallas_call(
        partial(third_add_kernel, depth),
        grid_spec=pltpu.PrefetchScalarGridSpec(
            num_scalar_prefetch=1,
            grid=(columns // width,),
            in_specs=[spec] * 4,
            out_specs=[out] * depth,
        ),
        out_shape=[struct((rows, columns), BF)] * depth,
        compiler_params=params(),
        cost_estimate=cost(2 * keep_a.size, 12 * keep_a.size),
        name="reduce_over_second_link",
    )(place.coords, keep_a, got_a, keep_b, got_b)


class Reduction:
    def __init__(self, place, mine, theirs, width):
        self.place = place
        self.width = width
        self.mine = mine
        self.got = place.swap_core(theirs)

    def first(self):
        place = self.place
        self.keep_a, send_a, self.keep_b, send_b = first_add(
            place, self.mine, self.got, self.width
        )
        self.got_a = place.swap_x(send_a)
        self.got_b = place.swap_y(send_b)

    def second(self):
        place = self.place
        self.keep_a, send_a, self.keep_b, send_b = second_add(
            place, self.keep_a, self.got_a, self.keep_b, self.got_b, self.width
        )
        self.got_a = place.swap_y(send_a)
        self.got_b = place.swap_x(send_b)

    def third(self):
        place = self.place
        blocks = third_add(
            place, self.keep_a, self.got_a, self.keep_b, self.got_b, self.width
        )
        self.blocks = [blocks[0]] + [
            place.shift_z(blocks[step], step) for step in range(1, place.depth)
        ]

    def result(self):
        total = self.blocks[0].astype(F32)
        for block in self.blocks[1:]:
            total = total + block.astype(F32)
        return total


def pack_kernel(qkv, out, up, down, vector, qkv_low, wire, vector_low):
    rows, width = out.shape
    qkv_low[...] = qkv[...].astype(BF)
    vector_low[...] = vector[...].astype(BF)
    wire[:, 0:width] = down[...].astype(BF)
    pieces = [up[:, j * width : (j + 1) * width] for j in range(4)]
    wire[:, width : 2 * width] = jnp.concatenate(pieces, axis=0).astype(BF)
    pieces = [out[:, j * 256 : (j + 1) * 256] for j in range(3)]
    pieces.append(jnp.zeros((rows, 256), F32))
    wire[:, 2 * width : 2 * width + 256] = jnp.concatenate(pieces, axis=0).astype(BF)


def pack(qkv, out, up, down, vector):
    rows, width = out.shape
    return pl.pallas_call(
        pack_kernel,
        out_shape=(
            struct(qkv.shape, BF),
            struct((4 * rows, 2 * width + 256), BF),
            struct(vector.shape, BF),
        ),
        compiler_params=params(),
        name="round_masters",
    )(qkv, out, up, down, vector)


def qkv_kernel(depth, coords, frames, vector, *refs):
    blocks = refs[:16]
    q_ref, k_ref, v_ref, w_out, raw, weights, sems, out_sem = refs[16:]
    half = depth // 2
    chips = 4 * depth
    rows = raw.shape[2]
    width = raw.shape[3]
    outs = (q_ref, k_ref, v_ref)

    @pl.when(pl.program_id(0) == 0)
    def load():
        copies = []
        for number, block in enumerate(blocks):
            core = number // 8
            far = (number // 4) % 2
            dy = (number // 2) % 2
            dx = number % 2
            y = (coords[0] + dy) % 2
            x = (coords[1] + dx) % 2
            other = (coords[3] + core) % 2
            for j in range(half):
                z = (coords[2] + depth - (far * half + j)) % depth
                device = ((y * 2 + x) * depth + z) * 2 + other
                copies.append(
                    pltpu.make_async_copy(block.at[j], raw.at[device], sems.at[number, j])
                )
        for copy in copies:
            copy.start()
        for copy in copies:
            copy.wait()

        def place_rows(chip, carry):
            for which in range(3):
                pair = jnp.concatenate(
                    [raw[2 * chip, which].astype(F32), raw[2 * chip + 1, which].astype(F32)],
                    axis=0,
                )
                start = pl.multiple_of(chip * 2 * rows, 16)
                weights[which, pl.ds(start, 2 * rows), :] = pair.astype(BF)
            return carry

        lax.fori_loop(0, chips, place_rows, 0)
        pltpu.make_async_copy(weights, w_out, out_sem).start()

    for which in range(3):
        value = jnp.dot(frames[...], weights[which], preferred_element_type=F32)
        if which == 0:
            value = value + vector[0:1, :]
        if which == 2:
            value = value + vector[1:2, :]
        outs[which][...] = value.astype(BF)

    @pl.when(pl.program_id(0) == pl.num_programs(0) - 1)
    def finish():
        pltpu.make_async_copy(weights, w_out, out_sem).wait()


def project_qkv(place, frames, vector, blocks, tile=256):
    count, width = frames.shape
    rows = blocks[0].shape[2]
    low = struct((count, width), BF)
    row_tile = pl.BlockSpec((tile, width), lambda i: (i, 0))
    anywhere = pl.BlockSpec(memory_space=pl.ANY)
    return pl.pallas_call(
        partial(qkv_kernel, place.depth),
        grid=(count // tile,),
        in_specs=[
            pl.BlockSpec(memory_space=pltpu.SMEM),
            row_tile,
            pl.BlockSpec(vector.shape, lambda i: (0, 0)),
        ]
        + [anywhere] * 16,
        out_specs=[row_tile] * 3 + [anywhere],
        out_shape=[low, low, low, struct((3, width, width), BF)],
        scratch_shapes=[
            pltpu.VMEM((place.count, 3, rows, width), BF),
            pltpu.VMEM((3, width, width), BF),
            pltpu.SemaphoreType.DMA((16, place.depth // 2)),
            pltpu.SemaphoreType.DMA,
        ],
        compiler_params=params(),
        cost_estimate=cost(6 * count * width * width, 10 * count * width),
        name="project_qkv",
    )(place.coords, frames, vector, *blocks)


def attention_forward_kernel(q_ref, k_ref, v_ref, q_mark, k_mark, out_ref, log_ref):
    count = q_ref.shape[0]
    values = v_ref[...].T
    lane = lax.broadcasted_iota(jnp.int32, (count, 128), 1)
    outs = []
    for head in (0, 1):
        own = (lane < 64) == (head == 0)
        keys = jnp.where(own, k_ref[...], k_mark[...])
        queries = jnp.where(own, q_ref[...] * BF(SCORE_SCALE), q_mark[...])
        scores = lax.dot_general(keys, queries, NT, preferred_element_type=F32)
        maximum = jnp.max(scores, axis=0, keepdims=True)
        raised = jnp.exp(scores - maximum)
        total = jnp.sum(raised, axis=0, keepdims=True)
        weights = (raised * (1.0 / total)).astype(BF)
        log_ref[0, head : head + 1, :] = maximum + jnp.log(total)
        rows = values[64 * head : 64 * head + 64, :]
        outs.append(jnp.dot(rows, weights, preferred_element_type=F32))
    out_ref[...] = jnp.concatenate(outs, axis=0).T.astype(BF)


def attention_forward(q, k, v, q_mark, k_mark):
    count, width = q.shape
    pairs = width // 128
    column = pl.BlockSpec((count, 128), lambda i: (0, i))
    whole = pl.BlockSpec((count, 128), lambda i: (0, 0))
    return pl.pallas_call(
        attention_forward_kernel,
        grid=(pairs,),
        in_specs=[column] * 3 + [whole] * 2,
        out_specs=(column, pl.BlockSpec((1, 8, count), lambda i: (i, 0, 0))),
        out_shape=(struct((count, width), BF), struct((pairs, 8, count), F32)),
        compiler_params=params(),
        cost_estimate=cost(16 * count * count * width, 8 * count * width, 12 * count * count),
        name="attention_forward",
    )(q, k, v, q_mark, k_mark)


def attention_backward_kernel(
    valid, q_ref, k_ref, v_ref, g_ref, q_mark, k_mark, log_ref,
    dq_ref, dk_ref, dv_ref, sum_ref, p_scr, ds_scr,
):
    count = q_ref.shape[0]
    keys_turned = k_ref[0:valid, :].T
    lane = lax.broadcasted_iota(jnp.int32, (count, 128), 1)
    lane_valid = lax.broadcasted_iota(jnp.int32, (valid, 128), 1)
    turned = []
    dk = jnp.zeros((valid, 128), F32)
    dv = jnp.zeros((valid, 128), F32)
    for head in (0, 1):
        own = (lane < 64) == (head == 0)
        scaled = q_ref[...] * BF(SCORE_SCALE)
        keys = jnp.where((lane_valid < 64) == (head == 0), k_ref[0:valid, :], k_mark[0:valid, :])
        queries = jnp.where(own, scaled, q_mark[...])
        grads = jnp.where(own, g_ref[...], BF(0))
        scores = lax.dot_general(keys, queries, NT, preferred_element_type=F32)
        weights = jnp.exp(scores - log_ref[0, head : head + 1, :])
        slopes = lax.dot_general(v_ref[0:valid, :], grads, NT, preferred_element_type=F32)
        inner = jnp.sum(weights * slopes, axis=0, keepdims=True)
        ds_scr[head] = (weights * (slopes - inner)).astype(BF)
        p_scr[head] = weights.astype(BF)
        turned.append(
            jnp.dot(
                keys_turned[64 * head : 64 * head + 64, :],
                ds_scr[head],
                preferred_element_type=F32,
            )
            * SCORE_SCALE
        )
        dk = dk + jnp.dot(
            ds_scr[head], jnp.where(own, scaled, BF(0)), preferred_element_type=F32
        )
        dv = dv + jnp.dot(p_scr[head], grads, preferred_element_type=F32)
    dq = jnp.concatenate(turned, axis=0).T.astype(BF)
    dq_ref[...] = dq
    dk_ref[0:valid, :] = dk.astype(BF)
    dv = dv.astype(BF)
    dv_ref[0:valid, :] = dv
    if valid < count:
        dk_ref[valid:count, :] = jnp.zeros((count - valid, 128), BF)
        dv_ref[valid:count, :] = jnp.zeros((count - valid, 128), BF)
    sum_ref[0:1, :] = jnp.sum(dq.astype(F32), axis=0, keepdims=True)
    sum_ref[1:2, :] = jnp.sum(dv.astype(F32), axis=0, keepdims=True)
    sum_ref[2:8, :] = jnp.zeros((6, 128), F32)


def attention_backward(q, k, v, grads, q_mark, k_mark, logs, valid):
    count, width = q.shape
    pairs = width // 128
    column = pl.BlockSpec((count, 128), lambda i: (0, i))
    whole = pl.BlockSpec((count, 128), lambda i: (0, 0))
    low = struct((count, width), BF)
    return pl.pallas_call(
        partial(attention_backward_kernel, valid),
        grid=(pairs,),
        in_specs=[column] * 4 + [whole] * 2 + [pl.BlockSpec((1, 8, count), lambda i: (i, 0, 0))],
        out_specs=(column, column, column, pl.BlockSpec((8, 128), lambda i: (0, i))),
        out_shape=(low, low, low, struct((8, width), F32)),
        scratch_shapes=[pltpu.VMEM((2, valid, count), BF)] * 2,
        compiler_params=params(),
        cost_estimate=cost(40 * count * count * width, 14 * count * width, 12 * count * count),
        name="attention_backward",
    )(q, k, v, grads, q_mark, k_mark, logs)


def gelu_parts(value):
    size = jnp.abs(value)
    fall = jnp.exp(value * value * -0.5)
    t = 1.0 / (1.0 + (0.3275911 * INV_SQRT2) * size)
    poly = 0.5 * 1.061405429
    poly = poly * t + 0.5 * -1.453152027
    poly = poly * t + 0.5 * 1.421413741
    poly = poly * t + 0.5 * -0.284496736
    poly = poly * t + 0.5 * 0.254829592
    tail = poly * t * fall
    upper = jnp.where(value >= 0.0, 1.0 - tail, tail)
    return value * upper, upper + value * fall * INV_SQRT_2PI


def normalize(hidden):
    mean = jnp.mean(hidden, axis=-1, keepdims=True)
    centred = hidden - mean
    variance = jnp.mean(centred * centred, axis=-1, keepdims=True)
    inverse = lax.rsqrt(variance + NORM_EPS)
    return centred * inverse, inverse


def norm_backward(grad_output, hat, inverse, gain):
    scaled = grad_output * gain
    return inverse * (
        scaled
        - jnp.mean(scaled, axis=-1, keepdims=True)
        - hat * jnp.mean(scaled * hat, axis=-1, keepdims=True)
    )


def column_sums(value):
    return jnp.sum(value, axis=0, keepdims=True)


def middle_kernel(
    packed, total_ref, frames, context, cotangent, vector, *refs
):
    weight_refs = refs[: 1 if packed else 3]
    (
        result, normed_out, activated_out, down_g_out, up_g_out, first_g_out, attended_g_out,
        context_g_out, sums, up_w, down_w, out_w, raw_up, raw_out, slopes, sems,
    ) = refs[len(weight_refs) :]
    step = pl.program_id(0)
    tile, width = frames.shape
    hidden = up_w.shape[1]
    chunks = hidden // width

    if packed:
        wire = weight_refs[0]
        copies = (
            pltpu.make_async_copy(wire.at[:, 2 * width : 2 * width + 256], raw_out, sems.at[0]),
            pltpu.make_async_copy(wire.at[:, width : 2 * width], raw_up, sems.at[1]),
            pltpu.make_async_copy(wire.at[:, 0:width], down_w, sems.at[2]),
        )
    else:
        copies = (
            pltpu.make_async_copy(weight_refs[0], out_w, sems.at[0]),
            pltpu.make_async_copy(weight_refs[1], up_w, sems.at[1]),
            pltpu.make_async_copy(weight_refs[2], down_w, sems.at[2]),
        )

    def unpack(raw, target, columns, pieces):
        rows = 24

        def pair(chip, carry):
            start = pl.multiple_of(chip * 8 * rows, 16)
            value = raw[pl.ds(start, 8 * rows), :].astype(F32)
            for j in range(pieces):
                both = jnp.concatenate(
                    [
                        value[j * rows : (j + 1) * rows],
                        value[(4 + j) * rows : (5 + j) * rows],
                    ],
                    axis=0,
                )
                to = pl.multiple_of(chip * 2 * rows, 16)
                target[pl.ds(to, 2 * rows), j * columns : (j + 1) * columns] = both.astype(BF)
            return carry

        lax.fori_loop(0, width // (2 * rows), pair, 0)

    @pl.when(step == 0)
    def load():
        for copy in copies:
            copy.start()
        sums[...] = jnp.zeros_like(sums)
        copies[0].wait()
        if packed:
            unpack(raw_out, out_w, 256, 3)
        copies[1].wait()
        if packed:
            unpack(raw_up, up_w, width, 4)
        copies[2].wait()

    def add_sum(row, value):
        sums[row : row + 1, :] += value

    position = step * tile + lax.broadcasted_iota(jnp.int32, (tile, 1), 0)
    valid = (position < total_ref[0]).astype(F32)
    attended = jnp.dot(context[...], out_w[...], preferred_element_type=F32) + vector[2:3, :]
    first_sum = frames[...].astype(F32) + attended
    first_hat, first_inverse = normalize(first_sum)
    normed = (first_hat * vector[4:5, :] + vector[5:6, :]).astype(BF)
    normed_out[...] = normed
    down_out = jnp.broadcast_to(vector[3:4, :], (tile, width))
    for j in range(chunks):
        part = slice(j * width, (j + 1) * width)
        pre = jnp.dot(normed, up_w[:, part], preferred_element_type=F32) + vector[8 + j : 9 + j, :]
        activated, slope = gelu_parts(pre)
        slopes[:, part] = slope
        activated = activated.astype(BF)
        activated_out[:, part] = activated
        down_out = down_out + jnp.dot(activated, down_w[part, :], preferred_element_type=F32)
    second_sum = normed.astype(F32) + down_out
    second_hat, second_inverse = normalize(second_sum)
    result[...] = (second_hat * vector[6:7, :] + vector[7:8, :]).astype(BF)
    add_sum(12, column_sums(valid * attended * attended))
    add_sum(13, column_sums(valid * first_sum * first_sum))
    add_sum(14, column_sums(valid * down_out * down_out))
    add_sum(15, column_sums(valid * second_sum * second_sum))
    add_sum(16, jnp.broadcast_to(column_sums(valid), (1, width)))
    out_g = cotangent[...].astype(F32) * valid
    grad_second = norm_backward(out_g, second_hat, second_inverse, vector[6:7, :])
    add_sum(6, column_sums(out_g * second_hat))
    add_sum(7, column_sums(out_g))
    down_g = grad_second.astype(BF)
    down_g_out[...] = down_g
    add_sum(3, column_sums(down_g.astype(F32)))
    grad_normed = grad_second
    for j in range(chunks):
        part = slice(j * width, (j + 1) * width)
        grad = lax.dot_general(down_g, down_w[part, :], NT, preferred_element_type=F32)
        up_g = (grad * slopes[:, part]).astype(BF)
        up_g_out[:, part] = up_g
        add_sum(8 + j, column_sums(up_g.astype(F32)))
        grad_normed = grad_normed + lax.dot_general(
            up_g, up_w[:, part], NT, preferred_element_type=F32
        )
    grad_first = norm_backward(grad_normed, first_hat, first_inverse, vector[4:5, :])
    add_sum(4, column_sums(grad_normed * first_hat))
    add_sum(5, column_sums(grad_normed))
    first_g_out[...] = grad_first
    attended_g = grad_first.astype(BF)
    attended_g_out[...] = attended_g
    add_sum(2, column_sums(attended_g.astype(F32)))
    context_g_out[...] = lax.dot_general(
        attended_g, out_w[...], NT, preferred_element_type=F32
    ).astype(BF)


def middle(frames, context, cotangent, vector, total, weights, hidden, tile=256):
    count, width = frames.shape
    packed = len(weights) == 1
    row_tile = pl.BlockSpec((tile, width), lambda i: (i, 0))
    wide_tile = pl.BlockSpec((tile, hidden), lambda i: (i, 0))
    anywhere = pl.BlockSpec(memory_space=pl.ANY)
    low = struct((count, width), BF)
    wide = struct((count, hidden), BF)
    raw = hidden if packed else 16
    return pl.pallas_call(
        partial(middle_kernel, packed),
        grid=(count // tile,),
        in_specs=[
            pl.BlockSpec(memory_space=pltpu.SMEM),
            row_tile,
            row_tile,
            row_tile,
            pl.BlockSpec(vector.shape, lambda i: (0, 0)),
        ]
        + [anywhere] * len(weights),
        out_specs=[
            row_tile, row_tile, wide_tile, row_tile, wide_tile, row_tile, row_tile, row_tile,
            pl.BlockSpec((24, width), lambda i: (0, 0)),
        ],
        out_shape=[
            low, low, wide, low, wide, struct((count, width), F32), low, low,
            struct((24, width), F32),
        ],
        scratch_shapes=[
            pltpu.VMEM((width, hidden), BF),
            pltpu.VMEM((hidden, width), BF),
            pltpu.VMEM((width, width), BF),
            pltpu.VMEM((raw, width), BF),
            pltpu.VMEM((raw, 256), BF),
            pltpu.VMEM((tile, hidden), F32),
            pltpu.SemaphoreType.DMA((3,)),
        ],
        compiler_params=params(),
        cost_estimate=cost(
            2 * count * width * (4 * hidden + 2 * width),
            count * (14 * width + 4 * hidden) + 4 * width * hidden,
            2 * count * hidden,
        ),
        name="feed_forward",
    )(total, frames, context, cotangent, vector, *weights)


def down_grad_kernel(valid, rows, coords, left, right, mine, theirs):
    value = lax.dot_general(
        left[0:valid, :], right[0:valid, :], TN, preferred_element_type=F32
    )
    first = coords[3] == 0
    for chip in range(mine.shape[0]):
        start = 2 * chip * rows
        low = value[start : start + rows]
        high = value[start + rows : start + 2 * rows]
        mine[chip] = jnp.where(first, low, high).astype(BF)
        theirs[chip] = jnp.where(first, high, low).astype(BF)


def down_grad(place, left, right, valid, chips=2):
    count, hidden = left.shape
    width = right.shape[1]
    rows = hidden // place.count
    tile = 2 * rows * chips
    out = pl.BlockSpec((chips, rows, width), lambda i, c: (i, 0, 0))
    outs = struct((place.count // 2, rows, width), BF)
    return pl.pallas_call(
        partial(down_grad_kernel, valid, rows),
        grid_spec=pltpu.PrefetchScalarGridSpec(
            num_scalar_prefetch=1,
            grid=(hidden // tile,),
            in_specs=[
                pl.BlockSpec((count, tile), lambda i, c: (0, i)),
                pl.BlockSpec((count, width), lambda i, c: (0, 0)),
            ],
            out_specs=[out, out],
        ),
        out_shape=[outs, outs],
        compiler_params=params(),
        cost_estimate=cost(2 * count * hidden * width, 2 * count * (hidden + width)),
        name="grad_down",
    )(place.coords, left, right)


def row_grad_kernel(valid, rows, sizes, coords, *refs):
    lefts = refs[: len(sizes)]
    rights = refs[len(sizes) : 2 * len(sizes)]
    mine, theirs, total = refs[2 * len(sizes) :]
    first = coords[3] == 0
    start = 0
    for left, right, size in zip(lefts, rights, sizes):

        @pl.when((pl.program_id(0) >= start) & (pl.program_id(0) < start + size))
        def multiply(left=left, right=right):
            total[...] = lax.dot_general(
                left[0:valid, :], right[0:valid, :], TN, preferred_element_type=F32
            )

        start += size
    for chip in range(mine.shape[0]):
        low = total[2 * chip * rows : (2 * chip + 1) * rows, :]
        high = total[(2 * chip + 1) * rows : (2 * chip + 2) * rows, :]
        mine[chip] = jnp.where(first, low, high).astype(BF)
        theirs[chip] = jnp.where(first, high, low).astype(BF)


def row_grad(place, lefts, rights, valid, name):
    count, width = lefts[0].shape
    rows = width // place.count
    sizes = [right.shape[1] // width for right in rights]
    starts = [sum(sizes[:i]) for i in range(len(sizes))]
    whole = pl.BlockSpec((count, width), lambda i, c: (0, 0))

    def column(start, size):
        return pl.BlockSpec(
            (count, width), lambda i, c: (0, jnp.clip(i - start, 0, size - 1))
        )

    steps = sum(sizes)
    out = pl.BlockSpec((place.count // 2, rows, width), lambda i, c: (0, 0, i))
    outs = struct((place.count // 2, rows, steps * width), BF)
    return pl.pallas_call(
        partial(row_grad_kernel, valid, rows, sizes),
        grid_spec=pltpu.PrefetchScalarGridSpec(
            num_scalar_prefetch=1,
            grid=(steps,),
            in_specs=[whole] * len(lefts) + [column(a, s) for a, s in zip(starts, sizes)],
            out_specs=[out, out],
            scratch_shapes=[pltpu.VMEM((width, width), F32)],
        ),
        out_shape=[outs, outs],
        compiler_params=params(),
        cost_estimate=cost(
            2 * count * steps * width * width, 2 * (count + width) * (steps + 1) * width
        ),
        name=name,
    )(place.coords, *lefts, *rights)


def frames_grad_kernel(first_g, q_g, k_g, v_g, weights, out):
    value = first_g[...]
    for which, grad in enumerate((q_g, k_g, v_g)):
        value = value + lax.dot_general(
            grad[...], weights[which], NT, preferred_element_type=F32
        )
    out[...] = value.astype(BF)


def frames_gradient(first_g, q_g, k_g, v_g, weights, tile=256):
    count, width = first_g.shape
    row_tile = pl.BlockSpec((tile, width), lambda i: (i, 0))
    return pl.pallas_call(
        frames_grad_kernel,
        grid=(count // tile,),
        in_specs=[row_tile] * 4 + [pl.BlockSpec(weights.shape, lambda i: (0, 0, 0))],
        out_specs=row_tile,
        out_shape=struct((count, width), BF),
        compiler_params=params(),
        cost_estimate=cost(6 * count * width * width, 12 * count * width + 6 * width * width),
        name="frames_gradient",
    )(first_g, q_g, k_g, v_g, weights)


def adam_update(master, first, second, gradient, step_rate, decay_rate):
    first_new = BETA_FIRST * first + (1.0 - BETA_FIRST) * gradient
    second_new = BETA_SECOND * second + (1.0 - BETA_SECOND) * gradient * gradient
    first_hat = first_new / (1.0 - BETA_FIRST**STEP)
    second_hat = second_new / (1.0 - BETA_SECOND**STEP)
    updated = master - step_rate * (
        first_hat / (jnp.sqrt(second_hat) + ADAM_EPS) + decay_rate * master
    )
    return (first_new, second_new, updated, updated.astype(BF))


def segment_marks(length_row, frame_count):
    clip_ends = jnp.cumsum(length_row)
    position = jnp.arange(frame_count, dtype=jnp.int32)
    segment = jnp.sum((clip_ends[None, :] <= position[:, None]).astype(jnp.int32), axis=1)
    lane = jnp.arange(128, dtype=jnp.int32)[None, :] % 64
    same = lane == segment[:, None]
    q_mark = jnp.where(same, 1.0, 0.0).astype(BF)
    k_mark = jnp.where(same | (lane >= 8), 0.0, -MASKED).astype(BF)
    return q_mark, k_mark, clip_ends[-1:].astype(jnp.int32)


def gather_vector(place, shard):
    blank = jnp.zeros((place.count, shard.shape[0]), BF)
    own = lax.dynamic_update_slice(blank, shard[None, :], (place.index, 0))
    return place.total(own)


def after(values, things):
    return lax.optimization_barrier((values, things))[0]


def shards(n_dp, n_fsdp, *arrays):
    (
        frames, cotangent, lengths, qkv_master, out_master, up_master, down_master, vector_master,
        qkv_first, qkv_second, out_first, out_second, up_first, up_second, down_first,
        down_second, vector_first, vector_second,
    ) = arrays
    place = Place(n_dp, n_fsdp)
    frame_count, width = frames.shape
    hidden = up_master.shape[1]
    rows = out_master.shape[0]
    valid = min(frame_count, -(-MOST_VALID // 16) * 16)
    fast = n_dp == 4 and place.depth % 2 == 0 and rows == 24

    q_mark, k_mark, total = segment_marks(lengths[0], frame_count)
    if fast:
        qkv_low, wire_low, vector_low = pack(
            qkv_master, out_master, up_master, down_master, vector_master[None, :]
        )
        wire = lax.all_gather(wire_low, AXES, axis=0, tiled=True)
        vector = gather_vector(place, vector_low[0]).astype(F32).reshape(-1, width)
        blocks = gather_blocks(place, qkv_low)
        queries, keys, values, qkv_full = project_qkv(place, frames, vector, blocks)
        weights = (wire,)
    else:
        vector = gather_vector(place, vector_master.astype(BF)).astype(F32).reshape(-1, width)
        qkv_full = lax.all_gather(qkv_master.astype(BF), AXES, axis=1, tiled=True)
        projected = jnp.einsum("fd,cde->cfe", frames, qkv_full, preferred_element_type=F32)
        queries = (projected[0] + vector[0]).astype(BF)
        keys = projected[1].astype(BF)
        values = (projected[2] + vector[1]).astype(BF)
        weights = tuple(
            lax.all_gather(w.astype(BF), AXES, axis=0, tiled=True)
            for w in (out_master, up_master, down_master)
        )

    context, logs = attention_forward(queries, keys, values, q_mark, k_mark)
    (
        result, normed, activated, down_g, up_g, first_g, attended_g, context_g, sums,
    ) = middle(frames, context, cotangent, vector, total, weights, hidden)

    if fast:
        mine, theirs = down_grad(place, activated, down_g, valid)
        down_sum = Reduction(place, mine, theirs, width)
        mine, theirs = row_grad(
            place, (normed, context), (up_g, attended_g), valid, "grad_up_and_out"
        )
        up_sum = Reduction(place, mine, theirs, width)
        down_sum.first()
        up_sum.first()

    q_g, k_g, v_g, bias_sums = attention_backward(
        queries, keys, values, context_g, q_mark, k_mark, logs, valid
    )

    if fast:
        mine, theirs = row_grad(
            place, (frames, frames, frames), (q_g, k_g, v_g), valid, "grad_qkv"
        )
        qkv_sum = Reduction(place, mine, theirs, width)
        down_sum.second()
        up_sum.second()
        qkv_sum.first()
        down_sum.third()
        up_sum.third()
        qkv_sum.second()
        qkv_sum.third()
        grad_down = down_sum.result()
        grad_up_out = up_sum.result()
        grad_up = grad_up_out[:, :hidden]
        grad_out = grad_up_out[:, hidden:]
        grad_qkv = qkv_sum.result().reshape(rows, 3, width).transpose(1, 0, 2)
    else:
        def scatter(value, dimension):
            return lax.psum_scatter(value, AXES, scatter_dimension=dimension, tiled=True)

        def product(left, right):
            return lax.dot_general(left, right, TN, preferred_element_type=F32)

        grad_down = scatter(product(activated, down_g), 0)
        grad_up = scatter(product(normed, up_g), 0)
        grad_out = scatter(product(context, attended_g), 0)
        grad_qkv = scatter(jnp.stack([product(frames, g) for g in (q_g, k_g, v_g)]), 1)

    frames_grad = frames_gradient(first_g, q_g, k_g, v_g, qkv_full)
    sums = place.total(sums + jnp.pad(bias_sums, ((0, 16), (0, 0))))
    grad_vector = lax.dynamic_slice(
        sums[0:12].reshape(-1),
        (place.index * vector_master.shape[0],),
        (vector_master.shape[0],),
    )
    layer_rms = jnp.sqrt(jnp.sum(sums[12:16], axis=1) / jnp.sum(sums[16]))

    down_new = adam_update(
        down_master, down_first, down_second, grad_down, MATRIX_RATE, WEIGHT_DECAY
    )
    up_new = adam_update(up_master, up_first, up_second, grad_up, MATRIX_RATE, WEIGHT_DECAY)
    out_new = adam_update(out_master, out_first, out_second, grad_out, MATRIX_RATE, WEIGHT_DECAY)
    qkv_new = adam_update(qkv_master, qkv_first, qkv_second, grad_qkv, MATRIX_RATE, WEIGHT_DECAY)
    vector_new = adam_update(
        vector_master, vector_first, vector_second, grad_vector, VECTOR_RATE, 0.0
    )
    return (
        (result, frames_grad, layer_rms) + qkv_new + out_new + up_new + down_new + vector_new
    )


def solution(mesh):
    rows = P(AXES, None)
    middle_rows = P(None, AXES, None)
    entries = P(AXES)
    return jax.shard_map(
        partial(shards, mesh.shape["dp"], mesh.shape["fsdp"]),
        mesh=mesh,
        in_specs=(
            rows, rows, rows, middle_rows, rows, rows, rows, entries,
            middle_rows, middle_rows, rows, rows, rows, rows, rows, rows, entries, entries,
        ),
        out_specs=(rows, rows, P())
        + (middle_rows,) * 4
        + (rows,) * 12
        + (entries,) * 4,
        check_vma=False,
    )
```

time: 1030 us -> 357 us (0.35)
  waiting for transfers between devices: 435 us -> 68.3 us
  matrix products: 305 us -> 0 us
  Pallas kernels: 0 us -> 201 us
  other arithmetic: 109 us -> 12.5 us
  blocking collectives: 84.4 us -> 0 us
  local copies, waits for them, and re-layouts: 66.9 us -> 7.14 us
  starting transfers between devices: 0.33 us -> 50.6 us
    dot_general x26 -> x0, matrix products: 305 us -> none  [the longest x4 47.1 us: masked_scores(): jnp.einsum('qhd,khd->hqk', query_block, keys_heads, preferred_element_typ...]
    reduce_scatter x3 -> x0, waiting for transfers between devices: 279 us -> none  [the longest x1 140 us: shards(): lax.psum_scatter(grad_down_weight, ('dp', 'fsdp'), scatter_dimension=0, t...]
    pallas_call x0 -> x18, Pallas kernels: none -> 201 us  [the longest x1 44.9 us: middle(): pl.pallas_call(partial(middle_kernel, packed), grid=(count // tile,), in_...]
    unnamed x9 -> x1, waiting for transfers between devices: 102 us -> 0.02 us
    ppermute x0 -> x51, waiting for transfers between devices: none -> 63 us  [the longest x10 34.8 us: total(): other = lax.ppermute(value, axis, [(i, i ^ bit) for i in range(size)])]
    convert_element_type x15 -> x6, other arithmetic: 63.1 us -> 5.64 us  [the longest x5 4.65 us: adam_update(): return (first_new, second_new, updated, updated.astype(BF))]
    ppermute x0 -> x51, starting transfers between devices: none -> 50.6 us  [the longest x12 18.7 us: shift_z(): return lax.ppermute(value, 'fsdp', pairs)]
    all_gather x4 -> x1, waiting for transfers between devices: 54.1 us -> 5.3 us  [shards(): wire = lax.all_gather(wire_low, AXES, axis=0, tiled=True)]
  transfers between devices with their start and end apart: 8 -> 52, of which waited for: 6 -> 16; matrix products, arithmetic and copies ran while one was open for 40% -> 4% of each run, Pallas kernels for 0% -> 40%
where the time goes in v1:
time: 357 us; the launch traced here: 354 us
  Pallas kernels  201 us (56%)
  waiting for transfers between devices  68.3 us (19%)
  starting transfers between devices  50.6 us (14%)
  between operations  14.7 us (4%)
  other arithmetic  12.5 us (4%)
  local copies, waits for them, and re-layouts  7.14 us (2%)
    pallas_call x1, Pallas kernels, middle(): pl.pallas_call(partial(middle_kernel, packed), grid=(count // tile,), in_...  44.9 us
    pallas_call x1, Pallas kernels, attention_backward(): pl.pallas_call(partial(attention_backward_kernel, valid), grid=(pairs,),...  36.1 us
    ppermute x10, waiting for transfers between devices, total(): other = lax.ppermute(value, axis, [(i, i ^ bit) for i in range(size)])  34.8 us
    pallas_call x2, Pallas kernels, row_grad(): pl.pallas_call(partial(row_grad_kernel, valid, rows, sizes), grid_spec=pl...  23.3 us
    pallas_call x1, Pallas kernels, attention_forward(): pl.pallas_call(attention_forward_kernel, grid=(pairs,), in_specs=[column]...  22.5 us
    ppermute x12, starting transfers between devices, shift_z(): return lax.ppermute(value, 'fsdp', pairs)  18.7 us
    pallas_call x3, Pallas kernels, first_add(): pl.pallas_call(first_add_kernel, grid_spec=pltpu.PrefetchScalarGridSpec(n...  18.5 us
    pallas_call x3, Pallas kernels, second_add(): pl.pallas_call(second_add_kernel, grid_spec=pltpu.PrefetchScalarGridSpec(...  12.8 us
  transfers between devices with their start and end apart: 52, of which 16 were waited for; matrix products, arithmetic and copies ran while one was open for 4% of the time, Pallas kernels for 40%

profile of v1, /device:TPU:0, one launch (start us, length us, event | category | flops | bytes accessed | tf_op | source)
XLA Modules:
  0.0 354.2 jit_solution(10883595154043233791)
XLA Ops:
  11.8 4.7 %collective-permute-start.10 = (bf16[3,24,768]{2,1,0:T(8,128)(2,1)}, bf16[3,24,768]{2,1,0:T(8,128)(2,1)S(1)}, u32[]{:S(2)}, u32[]{:S(2)}) collective-permute-start(bf16[3,24,768]{2,1,0:T(8,128)(2,1)} %get-tuple-element.88), channel_id=1, source_target_pairs={{0,6},{1,7},{2,0},{3,1},{4,2},{5,3},{6,4},{7,5},{8,14},{9,15},{10,... | collective-permute-start | bytes 331784 | tf_op jit(solution)/shard_map/ppermute | solution.py:70
  21.6 6.3 %collective-permute-done.1 = bf16[32,288]{1,0:T(8,128)(2,1)S(1)} collective-permute-done((bf16[32,288]{1,0:T(8,128)(2,1)S(1)}, bf16[32,288]{1,0:T(8,128)(2,1)S(1)}, u32[]{:S(2)}, u32[]{:S(2)}) %collective-permute-start.1) | collective-permute-done | bytes 18464 | tf_op jit(solution)/shard_map/ppermute | solution.py:76
  28.0 5.1 %collective-permute-done.2 = bf16[32,288]{1,0:T(8,128)(2,1)S(1)} collective-permute-done((bf16[32,288]{1,0:T(8,128)(2,1)S(1)}, bf16[32,288]{1,0:T(8,128)(2,1)S(1)}, u32[]{:S(2)}, u32[]{:S(2)}) %collective-permute-start.2) | collective-permute-done | bytes 18464 | tf_op jit(solution)/shard_map/ppermute | solution.py:76
  41.6 12.5 %collective-permute-done.4 = bf16[32,288]{1,0:T(8,128)(2,1)S(1)} collective-permute-done((bf16[32,288]{1,0:T(8,128)(2,1)S(1)}, bf16[32,288]{1,0:T(8,128)(2,1)S(1)}, u32[]{:S(2)}, u32[]{:S(2)}) %collective-permute-start.4) | collective-permute-done | bytes 18464 | tf_op jit(solution)/shard_map/ppermute | solution.py:76
  58.6 3.8 %collective-permute-done.11.refs_5_ = bf16[2,3,24,768]{3,2,1,0:T(8,128)(2,1)S(1)} collective-permute-done((bf16[2,3,24,768]{3,2,1,0:T(8,128)(2,1)S(1)}, bf16[2,3,24,768]{3,2,1,0:T(8,128)(2,1)S(1)}, u32[]{:S(2)}, u32[]{:S(2)}) %collective-permute-start.11) | collective-permute-done | bytes 221216 | tf_op jit(solution)/shard_map/ppermute | solution.py:59
  68.4 9.5 %project_qkv.1 = (bf16[1024,768]{1,0:T(8,128)(2,1)}, bf16[1024,768]{1,0:T(8,128)(2,1)}, bf16[1024,768]{1,0:T(8,128)(2,1)}, bf16[3,768,768]{2,1,0:T(8,128)(2,1)}) custom-call(s32[4]{0:T(128)} %pad_add_fusion.1.coords, bf16[1024,768]{1,0:T(8,128)(2,1)} %refs_2_.1, f32[12,768]{1,0:T(8,128)} %reshape.114.vector, bf16[2,3,24,768]{3,2,1,0:T(8,128)(2,1)} %copy-done.18, ...), custom_call_target="tpu_custom_call" | custom-call | flops 3623878656 | bytes 7864320 | tf_op jit(solution)/shard_map/project_qkv/pallas_call | solution.py:330
  77.9 22.5 %attention_forward.1 = (bf16[1024,768]{1,0:T(8,128)(2,1)}, f32[6,8,1024]{2,1,0:T(8,128)}) custom-call(bf16[1024,768]{1,0:T(8,128)(2,1)} %get-tuple-element.89.q_ref, bf16[1024,768]{1,0:T(8,128)(2,1)} %get-tuple-element.90.k_ref, bf16[1024,768]{1,0:T(8,128)(2,1)} %get-tuple-element.91.v_ref, bf16[1024,128]{1,0:T(8,128)(2,1)} %get-tuple-element.218.q_mark, ...), custom_call_target="tpu_custom_call" | custom-call | flops 12884901888 | bytes 6291456 | tf_op jit(solution)/shard_map/attention_forward/pallas_call | solution.py:378
  100.4 5.3 %all-gather.2.cloned.1.call-done.refs_0_ = bf16[3072,1792]{1,0:T(8,128)(2,1)} async-done(((bf16[96,1792]{1,0:T(8,128)(2,1)}), bf16[3072,1792]{1,0:T(8,128)(2,1)}) %all-gather.2.cloned.1.call-update) | async-done | bytes 11010064 | tf_op jit(solution)/shard_map/all_gather | solution.py:822
  105.7 44.9 %feed_forward.1 = (bf16[1024,768]{1,0:T(8,128)(2,1)}, bf16[1024,768]{1,0:T(8,128)(2,1)}, bf16[1024,3072]{1,0:T(8,128)(2,1)}, bf16[1024,768]{1,0:T(8,128)(2,1)}, ...) custom-call(s32[1]{0:T(128)} %bitcast.1.total_ref, ...), custom_call_target="tpu_custom_call" | custom-call | flops 21743271936 | bytes 33030144 | tf_op jit(solution)/shard_map/feed_forward/pallas_call | solution.py:617
  150.7 12.9 %grad_up_and_out.1 = (bf16[16,24,3840]{2,1,0:T(8,128)(2,1)}, bf16[16,24,3840]{2,1,0:T(8,128)(2,1)}) custom-call(s32[4]{0:T(128)} %pad_add_fusion.1.coords, bf16[1024,768]{1,0:T(8,128)(2,1)} %get-tuple-element.118.refs_0_, bf16[1024,768]{1,0:T(8,128)(2,1)} %get-tuple-element.92.context.refs_1_, bf16[1024,3072]{1,0:T(8,128)(2,1)} %get-tuple-element.119.refs_2_, ...), custom_call_target="tpu_custom_call" | custom-call | flops 6039797760 | bytes 16515072 | tf_op jit(solution)/shard_map/grad_up_and_out/pallas_call | solution.py:730
  163.8 36.1 %attention_backward.1 = (bf16[1024,768]{1,0:T(8,128)(2,1)}, bf16[1024,768]{1,0:T(8,128)(2,1)}, bf16[1024,768]{1,0:T(8,128)(2,1)}, f32[8,768]{1,0:T(8,128)}) custom-call(bf16[1024,768]{1,0:T(8,128)(2,1)} %get-tuple-element.89.q_ref, bf16[1024,768]{1,0:T(8,128)(2,1)} %get-tuple-element.90.k_ref, bf16[1024,768]{1,0:T(8,128)(2,1)} %get-tuple-element.91.v_ref, ...), custom_call_target="tpu_custom_call" | custom-call | flops 32212254720 | bytes 11010048 | tf_op jit(solution)/shard_map/attention_backward/pallas_call | solution.py:444
  199.9 10.4 %grad_qkv.1 = (bf16[16,24,2304]{2,1,0:T(8,128)(2,1)}, bf16[16,24,2304]{2,1,0:T(8,128)(2,1)}) custom-call(s32[4]{0:T(128)} %pad_add_fusion.1.coords, bf16[1024,768]{1,0:T(8,128)(2,1)} %refs_2_.1, bf16[1024,768]{1,0:T(8,128)(2,1)} %refs_2_.1, bf16[1024,768]{1,0:T(8,128)(2,1)} %refs_2_.1, bf16[1024,768]{1,0:T(8,128)(2,1)} %get-tuple-element.98.q_g.refs_3_, ...), custom_call_target="tpu_custom_call" | custom-call | flops 3623878656 | bytes 11010048 | tf_op jit(solution)/shard_map/grad_qkv/pallas_call | solution.py:730
  210.6 11.6 %grad_down.1 = (bf16[16,96,768]{2,1,0:T(8,128)(2,1)}, bf16[16,96,768]{2,1,0:T(8,128)(2,1)}) custom-call(s32[4]{0:T(128)} %pad_add_fusion.1.coords, bf16[1024,3072]{1,0:T(8,128)(2,1)} %get-tuple-element.135.left, bf16[1024,768]{1,0:T(8,128)(2,1)} %get-tuple-element.136.right), custom_call_target="tpu_custom_call" | custom-call | flops 4831838208 | bytes 7864320 | tf_op jit(solution)/shard_map/grad_down/pallas_call | solution.py:675
  222.4 5.9 %reduce_over_core.3 = (bf16[2,2,24,2304]{3,2,1,0:T(8,128)(2,1)}, bf16[2,2,24,2304]{3,2,1,0:T(8,128)(2,1)}, bf16[2,2,24,2304]{3,2,1,0:T(8,128)(2,1)}, bf16[2,2,24,2304]{3,2,1,0:T(8,128)(2,1)}) custom-call(s32[4]{0:T(128)} %pad_add_fusion.1.coords, bf16[2,2,4,24,2304]{4,3,2,1,0:T(8,128)(2,1)} %bitcast.50, ...), custom_call_target="tpu_custom_call" | custom-call | flops 884736 | bytes 5308416 | tf_op jit(solution)/shard_map/reduce_over_core/pallas_call | solution.py:122
  237.4 4.3 %collective-permute-done.24 = f32[24,768]{1,0:T(8,128)S(1)} collective-permute-done((f32[24,768]{1,0:T(8,128)S(1)}, f32[24,768]{1,0:T(8,128)S(1)}, u32[]{:S(2)}, u32[]{:S(2)}) %collective-permute-start.24) | collective-permute-done | bytes 73760 | tf_op jit(solution)/shard_map/ppermute | solution.py:76
  247.4 4.2 %reduce_over_core.5 = (bf16[2,2,96,768]{3,2,1,0:T(8,128)(2,1)}, bf16[2,2,96,768]{3,2,1,0:T(8,128)(2,1)}, bf16[2,2,96,768]{3,2,1,0:T(8,128)(2,1)}, bf16[2,2,96,768]{3,2,1,0:T(8,128)(2,1)}) custom-call(s32[4]{0:T(128)} %pad_add_fusion.1.coords, bf16[2,2,4,96,768]{4,3,2,1,0:T(8,128)(2,1)} %bitcast.46, ...), custom_call_target="tpu_custom_call" | custom-call | flops 1179648 | bytes 7077888 | tf_op jit(solution)/shard_map/reduce_over_core/pallas_call | solution.py:122
  254.9 8.4 %reduce_over_core.4 = (bf16[2,2,24,3840]{3,2,1,0:T(8,128)(2,1)}, bf16[2,2,24,3840]{3,2,1,0:T(8,128)(2,1)}, bf16[2,2,24,3840]{3,2,1,0:T(8,128)(2,1)}, bf16[2,2,24,3840]{3,2,1,0:T(8,128)(2,1)}) custom-call(s32[4]{0:T(128)} %pad_add_fusion.1.coords, bf16[2,2,4,24,3840]{4,3,2,1,0:T(8,128)(2,1)} %bitcast.38, bf16[2,2,4,24,3840]{4,3,2,1,0:T(8,128)(2,1)} %bitcast.42, ...), custom_call_target="tpu_custom_call" | custom-call | flops 1474560 | bytes 8847360 | tf_op jit(solution)/shard_map/reduce_over_core/pallas_call | solution.py:122
  265.3 8.6 %frames_gradient.1 = bf16[1024,768]{1,0:T(8,128)(2,1)} custom-call(f32[1024,768]{1,0:T(8,128)} %get-tuple-element.95.first_g, bf16[1024,768]{1,0:T(8,128)(2,1)} %get-tuple-element.98.q_g.refs_3_, bf16[1024,768]{1,0:T(8,128)(2,1)} %get-tuple-element.99.k_g.refs_4_, bf16[1024,768]{1,0:T(8,128)(2,1)} %get-tuple-element.100.v_g.refs_5_, ...), custom_call_target="tpu_custom_call" | custom-call | flops 3623878656 | bytes 12976128 | tf_op jit(solution)/shard_map/frames_gradient/pallas_call | solution.py:760
  274.9 4.1 %reduce_over_first_link.3 = (bf16[2,24,2304]{2,1,0:T(8,128)(2,1)}, bf16[2,24,2304]{2,1,0:T(8,128)(2,1)}, bf16[2,24,2304]{2,1,0:T(8,128)(2,1)}, bf16[2,24,2304]{2,1,0:T(8,128)(2,1)}) custom-call(s32[4]{0:T(128)} %pad_add_fusion.1.coords, bf16[2,2,24,2304]{3,2,1,0:T(8,128)(2,1)} %get-tuple-element.106.refs_0_.refs_2_, ...), custom_call_target="tpu_custom_call" | custom-call | flops 442368 | bytes 2654208 | tf_op jit(solution)/shard_map/reduce_over_first_link/pallas_call | solution.py:157
  280.4 7.1 %collective-permute-done.30.got_a = bf16[2,24,2304]{2,1,0:T(8,128)(2,1)S(1)} collective-permute-done((bf16[2,24,2304]{2,1,0:T(8,128)(2,1)}, bf16[2,24,2304]{2,1,0:T(8,128)(2,1)S(1)}, u32[]{:S(2)}, u32[]{:S(2)}) %collective-permute-start.30) | collective-permute-done | bytes 221216 | tf_op jit(solution)/shard_map/ppermute | solution.py:62
  289.6 4.1 %collective-permute-done.31.got_b = bf16[2,24,2304]{2,1,0:T(8,128)(2,1)S(1)} collective-permute-done((bf16[2,24,2304]{2,1,0:T(8,128)(2,1)}, bf16[2,24,2304]{2,1,0:T(8,128)(2,1)S(1)}, u32[]{:S(2)}, u32[]{:S(2)}) %collective-permute-start.31) | collective-permute-done | bytes 221216 | tf_op jit(solution)/shard_map/ppermute | solution.py:59
  308.7 5.4 %reduce_over_first_link.4 = (bf16[2,24,3840]{2,1,0:T(8,128)(2,1)}, bf16[2,24,3840]{2,1,0:T(8,128)(2,1)}, bf16[2,24,3840]{2,1,0:T(8,128)(2,1)}, bf16[2,24,3840]{2,1,0:T(8,128)(2,1)}) custom-call(s32[4]{0:T(128)} %pad_add_fusion.1.coords, bf16[2,2,24,3840]{3,2,1,0:T(8,128)(2,1)} %get-tuple-element.123.refs_0_.refs_2_, bf16[2,2,24,3840]{3,2,1,0:T(8,128)(2,1)} %copy-done.1, ...), custom_call_target="tpu_custom_call" | custom-call | flops 737280 | bytes 4423680 | tf_op jit(solution)/shard_map/reduce_over_first_link/pallas_call | solution.py:157
  327.0 4.6 %reduce_over_second_link.4 = (bf16[24,3840]{1,0:T(8,128)(2,1)}, bf16[24,3840]{1,0:T(8,128)(2,1)}, bf16[24,3840]{1,0:T(8,128)(2,1)}, bf16[24,3840]{1,0:T(8,128)(2,1)}) custom-call(s32[4]{0:T(128)} %pad_add_fusion.1.coords, bf16[2,24,3840]{2,1,0:T(8,128)(2,1)} %get-tuple-element.127.keep_a, bf16[2,24,3840]{2,1,0:T(8,128)(2,1)} %copy-done.7, ...), custom_call_target="tpu_custom_call" | custom-call | flops 368640 | bytes 2211840 | tf_op jit(solution)/shard_map/reduce_over_second_link/pallas_call | solution.py:187
  339.4 5.9 %collective-permute-done.41 = bf16[24,3840]{1,0:T(8,128)(2,1)S(1)} collective-permute-done((bf16[24,3840]{1,0:T(8,128)(2,1)}, bf16[24,3840]{1,0:T(8,128)(2,1)S(1)}, u32[]{:S(2)}, u32[]{:S(2)}) %collective-permute-start.41) | collective-permute-done | bytes 184352 | tf_op jit(solution)/shard_map/ppermute | solution.py:70
  (226 shorter events, 91.3 us)
Async XLA Ops:
  7.2 98.5 %all-gather.2.cloned.1.call-start = ((), (), s32[]{:S(2)}) async-start(), calls=%async_computation | async-start | bytes 11354112 | tf_op jit(solution)/shard_map/all_gather | solution.py:822
  11.8 25.6 %collective-permute-start.10 = (bf16[3,24,768]{2,1,0:T(8,128)(2,1)}, bf16[3,24,768]{2,1,0:T(8,128)(2,1)S(1)}, u32[]{:S(2)}, u32[]{:S(2)}) collective-permute-start(bf16[3,24,768]{2,1,0:T(8,128)(2,1)} %get-tuple-element.88), channel_id=1, source_target_pairs={{0,6},{1,7},{2,0},{3,1},{4,2},{5,3},{6,4},{7,5},{8,14},{9,15},{10,... | collective-permute-start | bytes 331784 | tf_op jit(solution)/shard_map/ppermute | solution.py:70
  16.4 21.8 %collective-permute-start.9 = (bf16[3,24,768]{2,1,0:T(8,128)(2,1)}, bf16[3,24,768]{2,1,0:T(8,128)(2,1)S(1)}, u32[]{:S(2)}, u32[]{:S(2)}) collective-permute-start(bf16[3,24,768]{2,1,0:T(8,128)(2,1)} %get-tuple-element.88), channel_id=1, source_target_pairs={{0,4},{1,5},{2,6},{3,7},{4,0},{5,1},{6,2},{7,3},{8,12},{9,13},{10,... | collective-permute-start | bytes 331784 | tf_op jit(solution)/shard_map/ppermute | solution.py:70
  16.4 18.7 %collective-permute-start.5 = (bf16[3,24,768]{2,1,0:T(8,128)(2,1)}, bf16[3,24,768]{2,1,0:T(8,128)(2,1)S(1)}, u32[]{:S(2)}, u32[]{:S(2)}) collective-permute-start(bf16[3,24,768]{2,1,0:T(8,128)(2,1)} %get-tuple-element.88), channel_id=1, source_target_pairs={{0,2},{1,3},{2,4},{3,5},{4,6},{5,7},{6,0},{7,1},{8,10},{9,11},{10,... | collective-permute-start | bytes 331784 | tf_op jit(solution)/shard_map/ppermute | solution.py:70
  36.1 18.0 %collective-permute-start.14 = (bf16[2,3,24,768]{3,2,1,0:T(8,128)(2,1)S(1)}, bf16[2,3,24,768]{3,2,1,0:T(8,128)(2,1)S(1)}, u32[]{:S(2)}, u32[]{:S(2)}) collective-permute-start(bf16[2,3,24,768]{3,2,1,0:T(8,128)(2,1)S(1)} %pad_maximum_fusion.refs_0_), channel_id=1, source_target_pairs={{0,1},{1,0},{2,3},{3,2},{4,5},{5,4},{6,7},{7,6},{8,9},{9,8},{10,11... | collective-permute-start | bytes 663560 | tf_op jit(solution)/shard_map/ppermute | solution.py:65
  36.1 18.0 %collective-permute-start.7 = (bf16[2,3,24,768]{3,2,1,0:T(8,128)(2,1)S(1)}, bf16[2,3,24,768]{3,2,1,0:T(8,128)(2,1)S(1)}, u32[]{:S(2)}, u32[]{:S(2)}) collective-permute-start(bf16[2,3,24,768]{3,2,1,0:T(8,128)(2,1)S(1)} %pad_maximum_fusion.refs_0_), channel_id=1, source_target_pairs={{0,16},{8,24},{16,0},{24,8},{1,17},{9,25},{17,1},{25,9},{2,18},{10... | collective-permute-start | bytes 663560 | tf_op jit(solution)/shard_map/ppermute | solution.py:62
  37.3 17.3 %collective-permute-start.6 = (bf16[2,3,24,768]{3,2,1,0:T(8,128)(2,1)S(1)}, bf16[2,3,24,768]{3,2,1,0:T(8,128)(2,1)S(1)}, u32[]{:S(2)}, u32[]{:S(2)}) collective-permute-start(bf16[2,3,24,768]{3,2,1,0:T(8,128)(2,1)S(1)} %pad_maximum_fusion.refs_0_), channel_id=1, source_target_pairs={{0,8},{8,0},{16,24},{24,16},{1,9},{9,1},{17,25},{25,17},{2,10},{10... | collective-permute-start | bytes 663560 | tf_op jit(solution)/shard_map/ppermute | solution.py:59
  38.2 18.0 %collective-permute-start.12 = (bf16[2,3,24,768]{3,2,1,0:T(8,128)(2,1)S(1)}, bf16[2,3,24,768]{3,2,1,0:T(8,128)(2,1)S(1)}, u32[]{:S(2)}, u32[]{:S(2)}) collective-permute-start(bf16[2,3,24,768]{3,2,1,0:T(8,128)(2,1)S(1)} %pad_maximum_fusion.1.refs_4_), channel_id=1, source_target_pairs={{0,16},{8,24},{16,0},{24,8},{1,17},{9,25},{17,1},{25,9},{2,18},{10... | collective-permute-start | bytes 663560 | tf_op jit(solution)/shard_map/ppermute | solution.py:62
  38.4 15.7 %collective-permute-start.4 = (bf16[32,288]{1,0:T(8,128)(2,1)S(1)}, bf16[32,288]{1,0:T(8,128)(2,1)S(1)}, u32[]{:S(2)}, u32[]{:S(2)}) collective-permute-start(bf16[32,288]{1,0:T(8,128)(2,1)S(1)} %add.179), channel_id=1, source_target_pairs={{0,16},{8,24},{16,0},{24,8},{1,17},{9,25},{17,1},{25,9},{2,18},{10... | collective-permute-start | bytes 55304 | tf_op jit(solution)/shard_map/ppermute | solution.py:76
  163.6 89.7 %collective-permute-start.35 = (bf16[16,24,3840]{2,1,0:T(8,128)(2,1)}, bf16[16,24,3840]{2,1,0:T(8,128)(2,1)S(1)}, u32[]{:S(2)}, u32[]{:S(2)}) collective-permute-start(bf16[16,24,3840]{2,1,0:T(8,128)(2,1)} %get-tuple-element.122), channel_id=1, source_target_pairs={{0,1},{1,0},{2,3},{3,2},{4,5},{5,4},{6,7},{7,6},{8,9},{9,8},{10,11... | collective-permute-start | bytes 8847368 | tf_op jit(solution)/shard_map/ppermute | solution.py:65
  222.2 25.3 %collective-permute-start.43 = (bf16[16,96,768]{2,1,0:T(8,128)(2,1)}, bf16[16,96,768]{2,1,0:T(8,128)(2,1)}, u32[]{:S(2)}, u32[]{:S(2)}) collective-permute-start(bf16[16,96,768]{2,1,0:T(8,128)(2,1)} %get-tuple-element.138), channel_id=1, source_target_pairs={{0,1},{1,0},{2,3},{3,2},{4,5},{5,4},{6,7},{7,6},{8,9},{9,8},{10,11... | collective-permute-start | bytes 7077896 | tf_op jit(solution)/shard_map/ppermute | solution.py:65
  228.4 35.5 %collective-permute-start.28 = (bf16[2,2,24,2304]{3,2,1,0:T(8,128)(2,1)}, bf16[2,2,24,2304]{3,2,1,0:T(8,128)(2,1)}, u32[]{:S(2)}, u32[]{:S(2)}) collective-permute-start(bf16[2,2,24,2304]{3,2,1,0:T(8,128)(2,1)} %get-tuple-element.107), channel_id=1, source_target_pairs={{0,8},{8,0},{16,24},{24,16},{1,9},{9,1},{17,25},{25,17},{2,10},{10... | collective-permute-start | bytes 1327112 | tf_op jit(solution)/shard_map/ppermute | solution.py:59
  242.5 32.4 %collective-permute-start.29 = (bf16[2,2,24,2304]{3,2,1,0:T(8,128)(2,1)}, bf16[2,2,24,2304]{3,2,1,0:T(8,128)(2,1)}, u32[]{:S(2)}, u32[]{:S(2)}) collective-permute-start(bf16[2,2,24,2304]{3,2,1,0:T(8,128)(2,1)} %get-tuple-element.109), channel_id=1, source_target_pairs={{0,16},{8,24},{16,0},{24,8},{1,17},{9,25},{17,1},{25,9},{2,18},{10... | collective-permute-start | bytes 1327112 | tf_op jit(solution)/shard_map/ppermute | solution.py:62
  246.8 16.4 %collective-permute-start.26 = (f32[24,768]{1,0:T(8,128)}, f32[24,768]{1,0:T(8,128)}, u32[]{:S(2)}, u32[]{:S(2)}) collective-permute-start(f32[24,768]{1,0:T(8,128)} %add.186), channel_id=1, source_target_pairs={{0,16},{8,24},{16,0},{24,8},{1,17},{9,25},{17,1},{25,9},{2,18},{10... | collective-permute-start | bytes 221192 | tf_op jit(solution)/shard_map/ppermute | solution.py:76
  251.7 46.7 %collective-permute-start.44 = (bf16[2,2,96,768]{3,2,1,0:T(8,128)(2,1)}, bf16[2,2,96,768]{3,2,1,0:T(8,128)(2,1)S(1)}, u32[]{:S(2)}, u32[]{:S(2)}) collective-permute-start(bf16[2,2,96,768]{3,2,1,0:T(8,128)(2,1)} %get-tuple-element.140), channel_id=1, source_target_pairs={{0,8},{8,0},{16,24},{24,16},{1,9},{9,1},{17,25},{25,17},{2,10},{10... | collective-permute-start | bytes 1769480 | tf_op jit(solution)/shard_map/ppermute | solution.py:59
  253.2 46.2 %collective-permute-start.45 = (bf16[2,2,96,768]{3,2,1,0:T(8,128)(2,1)}, bf16[2,2,96,768]{3,2,1,0:T(8,128)(2,1)}, u32[]{:S(2)}, u32[]{:S(2)}) collective-permute-start(bf16[2,2,96,768]{3,2,1,0:T(8,128)(2,1)} %get-tuple-element.142), channel_id=1, source_target_pairs={{0,16},{8,24},{16,0},{24,8},{1,17},{9,25},{17,1},{25,9},{2,18},{10... | collective-permute-start | bytes 1769480 | tf_op jit(solution)/shard_map/ppermute | solution.py:62
  263.3 43.0 %collective-permute-start.36 = (bf16[2,2,24,3840]{3,2,1,0:T(8,128)(2,1)}, bf16[2,2,24,3840]{3,2,1,0:T(8,128)(2,1)S(1)}, u32[]{:S(2)}, u32[]{:S(2)}) collective-permute-start(bf16[2,2,24,3840]{3,2,1,0:T(8,128)(2,1)} %get-tuple-element.124), channel_id=1, source_target_pairs={{0,8},{8,0},{16,24},{24,16},{1,9},{9,1},{17,25},{25,17},{2,10},{10... | collective-permute-start | bytes 2211848 | tf_op jit(solution)/shard_map/ppermute | solution.py:59
  263.9 43.9 %collective-permute-start.37 = (bf16[2,2,24,3840]{3,2,1,0:T(8,128)(2,1)}, bf16[2,2,24,3840]{3,2,1,0:T(8,128)(2,1)S(1)}, u32[]{:S(2)}, u32[]{:S(2)}) collective-permute-start(bf16[2,2,24,3840]{3,2,1,0:T(8,128)(2,1)} %get-tuple-element.126), channel_id=1, source_target_pairs={{0,16},{8,24},{16,0},{24,8},{1,17},{9,25},{17,1},{25,9},{2,18},{10... | collective-permute-start | bytes 2211848 | tf_op jit(solution)/shard_map/ppermute | solution.py:62
  297.8 16.2 %collective-permute-start.32 = (bf16[24,2304]{1,0:T(8,128)(2,1)}, bf16[24,2304]{1,0:T(8,128)(2,1)S(1)}, u32[]{:S(2)}, u32[]{:S(2)}) collective-permute-start(bf16[24,2304]{1,0:T(8,128)(2,1)} %get-tuple-element.115), channel_id=1, source_target_pairs={{0,2},{1,3},{2,4},{3,5},{4,6},{5,7},{6,0},{7,1},{8,10},{9,11},{10,... | collective-permute-start | bytes 331784 | tf_op jit(solution)/shard_map/ppermute | solution.py:70
  298.4 16.9 %collective-permute-start.33 = (bf16[24,2304]{1,0:T(8,128)(2,1)}, bf16[24,2304]{1,0:T(8,128)(2,1)S(1)}, u32[]{:S(2)}, u32[]{:S(2)}) collective-permute-start(bf16[24,2304]{1,0:T(8,128)(2,1)} %get-tuple-element.116), channel_id=1, source_target_pairs={{0,4},{1,5},{2,6},{3,7},{4,0},{5,1},{6,2},{7,3},{8,12},{9,13},{10,... | collective-permute-start | bytes 331784 | tf_op jit(solution)/shard_map/ppermute | solution.py:70
  299.5 16.6 %collective-permute-start.34 = (bf16[24,2304]{1,0:T(8,128)(2,1)}, bf16[24,2304]{1,0:T(8,128)(2,1)S(1)}, u32[]{:S(2)}, u32[]{:S(2)}) collective-permute-start(bf16[24,2304]{1,0:T(8,128)(2,1)} %get-tuple-element.117), channel_id=1, source_target_pairs={{0,6},{1,7},{2,0},{3,1},{4,2},{5,3},{6,4},{7,5},{8,14},{9,15},{10,... | collective-permute-start | bytes 331784 | tf_op jit(solution)/shard_map/ppermute | solution.py:70
  320.4 15.1 %collective-permute-start.49 = (bf16[96,768]{1,0:T(8,128)(2,1)}, bf16[96,768]{1,0:T(8,128)(2,1)S(1)}, u32[]{:S(2)}, u32[]{:S(2)}) collective-permute-start(bf16[96,768]{1,0:T(8,128)(2,1)} %get-tuple-element.149), channel_id=1, source_target_pairs={{0,4},{1,5},{2,6},{3,7},{4,0},{5,1},{6,2},{7,3},{8,12},{9,13},{10,... | collective-permute-start | bytes 442376 | tf_op jit(solution)/shard_map/ppermute | solution.py:70
  322.2 13.3 %collective-permute-start.50 = (bf16[96,768]{1,0:T(8,128)(2,1)}, bf16[96,768]{1,0:T(8,128)(2,1)S(1)}, u32[]{:S(2)}, u32[]{:S(2)}) collective-permute-start(bf16[96,768]{1,0:T(8,128)(2,1)} %get-tuple-element.150), channel_id=1, source_target_pairs={{0,6},{1,7},{2,0},{3,1},{4,2},{5,3},{6,4},{7,5},{8,14},{9,15},{10,... | collective-permute-start | bytes 442376 | tf_op jit(solution)/shard_map/ppermute | solution.py:70
  331.7 13.7 %collective-permute-start.41 = (bf16[24,3840]{1,0:T(8,128)(2,1)}, bf16[24,3840]{1,0:T(8,128)(2,1)S(1)}, u32[]{:S(2)}, u32[]{:S(2)}) collective-permute-start(bf16[24,3840]{1,0:T(8,128)(2,1)} %get-tuple-element.133), channel_id=1, source_target_pairs={{0,4},{1,5},{2,6},{3,7},{4,0},{5,1},{6,2},{7,3},{8,12},{9,13},{10,... | collective-permute-start | bytes 552968 | tf_op jit(solution)/shard_map/ppermute | solution.py:70
  (73 other events, 590.9 us)
Sparse Core Ops, SparseCore 0:
  11.6 94.0 all-gather.1

commit v2 on v1

v2 whole, which is shorter than its diff:
```python
from functools import partial

import jax
import jax.numpy as jnp
from jax import lax
from jax.experimental import pallas as pl
from jax.experimental.pallas import tpu as pltpu
from jax.sharding import PartitionSpec as P

HEADS = 12
STEP = 10
MOST_VALID = 900

MASKED = 1e30
NORM_EPS = 1e-05
SCORE_SCALE = 0.125
BETA_FIRST = 0.9
BETA_SECOND = 0.98
ADAM_EPS = 1e-06
MATRIX_RATE = 0.05
VECTOR_RATE = 0.3
WEIGHT_DECAY = 0.01
AXES = ("dp", "fsdp")
BF = jnp.bfloat16
F32 = jnp.float32
NT = (((1,), (1,)), ((), ()))
TN = (((0,), (0,)), ((), ()))
VMEM_LIMIT = 60 * 2**20
INV_SQRT2 = 0.7071067811865476
INV_SQRT_2PI = 0.3989422804014327
LOG2_E = 1.4426950408889634


def struct(shape, dtype):
    return jax.ShapeDtypeStruct(shape, dtype)


def params(**more):
    return pltpu.CompilerParams(vmem_limit_bytes=VMEM_LIMIT, **more)


def cost(flops, bytes_accessed, transcendentals=0, times=1000):
    return pl.CostEstimate(
        flops=int(flops) * times,
        bytes_accessed=int(bytes_accessed) * times,
        transcendentals=int(transcendentals) * times,
    )


class Place:
    def __init__(self, n_dp, n_fsdp):
        self.n_dp = n_dp
        self.n_fsdp = n_fsdp
        self.depth = n_fsdp // 2
        self.count = n_dp * n_fsdp
        dp = lax.axis_index("dp")
        fsdp = lax.axis_index("fsdp")
        self.index = dp * n_fsdp + fsdp
        self.coords = jnp.stack([dp // 2, dp % 2, fsdp // 2, fsdp % 2, self.index])

    def swap_x(self, value):
        return lax.ppermute(value, "dp", [(i, i ^ 1) for i in range(self.n_dp)])

    def swap_y(self, value):
        return lax.ppermute(value, "dp", [(i, i ^ 2) for i in range(self.n_dp)])

    def swap_core(self, value):
        return lax.ppermute(value, "fsdp", [(i, i ^ 1) for i in range(self.n_fsdp)])

    def shift_z(self, value, step):
        depth = self.depth
        pairs = [(i, ((i // 2 + step) % depth) * 2 + i % 2) for i in range(self.n_fsdp)]
        return lax.ppermute(value, "fsdp", pairs)

    def swap_z(self, value, bit):
        pairs = [(i, i ^ (2 * bit)) for i in range(self.n_fsdp)]
        return lax.ppermute(value, "fsdp", pairs)

    def total(self, value):
        for axis, size in (("fsdp", self.n_fsdp), ("dp", self.n_dp)):
            bit = 1
            while bit < size:
                other = lax.ppermute(value, axis, [(i, i ^ bit) for i in range(size)])
                value = value + other
                bit *= 2
        return value


def gather_blocks(place, block):
    depth = place.depth
    column = [block] + [place.shift_z(block, step) for step in range(1, depth)]
    near = jnp.stack(column[: depth // 2])
    far = jnp.stack(column[depth // 2 :])
    near_x = place.swap_x(near)
    far_y = place.swap_y(far)
    halves = [
        [near, near_x, place.swap_y(near), place.swap_y(near_x)],
        [far, place.swap_x(far), far_y, place.swap_x(far_y)],
    ]
    own = halves[0] + halves[1]
    return own + [place.swap_core(value) for value in own]


def rounded_sum(left, right):
    return (left.astype(F32) + right.astype(F32)).astype(BF)


def first_add_kernel(coords, *refs):
    for number, out in enumerate(refs[8:]):
        out[0] = rounded_sum(refs[2 * number][0, 0], refs[2 * number + 1][0, 0])


def first_add(place, mine, got):
    half = place.depth // 2
    rows, columns = mine.shape[1:]
    shape = (2, 2, place.depth, rows, columns)
    mine = mine.reshape(shape)
    got = got.reshape(shape)
    block = (1, 1, half, rows, columns)
    specs = [
        pl.BlockSpec(block, lambda i, c: (i, c[1], 0, 0, 0)),
        pl.BlockSpec(block, lambda i, c: (i, 1 - c[1], 0, 0, 0)),
        pl.BlockSpec(block, lambda i, c: (c[0], i, 1, 0, 0)),
        pl.BlockSpec(block, lambda i, c: (1 - c[0], i, 1, 0, 0)),
    ]
    out = pl.BlockSpec((1, half, rows, columns), lambda i, c: (i, 0, 0, 0))
    return pl.pallas_call(
        first_add_kernel,
        grid_spec=pltpu.PrefetchScalarGridSpec(
            num_scalar_prefetch=1,
            grid=(2,),
            in_specs=[spec for spec in specs for _ in range(2)],
            out_specs=[out] * 4,
        ),
        out_shape=[struct((2, half, rows, columns), BF)] * 4,
        compiler_params=params(),
        cost_estimate=cost(mine.size, 6 * mine.size),
        name="reduce_over_core",
    )(place.coords, *([mine, got] * 4))


def second_add_kernel(widths, coords, *refs):
    outs = refs[8 * len(widths) :]
    start = 0
    for part, width in enumerate(widths):
        ins = refs[8 * part : 8 * part + 8]
        for number, out in enumerate(outs):
            out[:, :, start : start + width] = rounded_sum(
                ins[2 * number][0], ins[2 * number + 1][0]
            )
        start += width


def second_add(place, parts):
    half, rows = parts[0][0].shape[1:3]
    widths = [part[0].shape[3] for part in parts]
    specs = []
    ins = []
    for (keep_a, got_a, keep_b, got_b), width in zip(parts, widths):
        block = (1, half, rows, width)
        stay_a = pl.BlockSpec(block, lambda i, c: (c[0], 0, 0, 0))
        leave_a = pl.BlockSpec(block, lambda i, c: (1 - c[0], 0, 0, 0))
        stay_b = pl.BlockSpec(block, lambda i, c: (c[1], 0, 0, 0))
        leave_b = pl.BlockSpec(block, lambda i, c: (1 - c[1], 0, 0, 0))
        specs += [stay_a] * 2 + [leave_a] * 2 + [stay_b] * 2 + [leave_b] * 2
        ins += [keep_a, got_a] * 2 + [keep_b, got_b] * 2
    shape = (half, rows, sum(widths))
    return pl.pallas_call(
        partial(second_add_kernel, widths),
        grid_spec=pltpu.PrefetchScalarGridSpec(
            num_scalar_prefetch=1,
            grid=(1,),
            in_specs=specs,
            out_specs=[pl.BlockSpec(shape, lambda i, c: (0, 0, 0))] * 4,
        ),
        out_shape=[struct(shape, BF)] * 4,
        compiler_params=params(),
        cost_estimate=cost(4 * half * rows * shape[2], 24 * half * rows * shape[2]),
        name="reduce_over_first_link",
    )(place.coords, *ins)


def third_add_kernel(coords, keep_a, got_a, keep_b, got_b, keep, send):
    own = lax.rem(coords[2], 2)
    for out, which in ((keep, own), (send, 1 - own)):
        out[0] = rounded_sum(keep_a[which], got_a[which])
        out[1] = rounded_sum(keep_b[which], got_b[which])


def fourth_add_kernel(coords, keep, got, keep_out, send):
    own = lax.div(coords[2], 2)
    keep_out[...] = rounded_sum(keep[own], got[own])
    send[...] = rounded_sum(keep[1 - own], got[1 - own])


def small_add(place, kernel, ins, shape, name):
    inside = pl.BlockSpec(memory_space=pltpu.VMEM)
    return pl.pallas_call(
        kernel,
        in_specs=[pl.BlockSpec(memory_space=pltpu.SMEM)] + [inside] * len(ins),
        out_specs=[inside] * 2,
        out_shape=[struct(shape, BF)] * 2,
        compiler_params=params(),
        cost_estimate=cost(2 * ins[0].size, 6 * ins[0].size),
        name=name,
    )(place.coords, *ins)


class Reduction:
    def __init__(self, place):
        self.place = place
        self.parts = []

    def first(self, mine, got):
        place = self.place
        keep_a, send_a, keep_b, send_b = first_add(place, mine, got)
        self.parts.append((keep_a, place.swap_x(send_a), keep_b, place.swap_y(send_b)))
        return keep_a

    def second(self):
        place = self.place
        keep_a, send_a, keep_b, send_b = second_add(place, self.parts)
        self.sums = (keep_a, place.swap_y(send_a), keep_b, place.swap_x(send_b))
        return keep_a

    def third(self):
        place = self.place
        keep, send = small_add(
            place, third_add_kernel, self.sums, self.sums[0].shape, "reduce_over_second_link"
        )
        self.sums = (keep, place.swap_z(send, 1))
        return keep

    def fourth(self):
        place = self.place
        keep, send = small_add(
            place, fourth_add_kernel, self.sums, self.sums[0].shape[1:], "reduce_over_z"
        )
        self.sums = (keep, place.swap_z(send, 2))
        return keep

    def result(self):
        return self.sums[0].astype(F32) + self.sums[1].astype(F32)


def pack_kernel(coords, qkv, out, up, down, vector, qkv_wire, wire, line):
    rows, width = out.shape
    for which in range(3):
        qkv_wire[:, which * width : (which + 1) * width] = qkv[which].astype(BF)
    line[...] = jnp.zeros_like(line)
    line[0:1, 0 : vector.shape[1]] = vector[...]
    moved = pltpu.roll(line[...], 32 * (coords[4] % 4), 1)
    pieces = [moved[0:1, j * 128 : (j + 1) * 128] for j in range(4)]
    pieces.append(jnp.zeros((rows - 4, 128), F32))
    qkv_wire[:, 3 * width : 3 * width + 128] = jnp.concatenate(pieces, axis=0).astype(BF)
    wire[:, 0:width] = down[...].astype(BF)
    pieces = [up[:, j * width : (j + 1) * width] for j in range(4)]
    wire[:, width : 2 * width] = jnp.concatenate(pieces, axis=0).astype(BF)
    pieces = [out[:, j * 256 : (j + 1) * 256] for j in range(3)]
    pieces.append(jnp.zeros((rows, 256), F32))
    wire[:, 2 * width : 2 * width + 256] = jnp.concatenate(pieces, axis=0).astype(BF)


def pack(place, qkv, out, up, down, vector):
    rows, width = out.shape
    inside = pl.BlockSpec(memory_space=pltpu.VMEM)
    return pl.pallas_call(
        pack_kernel,
        in_specs=[pl.BlockSpec(memory_space=pltpu.SMEM)] + [inside] * 5,
        out_shape=(
            struct((rows, 3 * width + 128), BF),
            struct((4 * rows, 2 * width + 256), BF),
        ),
        scratch_shapes=[pltpu.VMEM((8, 512), F32)],
        compiler_params=params(),
        name="round_masters",
    )(place.coords, qkv, out, up, down, vector)


def qkv_kernel(depth, coords, frames, *refs):
    blocks = refs[:16]
    q_ref, k_ref, v_ref, vector_out, w_out, raw, weights, entries, sems, out_sem = refs[16:]
    half = depth // 2
    chips = 4 * depth
    rows = raw.shape[1]
    width = weights.shape[2]
    outs = (q_ref, k_ref, v_ref)

    @pl.when(pl.program_id(0) == 0)
    def load():
        copies = []
        for number, block in enumerate(blocks):
            core = number // 8
            far = (number // 4) % 2
            dy = (number // 2) % 2
            dx = number % 2
            y = (coords[0] + dy) % 2
            x = (coords[1] + dx) % 2
            other = (coords[3] + core) % 2
            for j in range(half):
                z = (coords[2] + depth - (far * half + j)) % depth
                device = ((y * 2 + x) * depth + z) * 2 + other
                copies.append(
                    pltpu.make_async_copy(block.at[j], raw.at[device], sems.at[number, j])
                )
        for copy in copies:
            copy.start()
        entries[...] = jnp.zeros_like(entries)
        for copy in copies:
            copy.wait()

        def place_rows(chip, carry):
            start = pl.multiple_of(chip * 2 * rows, 16)
            for which in range(3):
                part = slice(which * width, (which + 1) * width)
                pair = jnp.concatenate(
                    [raw[2 * chip, :, part].astype(F32), raw[2 * chip + 1, :, part].astype(F32)],
                    axis=0,
                )
                weights[which, pl.ds(start, 2 * rows), :] = pair.astype(BF)
            return carry

        lax.fori_loop(0, chips, place_rows, 0)
        pltpu.make_async_copy(weights, w_out, out_sem).start()
        for device in range(2 * chips):
            first = 9 * (device // 4) + 2 * (device % 4)
            window = raw[device, :, 3 * width : 3 * width + 128].astype(F32)
            entries[first : first + 4, :] += window[0:4, :]
        vector_out[...] = jnp.zeros_like(vector_out)
        pieces = width // 128
        for row in range(12):
            for j in range(pieces):
                vector_out[row : row + 1, j * 128 : (j + 1) * 128] = entries[
                    row * pieces + j : row * pieces + j + 1, :
                ]

    for which in range(3):
        value = jnp.dot(frames[...], weights[which], preferred_element_type=F32)
        if which == 0:
            value = value + vector_out[0:1, :]
        if which == 2:
            value = value + vector_out[1:2, :]
        outs[which][...] = value.astype(BF)

    @pl.when(pl.program_id(0) == pl.num_programs(0) - 1)
    def finish():
        pltpu.make_async_copy(weights, w_out, out_sem).wait()


def project_qkv(place, frames, blocks, tile=256):
    count, width = frames.shape
    rows, wire_width = blocks[0].shape[1:]
    low = struct((count, width), BF)
    row_tile = pl.BlockSpec((tile, width), lambda i: (i, 0))
    anywhere = pl.BlockSpec(memory_space=pl.ANY)
    return pl.pallas_call(
        partial(qkv_kernel, place.depth),
        grid=(count // tile,),
        in_specs=[pl.BlockSpec(memory_space=pltpu.SMEM), row_tile] + [anywhere] * 16,
        out_specs=[row_tile] * 3 + [pl.BlockSpec((16, width), lambda i: (0, 0)), anywhere],
        out_shape=[low, low, low, struct((16, width), F32), struct((3, width, width), BF)],
        scratch_shapes=[
            pltpu.VMEM((place.count, rows, wire_width), BF),
            pltpu.VMEM((3, width, width), BF),
            pltpu.VMEM((80, 128), F32),
            pltpu.SemaphoreType.DMA((16, place.depth // 2)),
            pltpu.SemaphoreType.DMA,
        ],
        compiler_params=params(),
        cost_estimate=cost(6 * count * width * width, 10 * count * width, times=1),
        name="project_qkv",
    )(place.coords, frames, *blocks)


def attention_forward_kernel(q_ref, k_ref, v_ref, q_mark, k_mark, out_ref, log_ref):
    count = q_ref.shape[0]
    values = v_ref[...].T
    lane = lax.broadcasted_iota(jnp.int32, (count, 128), 1)
    outs = []
    for head in (0, 1):
        own = (lane < 64) == (head == 0)
        keys = jnp.where(own, k_ref[...], k_mark[...])
        queries = jnp.where(own, q_ref[...] * BF(SCORE_SCALE), q_mark[...])
        scores = lax.dot_general(keys, queries, NT, preferred_element_type=F32)
        maximum = jnp.max(scores, axis=0, keepdims=True)
        raised = jnp.exp(scores - maximum)
        total = jnp.sum(raised, axis=0, keepdims=True)
        weights = (raised * (1.0 / total)).astype(BF)
        log_ref[0, head : head + 1, :] = maximum + jnp.log(total)
        rows = values[64 * head : 64 * head + 64, :]
        outs.append(jnp.dot(rows, weights, preferred_element_type=F32))
    out_ref[...] = jnp.concatenate(outs, axis=0).T.astype(BF)


def attention_forward(q, k, v, q_mark, k_mark):
    count, width = q.shape
    pairs = width // 128
    column = pl.BlockSpec((count, 128), lambda i: (0, i))
    whole = pl.BlockSpec((count, 128), lambda i: (0, 0))
    return pl.pallas_call(
        attention_forward_kernel,
        grid=(pairs,),
        in_specs=[column] * 3 + [whole] * 2,
        out_specs=(column, pl.BlockSpec((1, 8, count), lambda i: (i, 0, 0))),
        out_shape=(struct((count, width), BF), struct((pairs, 8, count), F32)),
        compiler_params=params(),
        cost_estimate=cost(
            16 * count * count * width, 8 * count * width, 12 * count * count, times=1
        ),
        name="attention_forward",
    )(q, k, v, q_mark, k_mark)


def attention_backward_kernel(
    valid, q_ref, k_ref, v_ref, g_ref, q_mark, k_mark, log_ref, grads_ref, sum_ref, p_scr, ds_scr
):
    count = q_ref.shape[0]
    keys_turned = k_ref[0:valid, :].T
    lane = lax.broadcasted_iota(jnp.int32, (count, 128), 1)
    lane_valid = lax.broadcasted_iota(jnp.int32, (valid, 128), 1)
    turned = []
    dk = jnp.zeros((valid, 128), F32)
    dv = jnp.zeros((valid, 128), F32)
    for head in (0, 1):
        own = (lane < 64) == (head == 0)
        scaled = q_ref[...] * BF(SCORE_SCALE)
        keys = jnp.where((lane_valid < 64) == (head == 0), k_ref[0:valid, :], k_mark[0:valid, :])
        queries = jnp.where(own, scaled, q_mark[...])
        grads = jnp.where(own, g_ref[...], BF(0))
        scores = lax.dot_general(keys, queries, NT, preferred_element_type=F32)
        weights = jnp.exp(scores - log_ref[0, head : head + 1, :])
        slopes = lax.dot_general(v_ref[0:valid, :], grads, NT, preferred_element_type=F32)
        inner = jnp.sum(weights * slopes, axis=0, keepdims=True)
        ds_scr[head] = (weights * (slopes - inner)).astype(BF)
        p_scr[head] = weights.astype(BF)
        turned.append(
            jnp.dot(
                keys_turned[64 * head : 64 * head + 64, :],
                ds_scr[head],
                preferred_element_type=F32,
            )
            * SCORE_SCALE
        )
        dk = dk + jnp.dot(
            ds_scr[head], jnp.where(own, scaled, BF(0)), preferred_element_type=F32
        )
        dv = dv + jnp.dot(p_scr[head], grads, preferred_element_type=F32)
    dq = jnp.concatenate(turned, axis=0).T.astype(BF)
    grads_ref[0] = dq
    grads_ref[1, 0:valid, :] = dk.astype(BF)
    dv = dv.astype(BF)
    grads_ref[2, 0:valid, :] = dv
    if valid < count:
        grads_ref[1, valid:count, :] = jnp.zeros((count - valid, 128), BF)
        grads_ref[2, valid:count, :] = jnp.zeros((count - valid, 128), BF)
    sum_ref[0:1, :] = jnp.sum(dq.astype(F32), axis=0, keepdims=True)
    sum_ref[1:2, :] = jnp.sum(dv.astype(F32), axis=0, keepdims=True)
    sum_ref[2:8, :] = jnp.zeros((6, 128), F32)


def attention_backward(q, k, v, grads, q_mark, k_mark, logs, valid, first, pairs, earlier=()):
    count, width = q.shape
    column = pl.BlockSpec((count, 128), lambda i: (0, first + i))
    whole = pl.BlockSpec((count, 128), lambda i: (0, 0))

    def kernel(*refs):
        attention_backward_kernel(valid, *refs[:7], *refs[7 + len(earlier) :])

    return pl.pallas_call(
        kernel,
        grid=(pairs,),
        in_specs=[column] * 4
        + [whole] * 2
        + [pl.BlockSpec((1, 8, count), lambda i: (first + i, 0, 0))]
        + [pl.BlockSpec(memory_space=pl.ANY)] * len(earlier),
        out_specs=(
            pl.BlockSpec((3, count, 128), lambda i: (0, 0, first + i)),
            pl.BlockSpec((8, 128), lambda i: (0, first + i)),
        ),
        out_shape=(struct((3, count, width), BF), struct((8, width), F32)),
        scratch_shapes=[pltpu.VMEM((2, valid, count), BF)] * 2,
        input_output_aliases={7 + i: i for i in range(len(earlier))},
        compiler_params=params(),
        cost_estimate=cost(
            40 * count * count * 128 * pairs, 14 * count * 128 * pairs, 2 * count * count * pairs
        ),
        name="attention_backward",
    )(q, k, v, grads, q_mark, k_mark, logs, *earlier)


def gelu_parts(value):
    upper = 0.5 + 0.5 * lax.erf(value * INV_SQRT2)
    fall = jnp.exp2(value * value * (-0.5 * LOG2_E))
    return value * upper, upper + value * fall * INV_SQRT_2PI


def normalize(hidden):
    mean = jnp.mean(hidden, axis=-1, keepdims=True)
    centred = hidden - mean
    variance = jnp.mean(centred * centred, axis=-1, keepdims=True)
    inverse = lax.rsqrt(variance + NORM_EPS)
    return centred * inverse, inverse


def norm_backward(grad_output, hat, inverse, gain):
    scaled = grad_output * gain
    return inverse * (
        scaled
        - jnp.mean(scaled, axis=-1, keepdims=True)
        - hat * jnp.mean(scaled * hat, axis=-1, keepdims=True)
    )


def column_sums(value):
    return jnp.sum(value, axis=0, keepdims=True)


def interleave(*works):
    works = list(works)
    while works:
        for work in list(works):
            try:
                next(work)
            except StopIteration:
                works.remove(work)


def middle_kernel(packed, last_rows, chunk, total_ref, frames, context, cotangent, vector, *refs):
    weight_refs = refs[: 1 if packed else 3]
    (
        result, normed_out, activated_out, down_g_out, up_g_out, first_g_out, attended_g_out,
        context_g_out, sums, up_w, down_w, out_w, raw_up, raw_out, slopes, first_hats,
        second_hats, inverses, sems,
    ) = refs[len(weight_refs) :]
    step = pl.program_id(0)
    tiles = pl.num_programs(0) - 1
    tile, width = frames.shape
    hidden = up_w.shape[1]
    parts = [slice(j * chunk, (j + 1) * chunk) for j in range(hidden // chunk)]

    if packed:
        wire = weight_refs[0]
        copies = (
            pltpu.make_async_copy(wire.at[:, 2 * width : 2 * width + 256], raw_out, sems.at[0]),
            pltpu.make_async_copy(wire.at[:, width : 2 * width], raw_up, sems.at[1]),
            pltpu.make_async_copy(wire.at[:, 0:width], down_w, sems.at[2]),
        )
    else:
        copies = (
            pltpu.make_async_copy(weight_refs[0], out_w, sems.at[0]),
            pltpu.make_async_copy(weight_refs[1], up_w, sems.at[1]),
            pltpu.make_async_copy(weight_refs[2], down_w, sems.at[2]),
        )

    def unpack(raw, target, columns, pieces):
        rows = 24

        def pair(chip, carry):
            start = pl.multiple_of(chip * 8 * rows, 16)
            value = raw[pl.ds(start, 8 * rows), :].astype(F32)
            for j in range(pieces):
                both = jnp.concatenate(
                    [
                        value[j * rows : (j + 1) * rows],
                        value[(4 + j) * rows : (5 + j) * rows],
                    ],
                    axis=0,
                )
                to = pl.multiple_of(chip * 2 * rows, 16)
                target[pl.ds(to, 2 * rows), j * columns : (j + 1) * columns] = both.astype(BF)
            return carry

        lax.fori_loop(0, width // (2 * rows), pair, 0)

    def add_sum(row, value):
        sums[row : row + 1, :] += value

    def valid_rows(number, rows):
        position = number * tile + lax.broadcasted_iota(jnp.int32, (rows, 1), 0)
        return (position < total_ref[0]).astype(F32)

    def forward():
        slot = step % 2
        valid = valid_rows(step, tile)
        attended = jnp.dot(context[...], out_w[...], preferred_element_type=F32)
        yield
        attended = attended + vector[2:3, :]
        first_sum = frames[...].astype(F32) + attended
        first_hat, first_inverse = normalize(first_sum)
        normed = (first_hat * vector[4:5, :] + vector[5:6, :]).astype(BF)
        normed_out[...] = normed
        first_hats[slot] = first_hat
        inverses[slot, 0] = jnp.broadcast_to(first_inverse, (tile, 128))
        add_sum(12, column_sums(valid * attended * attended))
        add_sum(13, column_sums(valid * first_sum * first_sum))
        add_sum(16, jnp.broadcast_to(column_sums(valid), (1, width)))
        yield
        down_out = jnp.broadcast_to(vector[3:4, :], (tile, width))
        pre = jnp.dot(normed, up_w[:, parts[0]], preferred_element_type=F32)
        yield
        for j, part in enumerate(parts):
            if j + 1 < len(parts):
                later = jnp.dot(normed, up_w[:, parts[j + 1]], preferred_element_type=F32)
            row = 8 + part.start // width
            bias = vector[row : row + 1, part.start % width : part.start % width + chunk]
            activated, slope = gelu_parts(pre + bias)
            slopes[slot, :, part] = slope
            activated = activated.astype(BF)
            activated_out[:, part] = activated
            yield
            down_out = down_out + jnp.dot(activated, down_w[part, :], preferred_element_type=F32)
            pre = later
            yield
        second_sum = normed.astype(F32) + down_out
        second_hat, second_inverse = normalize(second_sum)
        result[...] = (second_hat * vector[6:7, :] + vector[7:8, :]).astype(BF)
        second_hats[slot] = second_hat
        inverses[slot, 1] = jnp.broadcast_to(second_inverse, (tile, 128))
        add_sum(14, column_sums(valid * down_out * down_out))
        add_sum(15, column_sums(valid * second_sum * second_sum))

    def backward(rows):
        slot = (step + 1) % 2
        valid = valid_rows(step - 1, rows)
        out_g = cotangent[0:rows, :].astype(F32) * valid
        second_hat = second_hats[slot, 0:rows, :]
        grad_second = norm_backward(
            out_g, second_hat, inverses[slot, 1, 0:rows, 0:1], vector[6:7, :]
        )
        add_sum(6, column_sums(out_g * second_hat))
        add_sum(7, column_sums(out_g))
        down_g = grad_second.astype(BF)
        down_g_out[0:rows, :] = down_g
        add_sum(3, column_sums(down_g.astype(F32)))
        yield
        grad_normed = grad_second
        grad = lax.dot_general(down_g, down_w[parts[0], :], NT, preferred_element_type=F32)
        yield
        for j, part in enumerate(parts):
            if j + 1 < len(parts):
                later = lax.dot_general(
                    down_g, down_w[parts[j + 1], :], NT, preferred_element_type=F32
                )
            up_g = (grad * slopes[slot, 0:rows, part]).astype(BF)
            up_g_out[0:rows, part] = up_g
            row = 8 + part.start // width
            lanes = slice(part.start % width, part.start % width + chunk)
            sums[row : row + 1, lanes] += column_sums(up_g.astype(F32))
            yield
            grad_normed = grad_normed + lax.dot_general(
                up_g, up_w[:, part], NT, preferred_element_type=F32
            )
            grad = later
            yield
        first_hat = first_hats[slot, 0:rows, :]
        grad_first = norm_backward(
            grad_normed, first_hat, inverses[slot, 0, 0:rows, 0:1], vector[4:5, :]
        )
        add_sum(4, column_sums(grad_normed * first_hat))
        add_sum(5, column_sums(grad_normed))
        first_g_out[0:rows, :] = grad_first
        attended_g = grad_first.astype(BF)
        attended_g_out[0:rows, :] = attended_g
        add_sum(2, column_sums(attended_g.astype(F32)))
        yield
        context_g_out[0:rows, :] = lax.dot_general(
            attended_g, out_w[...], NT, preferred_element_type=F32
        ).astype(BF)

    @pl.when(step == 0)
    def first_step():
        for copy in copies:
            copy.start()
        sums[...] = jnp.zeros_like(sums)
        copies[0].wait()
        if packed:
            unpack(raw_out, out_w, 256, 3)
        copies[1].wait()
        if packed:
            unpack(raw_up, up_w, width, 4)
        copies[2].wait()
        interleave(forward())

    @pl.when((step > 0) & (step < tiles))
    def middle_step():
        interleave(forward(), backward(tile))

    @pl.when(step == tiles)
    def last_step():
        interleave(backward(last_rows))
        if last_rows < tile:
            for ref in (down_g_out, up_g_out, first_g_out, attended_g_out, context_g_out):
                ref[last_rows:tile, :] = jnp.zeros((tile - last_rows, ref.shape[1]), ref.dtype)


def middle(frames, context, cotangent, vector, total, weights, hidden, valid, tile=256, chunk=768):
    count, width = frames.shape
    packed = len(weights) == 1
    tiles = count // tile
    last_rows = min(tile, valid - (tiles - 1) * tile)

    def early(columns):
        return pl.BlockSpec((tile, columns), lambda i: (jnp.minimum(i, tiles - 1), 0))

    def late(columns):
        return pl.BlockSpec((tile, columns), lambda i: (jnp.maximum(i - 1, 0), 0))

    anywhere = pl.BlockSpec(memory_space=pl.ANY)
    low = struct((count, width), BF)
    wide = struct((count, hidden), BF)
    raw = hidden if packed else 16
    return pl.pallas_call(
        partial(middle_kernel, packed, last_rows, chunk),
        grid=(tiles + 1,),
        in_specs=[
            pl.BlockSpec(memory_space=pltpu.SMEM),
            early(width),
            early(width),
            late(width),
            pl.BlockSpec(vector.shape, lambda i: (0, 0)),
        ]
        + [anywhere] * len(weights),
        out_specs=[
            early(width), early(width), early(hidden), late(width), late(hidden), late(width),
            late(width), late(width), pl.BlockSpec((24, width), lambda i: (0, 0)),
        ],
        out_shape=[
            low, low, wide, low, wide, struct((count, width), F32), low, low,
            struct((24, width), F32),
        ],
        scratch_shapes=[
            pltpu.VMEM((width, hidden), BF),
            pltpu.VMEM((hidden, width), BF),
            pltpu.VMEM((width, width), BF),
            pltpu.VMEM((raw, width), BF),
            pltpu.VMEM((raw, 256), BF),
            pltpu.VMEM((2, tile, hidden), F32),
            pltpu.VMEM((2, tile, width), F32),
            pltpu.VMEM((2, tile, width), F32),
            pltpu.VMEM((2, 2, tile, 128), F32),
            pltpu.SemaphoreType.DMA((3,)),
        ],
        compiler_params=params(),
        cost_estimate=cost(
            2 * count * width * (4 * hidden + 2 * width),
            count * (14 * width + 4 * hidden) + 4 * width * hidden,
            2 * count * hidden,
        ),
        name="feed_forward",
    )(total, frames, context, cotangent, vector, *weights)


def split_by_core(value, rows, first, mine, theirs):
    for chip in range(value.shape[0] // (2 * rows)):
        low = value[2 * chip * rows : (2 * chip + 1) * rows, :]
        high = value[(2 * chip + 1) * rows : (2 * chip + 2) * rows, :]
        mine[chip] = jnp.where(first, low, high).astype(BF)
        theirs[chip] = jnp.where(first, high, low).astype(BF)


def down_grad_kernel(valid, rows, coords, left, right, mine, theirs):
    value = lax.dot_general(
        left[0:valid, :], right[0:valid, :], TN, preferred_element_type=F32
    )
    first = coords[3] == 0
    width = right.shape[1]
    for chip in range(mine.shape[0]):
        for j in range(4):
            lanes = slice(j * width, (j + 1) * width)
            start = 8 * chip * rows + j * rows
            low = value[start : start + rows, :]
            high = value[start + 4 * rows : start + 5 * rows, :]
            mine[chip, :, lanes] = jnp.where(first, low, high).astype(BF)
            theirs[chip, :, lanes] = jnp.where(first, high, low).astype(BF)


def down_grad(place, left, right, valid, chips=4):
    count, hidden = left.shape
    width = right.shape[1]
    rows = width // place.count
    tile = 8 * rows * chips
    out = pl.BlockSpec((chips, rows, 4 * width), lambda i, c: (i, 0, 0))
    outs = struct((place.count // 2, rows, 4 * width), BF)
    return pl.pallas_call(
        partial(down_grad_kernel, valid, rows),
        grid_spec=pltpu.PrefetchScalarGridSpec(
            num_scalar_prefetch=1,
            grid=(hidden // tile,),
            in_specs=[
                pl.BlockSpec((count, tile), lambda i, c: (0, i)),
                pl.BlockSpec((count, width), lambda i, c: (0, 0)),
            ],
            out_specs=[out, out],
        ),
        out_shape=[outs, outs],
        compiler_params=params(),
        cost_estimate=cost(2 * count * hidden * width, 2 * count * (hidden + width)),
        name="grad_down",
    )(place.coords, left, right)


def up_grad_kernel(
    valid, rows, coords, left, right, out_left, out_right, mine, theirs, lefts, rights, sems
):
    step = pl.program_id(0)
    last = pl.num_programs(0) - 1
    copies = (
        pltpu.make_async_copy(out_left, lefts, sems.at[0]),
        pltpu.make_async_copy(out_right, rights, sems.at[1]),
    )

    @pl.when(step == 0)
    def fetch():
        for copy in copies:
            copy.start()

    @pl.when(step < last)
    def up_part():
        value = lax.dot_general(
            left[0:valid, :], right[0:valid, :], TN, preferred_element_type=F32
        )
        split_by_core(value, rows, coords[3] == 0, mine, theirs)

    @pl.when(step == last)
    def out_part():
        for copy in copies:
            copy.wait()
        value = lax.dot_general(
            lefts[0:valid, :], rights[0:valid, :], TN, preferred_element_type=F32
        )
        split_by_core(value, rows, coords[3] == 0, mine, theirs)


def up_grad(place, left, right, out_left, out_right, valid):
    count, width = left.shape
    rows = width // place.count
    steps = right.shape[1] // width + 1
    anywhere = pl.BlockSpec(memory_space=pl.ANY)
    out = pl.BlockSpec((place.count // 2, rows, width), lambda i, c: (0, 0, i))
    outs = struct((place.count // 2, rows, steps * width), BF)
    return pl.pallas_call(
        partial(up_grad_kernel, valid, rows),
        grid_spec=pltpu.PrefetchScalarGridSpec(
            num_scalar_prefetch=1,
            grid=(steps,),
            in_specs=[
                pl.BlockSpec((count, width), lambda i, c: (0, 0)),
                pl.BlockSpec((count, width), lambda i, c: (0, jnp.minimum(i, steps - 2))),
                anywhere,
                anywhere,
            ],
            out_specs=[out, out],
            scratch_shapes=[
                pltpu.VMEM((count, width), BF),
                pltpu.VMEM((count, width), BF),
                pltpu.SemaphoreType.DMA((2,)),
            ],
        ),
        out_shape=[outs, outs],
        compiler_params=params(),
        cost_estimate=cost(
            2 * count * steps * width * width, 2 * (count + width) * (steps + 1) * width
        ),
        name="grad_up_and_out",
    )(place.coords, left, right, out_left, out_right)


def qkv_grad_kernel(
    valid, rows, coords, left, right, sums, more, mine, theirs, kept, sent, entries, sems
):
    step = pl.program_id(0)
    width = left.shape[1]
    first = coords[3] == 0

    def copies(start, size, number):
        lanes = pl.ds(start, size)
        return (
            pltpu.make_async_copy(kept.at[:, :, lanes], mine.at[:, :, lanes], sems.at[0, number]),
            pltpu.make_async_copy(sent.at[:, :, lanes], theirs.at[:, :, lanes], sems.at[1, number]),
        )

    for which in range(3):

        @pl.when(step == which)
        def part(which=which):
            lanes = slice(which * width, (which + 1) * width)
            value = lax.dot_general(
                left[0:valid, :], right[0, 0:valid, :], TN, preferred_element_type=F32
            )
            split_by_core(value, rows, first, kept.at[:, :, lanes], sent.at[:, :, lanes])
            for copy in copies(which * width, width, which):
                copy.start()

    @pl.when(step == 2)
    def vector_part():
        pieces = width // 128
        entries[...] = jnp.zeros_like(entries)
        for row in range(12):
            value = sums[row : row + 1, :]
            if row < 2:
                value = value + more[row : row + 1, :]
            for j in range(pieces):
                entries[row * pieces + j : row * pieces + j + 1, :] = value[
                    :, j * 128 : (j + 1) * 128
                ]
        blank = jnp.zeros((rows - 4, 128), F32)
        lanes = slice(3 * width, 3 * width + 128)
        for chip in range(kept.shape[0]):
            windows = []
            for device in (2 * chip, 2 * chip + 1):
                start = 9 * (device // 4) + 2 * (device % 4)
                windows.append(jnp.concatenate([entries[start : start + 4, :], blank], axis=0))
            kept[chip, :, lanes] = jnp.where(first, windows[0], windows[1]).astype(BF)
            sent[chip, :, lanes] = jnp.where(first, windows[1], windows[0]).astype(BF)
        for copy in copies(3 * width, 128, 3):
            copy.start()
        for which in range(3):
            for copy in copies(which * width, width, which):
                copy.wait()
        for copy in copies(3 * width, 128, 3):
            copy.wait()


def qkv_grad(place, left, right, sums, more, valid):
    count, width = left.shape
    rows = width // place.count
    wire = (place.count // 2, rows, 3 * width + 128)
    anywhere = pl.BlockSpec(memory_space=pl.ANY)
    return pl.pallas_call(
        partial(qkv_grad_kernel, valid, rows),
        grid_spec=pltpu.PrefetchScalarGridSpec(
            num_scalar_prefetch=1,
            grid=(3,),
            in_specs=[
                pl.BlockSpec((count, width), lambda i, c: (0, 0)),
                pl.BlockSpec((1, count, width), lambda i, c: (i, 0, 0)),
                pl.BlockSpec(sums.shape, lambda i, c: (0, 0)),
                pl.BlockSpec(more.shape, lambda i, c: (0, 0)),
            ],
            out_specs=[anywhere, anywhere],
            scratch_shapes=[
                pltpu.VMEM(wire, BF),
                pltpu.VMEM(wire, BF),
                pltpu.VMEM((80, 128), F32),
                pltpu.SemaphoreType.DMA((2, 4)),
            ],
        ),
        out_shape=[struct(wire, BF)] * 2,
        compiler_params=params(),
        cost_estimate=cost(6 * count * width * width, 8 * (count + width) * width),
        name="grad_qkv",
    )(place.coords, left, right, sums, more)


def frames_grad_kernel(first_g, grads, weights, out):
    value = first_g[...]
    for which in range(3):
        value = value + lax.dot_general(
            grads[which], weights[which], NT, preferred_element_type=F32
        )
    out[...] = value.astype(BF)


def frames_gradient(first_g, grads, weights, tile=256):
    count, width = first_g.shape
    row_tile = pl.BlockSpec((tile, width), lambda i: (i, 0))
    return pl.pallas_call(
        frames_grad_kernel,
        grid=(count // tile,),
        in_specs=[
            row_tile,
            pl.BlockSpec((3, tile, width), lambda i: (0, i, 0)),
            pl.BlockSpec(weights.shape, lambda i: (0, 0, 0)),
        ],
        out_specs=row_tile,
        out_shape=struct((count, width), BF),
        compiler_params=params(),
        cost_estimate=cost(6 * count * width * width, 12 * count * width + 6 * width * width),
        name="frames_gradient",
    )(first_g, grads, weights)


def adam_update(master, first, second, gradient, step_rate, decay_rate):
    first_new = BETA_FIRST * first + (1.0 - BETA_FIRST) * gradient
    second_new = BETA_SECOND * second + (1.0 - BETA_SECOND) * gradient * gradient
    first_hat = first_new / (1.0 - BETA_FIRST**STEP)
    second_hat = second_new / (1.0 - BETA_SECOND**STEP)
    updated = master - step_rate * (
        first_hat / (jnp.sqrt(second_hat) + ADAM_EPS) + decay_rate * master
    )
    return (first_new, second_new, updated, updated.astype(BF))


def segment_marks(length_row, frame_count):
    clip_ends = jnp.cumsum(length_row)
    position = jnp.arange(frame_count, dtype=jnp.int32)
    segment = jnp.sum((clip_ends[None, :] <= position[:, None]).astype(jnp.int32), axis=1)
    lane = jnp.arange(128, dtype=jnp.int32)[None, :] % 64
    same = lane == segment[:, None]
    q_mark = jnp.where(same, 1.0, 0.0).astype(BF)
    k_mark = jnp.where(same | (lane >= 8), 0.0, -MASKED).astype(BF)
    return q_mark, k_mark, clip_ends[-1:].astype(jnp.int32)


def gather_vector(place, shard):
    blank = jnp.zeros((place.count, shard.shape[0]), BF)
    own = lax.dynamic_update_slice(blank, shard[None, :], (place.index, 0))
    return place.total(own)


def after(values, things):
    return lax.optimization_barrier((values, things))[0]


def shards(n_dp, n_fsdp, *arrays):
    (
        frames, cotangent, lengths, qkv_master, out_master, up_master, down_master, vector_master,
        qkv_first, qkv_second, out_first, out_second, up_first, up_second, down_first,
        down_second, vector_first, vector_second,
    ) = arrays
    place = Place(n_dp, n_fsdp)
    frame_count, width = frames.shape
    hidden = up_master.shape[1]
    rows = out_master.shape[0]
    valid = min(frame_count, -(-MOST_VALID // 16) * 16)
    fast = n_dp == 4 and place.depth == 4 and rows == 24

    q_mark, k_mark, total = segment_marks(lengths[0], frame_count)
    if fast:
        qkv_wire, wire_low = pack(
            place, qkv_master, out_master, up_master, down_master, vector_master[None, :]
        )
        wire = lax.all_gather(wire_low, AXES, axis=0, tiled=True)
        blocks = gather_blocks(place, qkv_wire)
        queries, keys, values, vector, qkv_full = project_qkv(place, frames, blocks)
        weights = (wire,)
    else:
        vector = gather_vector(place, vector_master.astype(BF)).astype(F32).reshape(-1, width)
        qkv_full = lax.all_gather(qkv_master.astype(BF), AXES, axis=1, tiled=True)
        projected = jnp.einsum("fd,cde->cfe", frames, qkv_full, preferred_element_type=F32)
        queries = (projected[0] + vector[0]).astype(BF)
        keys = projected[1].astype(BF)
        values = (projected[2] + vector[1]).astype(BF)
        weights = tuple(
            lax.all_gather(w.astype(BF), AXES, axis=0, tiled=True)
            for w in (out_master, up_master, down_master)
        )

    context, logs = attention_forward(queries, keys, values, q_mark, k_mark)
    (
        result, normed, activated, down_g, up_g, first_g, attended_g, context_g, sums,
    ) = middle(frames, context, cotangent, vector, total, weights, hidden, valid)

    def attention_part(first, pairs, start, earlier=()):
        return attention_backward(
            start, keys, values, context_g, q_mark, k_mark, logs, valid, first, pairs, earlier
        )

    if fast:
        down_mine, theirs = down_grad(place, activated, down_g, valid)
        down_got = place.swap_core(theirs)
        up_mine, theirs = up_grad(
            place, after(normed, down_mine), up_g, context, attended_g, valid
        )
        up_got = place.swap_core(theirs)
        all_sums = lax.all_gather(sums, AXES, axis=0)
        most = Reduction(place)
        done = most.first(after(down_mine, up_mine), down_got)
        grads = attention_part(0, 2, after(queries, done))
        done = most.first(after(up_mine, grads[1]), up_got)
        grads = attention_part(2, 2, after(queries, done), grads)
        most.parts[0] = after(most.parts[0], grads[1])
        done = most.second()
        qkv_g, bias_sums = attention_part(4, 2, after(queries, done), grads)
        most.sums = after(most.sums, bias_sums)
        done = most.third()
        mine, theirs = qkv_grad(place, after(frames, done), qkv_g, sums, bias_sums, valid)
        got = place.swap_core(theirs)
        frames_grad = frames_gradient(after(first_g, mine), qkv_g, qkv_full)
        most.sums = after(most.sums, frames_grad)
        done = most.fourth()
        last = Reduction(place)
        last.first(after(mine, done), got)
        done = last.second()
        most.sums = after(most.sums, done)
        last.third()
        last.fourth()
        grad_most = most.result()
        grad_qkv = last.result()
        grad_down = grad_most[:, : 4 * width].reshape(rows, 4, width)
        grad_down = grad_down.transpose(1, 0, 2).reshape(4 * rows, width)
        grad_up = grad_most[:, 4 * width : 8 * width]
        grad_out = grad_most[:, 8 * width :]
        window = grad_qkv[0:4, 3 * width :].reshape(-1)
        grad_vector = lax.dynamic_slice(
            window, (32 * (place.index % 4),), (vector_master.shape[0],)
        )
        grad_qkv = grad_qkv[:, : 3 * width].reshape(rows, 3, width).transpose(1, 0, 2)
        squares = jnp.sum(all_sums[:, 12:17], axis=(0, 2))
        layer_rms = jnp.sqrt(squares[0:4] / squares[4])
    else:
        def scatter(value, dimension):
            return lax.psum_scatter(value, AXES, scatter_dimension=dimension, tiled=True)

        def product(left, right):
            return lax.dot_general(left, right, TN, preferred_element_type=F32)

        qkv_g, bias_sums = attention_part(0, HEADS // 2, queries)
        grad_down = scatter(product(activated, down_g), 0)
        grad_up = scatter(product(normed, up_g), 0)
        grad_out = scatter(product(context, attended_g), 0)
        grad_qkv = scatter(jnp.stack([product(frames, qkv_g[i]) for i in range(3)]), 1)
        frames_grad = frames_gradient(first_g, qkv_g, qkv_full)
        sums = place.total(sums + jnp.pad(bias_sums, ((0, 16), (0, 0))))
        grad_vector = lax.dynamic_slice(
            sums[0:12].reshape(-1),
            (place.index * vector_master.shape[0],),
            (vector_master.shape[0],),
        )
        layer_rms = jnp.sqrt(jnp.sum(sums[12:16], axis=1) / jnp.sum(sums[16]))

    down_new = adam_update(
        down_master, down_first, down_second, grad_down, MATRIX_RATE, WEIGHT_DECAY
    )
    up_new = adam_update(up_master, up_first, up_second, grad_up, MATRIX_RATE, WEIGHT_DECAY)
    out_new = adam_update(out_master, out_first, out_second, grad_out, MATRIX_RATE, WEIGHT_DECAY)
    qkv_new = adam_update(qkv_master, qkv_first, qkv_second, grad_qkv, MATRIX_RATE, WEIGHT_DECAY)
    vector_new = adam_update(
        vector_master, vector_first, vector_second, grad_vector, VECTOR_RATE, 0.0
    )
    return (
        (result, frames_grad, layer_rms) + qkv_new + out_new + up_new + down_new + vector_new
    )


def solution(mesh):
    rows = P(AXES, None)
    middle_rows = P(None, AXES, None)
    entries = P(AXES)
    return jax.shard_map(
        partial(shards, mesh.shape["dp"], mesh.shape["fsdp"]),
        mesh=mesh,
        in_specs=(
            rows, rows, rows, middle_rows, rows, rows, rows, entries,
            middle_rows, middle_rows, rows, rows, rows, rows, rows, rows, entries, entries,
        ),
        out_specs=(rows, rows, P())
        + (middle_rows,) * 4
        + (rows,) * 12
        + (entries,) * 4,
        check_vma=False,
    )
```

time: 357 us -> 322 us (0.902)
  starting transfers between devices: 50.6 us -> 30.9 us
  Pallas kernels: 201 us -> 183 us
    ppermute x10 -> x4, waiting for transfers between devices: 34.8 us -> 11.4 us  [swap_z(): return lax.ppermute(value, 'fsdp', pairs)]
    all_gather x1, waiting for transfers between devices: 5.3 us -> 26 us  [shards(): wire = lax.all_gather(wire_low, AXES, axis=0, tiled=True)]
    ppermute x12 -> x3, starting transfers between devices: 18.7 us -> 6.11 us  [shift_z(): return lax.ppermute(value, 'fsdp', pairs)]
    pallas_call x11 -> x13, Pallas kernels: 130 us -> 120 us  [the longest x3 41.4 us: attention_backward(): pl.pallas_call(kernel, grid=(pairs,), in_specs=[column] * 4 + [whole] * 2...]
    ppermute x10 -> x4, starting transfers between devices: 11.6 us -> 3.51 us  [swap_z(): return lax.ppermute(value, 'fsdp', pairs)]
    pallas_call x3, Pallas kernels: 18.5 us -> 13.2 us  [first_add(): pl.pallas_call(first_add_kernel, grid_spec=pltpu.PrefetchScalarGridSpec(n...]
    ppermute x9 -> x8, waiting for transfers between devices: 7.13 us -> 11.6 us  [swap_y(): return lax.ppermute(value, 'dp', [(i, i ^ 2) for i in range(self.n_dp)])]
    ppermute x9 -> x8, starting transfers between devices: 8.64 us -> 11.5 us  [swap_x(): return lax.ppermute(value, 'dp', [(i, i ^ 1) for i in range(self.n_dp)])]
  transfers between devices with their start and end apart: 52 -> 36, of which waited for: 16 -> 19; matrix products, arithmetic and copies ran while one was open for 4% -> 3% of each run, Pallas kernels for 40% -> 44%
where the time goes in v2:
time: 322 us; the launch traced here: 316 us
  Pallas kernels  183 us (57%)
  waiting for transfers between devices  69.1 us (21%)
  starting transfers between devices  30.9 us (10%)
  between operations  14.9 us (5%)
  other arithmetic  11.4 us (4%)
  local copies, waits for them, and re-layouts  6.6 us (2%)
    pallas_call x3, Pallas kernels, attention_backward(): pl.pallas_call(kernel, grid=(pairs,), in_specs=[column] * 4 + [whole] * 2...  41.4 us
    pallas_call x1, Pallas kernels, middle(): pl.pallas_call(partial(middle_kernel, packed, last_rows, chunk), grid=(ti...  38.7 us
    all_gather x1, waiting for transfers between devices, shards(): wire = lax.all_gather(wire_low, AXES, axis=0, tiled=True)  26 us
    pallas_call x1, Pallas kernels, attention_forward(): pl.pallas_call(attention_forward_kernel, grid=(pairs,), in_specs=[column]...  22.5 us
    ppermute x8, waiting for transfers between devices, swap_x(): return lax.ppermute(value, 'dp', [(i, i ^ 1) for i in range(self.n_dp)])  13.6 us
    pallas_call x3, Pallas kernels, first_add(): pl.pallas_call(first_add_kernel, grid_spec=pltpu.PrefetchScalarGridSpec(n...  13.2 us
    ppermute x8, waiting for transfers between devices, swap_y(): return lax.ppermute(value, 'dp', [(i, i ^ 2) for i in range(self.n_dp)])  11.6 us
    pallas_call x1, Pallas kernels, up_grad(): pl.pallas_call(partial(up_grad_kernel, valid, rows), grid_spec=pltpu.Pref...  11.6 us
  transfers between devices with their start and end apart: 36, of which 19 were waited for; matrix products, arithmetic and copies ran while one was open for 3% of the time, Pallas kernels for 44%

profile of v2, /device:TPU:0, one launch (start us, length us, event | category | flops | bytes accessed | tf_op | source)
XLA Modules:
  0.0 316.3 jit_solution(10136156778500106411)
XLA Ops:
  11.2 3.1 collective-permute-start
  17.3 3.2 %collective-permute-done = bf16[24,2432]{1,0:T(8,128)(2,1)S(1)} collective-permute-done((bf16[24,2432]{1,0:T(8,128)(2,1)}, bf16[24,2432]{1,0:T(8,128)(2,1)S(1)}, u32[]{:S(2)}, u32[]{:S(2)}) %collective-permute-start) | collective-permute-done | bytes 116768 | tf_op jit(solution)/shard_map/ppermute | solution.py:73
  34.5 3.1 collective-permute-done.7.refs_6_
  47.2 9.6 %project_qkv.1 = (bf16[1024,768]{1,0:T(8,128)(2,1)}, bf16[1024,768]{1,0:T(8,128)(2,1)}, bf16[1024,768]{1,0:T(8,128)(2,1)}, f32[16,768]{1,0:T(8,128)}, bf16[3,768,768]{2,1,0:T(8,128)(2,1)}) custom-call(s32[5]{0:T(128)} %stack.41.coords, bf16[1024,768]{1,0:T(8,128)(2,1)} %left, bf16[2,24,2432]{2,1,0:T(8,128)(2,1)} %copy-done.11, ...), custom_call_target="tpu_custom_call" | custom-call | flops 3623878656 | bytes 7864320 | tf_op jit(solution)/shard_map/project_qkv/pallas_call | solution.py:356
  56.8 22.5 %attention_forward.1 = (bf16[1024,768]{1,0:T(8,128)(2,1)}, f32[6,8,1024]{2,1,0:T(8,128)}) custom-call(bf16[1024,768]{1,0:T(8,128)(2,1)} %get-tuple-element.146.q_ref.refs_0_, bf16[1024,768]{1,0:T(8,128)(2,1)} %get-tuple-element.104.k_ref.refs_1_, bf16[1024,768]{1,0:T(8,128)(2,1)} %get-tuple-element.105.v_ref.refs_2_, ...), custom_call_target="tpu_custom_call" | custom-call | flops 12884901888 | bytes 6291456 | tf_op jit(solution)/shard_map/attention_forward/pallas_call | solution.py:400
  79.3 26.0 %all-gather.4.cloned.1.call-done.refs_0_ = bf16[3072,1792]{1,0:T(8,128)(2,1)} async-done(((bf16[96,1792]{1,0:T(8,128)(2,1)}), bf16[3072,1792]{1,0:T(8,128)(2,1)}) %all-gather.4.cloned.1.call-update) | async-done | bytes 11010064 | tf_op jit(solution)/shard_map/all_gather | solution.py:1033
  105.3 38.7 %feed_forward.1 = (bf16[1024,768]{1,0:T(8,128)(2,1)}, bf16[1024,768]{1,0:T(8,128)(2,1)}, bf16[1024,3072]{1,0:T(8,128)(2,1)}, bf16[1024,768]{1,0:T(8,128)(2,1)}, ...) custom-call(s32[1]{0:T(128)} %bitcast.1.total_ref, ...), custom_call_target="tpu_custom_call" | custom-call | flops 21743271936000 | bytes 33030144000 | tf_op jit(solution)/shard_map/feed_forward/pallas_call | solution.py:712
  144.0 9.9 %grad_down.1 = (bf16[16,24,3072]{2,1,0:T(8,128)(2,1)}, bf16[16,24,3072]{2,1,0:T(8,128)(2,1)}) custom-call(s32[5]{0:T(128)} %stack.41.coords, bf16[1024,3072]{1,0:T(8,128)(2,1)} %get-tuple-element.111.left, bf16[1024,768]{1,0:T(8,128)(2,1)} %get-tuple-element.112.right), custom_call_target="tpu_custom_call" | custom-call | flops 4831838208000 | bytes 7864320000 | tf_op jit(solution)/shard_map/grad_down/pallas_call | solution.py:784
  154.1 11.6 %grad_up_and_out.1 = (bf16[16,24,3840]{2,1,0:T(8,128)(2,1)}, bf16[16,24,3840]{2,1,0:T(8,128)(2,1)}) custom-call(s32[5]{0:T(128)} %stack.41.coords, bf16[1024,768]{1,0:T(8,128)(2,1)} %get-tuple-element.115.left, bf16[1024,3072]{1,0:T(8,128)(2,1)} %get-tuple-element.116.right, bf16[1024,768]{1,0:T(8,128)(2,1)} %get-tuple-element.106.context.out_left, ...), custom_call_target="tpu_custom_call" | custom-call | flops 6039797760000 | bytes 16515072000 | tf_op jit(solution)/shard_map/grad_up_and_out/pallas_call | solution.py:841
  166.0 4.3 %reduce_over_core.3 = (bf16[2,2,24,3072]{3,2,1,0:T(8,128)(2,1)}, bf16[2,2,24,3072]{3,2,1,0:T(8,128)(2,1)}, bf16[2,2,24,3072]{3,2,1,0:T(8,128)(2,1)}, bf16[2,2,24,3072]{3,2,1,0:T(8,128)(2,1)}) custom-call(s32[5]{0:T(128)} %stack.41.coords, bf16[2,2,4,24,3072]{4,3,2,1,0:T(8,128)(2,1)} %bitcast.55, ...), custom_call_target="tpu_custom_call" | custom-call | flops 1179648000 | bytes 7077888000 | tf_op jit(solution)/shard_map/reduce_over_core/pallas_call | solution.py:127
  172.4 13.7 %attention_backward.3 = (bf16[3,1024,768]{2,1,0:T(8,128)(2,1)}, f32[8,768]{1,0:T(8,128)}) custom-call(bf16[1024,768]{1,0:T(8,128)(2,1)} %get-tuple-element.146.q_ref.refs_0_, bf16[1024,768]{1,0:T(8,128)(2,1)} %get-tuple-element.104.k_ref.refs_1_, bf16[1024,768]{1,0:T(8,128)(2,1)} %get-tuple-element.105.v_ref.refs_2_, ...), custom_call_target="tpu_custom_call" | custom-call | flops 10737418240000 | bytes 3670016000 | tf_op jit(solution)/shard_map/attention_backward/pallas_call | solution.py:469
  186.1 4.8 %reduce_over_core.4 = (bf16[2,2,24,3840]{3,2,1,0:T(8,128)(2,1)}, bf16[2,2,24,3840]{3,2,1,0:T(8,128)(2,1)}, bf16[2,2,24,3840]{3,2,1,0:T(8,128)(2,1)}, bf16[2,2,24,3840]{3,2,1,0:T(8,128)(2,1)}) custom-call(s32[5]{0:T(128)} %stack.41.coords, bf16[2,2,4,24,3840]{4,3,2,1,0:T(8,128)(2,1)} %bitcast.51, ...), custom_call_target="tpu_custom_call" | custom-call | flops 1474560000 | bytes 8847360000 | tf_op jit(solution)/shard_map/reduce_over_core/pallas_call | solution.py:127
  193.0 13.9 %attention_backward.4 = (bf16[3,1024,768]{2,1,0:T(8,128)(2,1)}, f32[8,768]{1,0:T(8,128)}) custom-call(bf16[1024,768]{1,0:T(8,128)(2,1)} %get-tuple-element.146.q_ref.refs_0_, bf16[1024,768]{1,0:T(8,128)(2,1)} %get-tuple-element.104.k_ref.refs_1_, bf16[1024,768]{1,0:T(8,128)(2,1)} %get-tuple-element.105.v_ref.refs_2_, ...), custom_call_target="tpu_custom_call", output_to_operand_aliasing={{0}: (7, {}), {1}: (8, {})} | custom-call | flops 10737418240000 | bytes 3670016000 | tf_op jit(solution)/shard_map/attention_backward/pallas_call | solution.py:469
  210.6 4.9 %reduce_over_first_link.2 = (bf16[2,24,6912]{2,1,0:T(8,128)(2,1)}, bf16[2,24,6912]{2,1,0:T(8,128)(2,1)}, bf16[2,24,6912]{2,1,0:T(8,128)(2,1)}, bf16[2,24,6912]{2,1,0:T(8,128)(2,1)}) custom-call(s32[5]{0:T(128)} %stack.41.coords, bf16[2,2,24,3072]{3,2,1,0:T(8,128)(2,1)} %get-tuple-element.135.refs_0_.refs_2_, ...), custom_call_target="tpu_custom_call" | custom-call | flops 1327104000 | bytes 7962624000 | tf_op jit(solution)/shard_map/reduce_over_first_link/pallas_call | solution.py:168
  217.5 13.7 %attention_backward.5 = (bf16[3,1024,768]{2,1,0:T(8,128)(2,1)}, f32[8,768]{1,0:T(8,128)}) custom-call(bf16[1024,768]{1,0:T(8,128)(2,1)} %get-tuple-element.146.q_ref.refs_0_, bf16[1024,768]{1,0:T(8,128)(2,1)} %get-tuple-element.104.k_ref.refs_1_, bf16[1024,768]{1,0:T(8,128)(2,1)} %get-tuple-element.105.v_ref.refs_2_, ...), custom_call_target="tpu_custom_call", output_to_operand_aliasing={{0}: (7, {}), {1}: (8, {})} | custom-call | flops 10737418240000 | bytes 3670016000 | tf_op jit(solution)/shard_map/attention_backward/pallas_call | solution.py:469
  231.4 3.0 reduce_over_second_link.2
  235.6 8.9 %grad_qkv.1 = (bf16[16,24,2432]{2,1,0:T(8,128)(2,1)}, bf16[16,24,2432]{2,1,0:T(8,128)(2,1)}) custom-call(s32[5]{0:T(128)} %stack.41.coords, bf16[1024,768]{1,0:T(8,128)(2,1)} %left, bf16[3,1024,768]{2,1,0:T(8,128)(2,1)} %get-tuple-element.155.right.grads, f32[24,768]{1,0:T(8,128)} %get-tuple-element.156.sums, f32[8,768]{1,0:T(8,128)} %get-tuple-element.148.more), custom_call_target="tpu_custom_call" | custom-call | flops 3623878656000 | bytes 11010048000 | tf_op jit(solution)/shard_map/grad_qkv/pallas_call | solution.py:929
  244.5 8.5 %frames_gradient.1 = bf16[1024,768]{1,0:T(8,128)(2,1)} custom-call(f32[1024,768]{1,0:T(8,128)} %get-tuple-element.158.first_g, bf16[3,1024,768]{2,1,0:T(8,128)(2,1)} %get-tuple-element.155.right.grads, bf16[3,768,768]{2,1,0:T(8,128)(2,1)} %get-tuple-element.159.weights), custom_call_target="tpu_custom_call" | custom-call | flops 3623878656000 | bytes 12976128000 | tf_op jit(solution)/shard_map/frames_gradient/pallas_call | solution.py:967
  255.3 4.1 %reduce_over_core.5 = (bf16[2,2,24,2432]{3,2,1,0:T(8,128)(2,1)}, bf16[2,2,24,2432]{3,2,1,0:T(8,128)(2,1)}, bf16[2,2,24,2432]{3,2,1,0:T(8,128)(2,1)}, bf16[2,2,24,2432]{3,2,1,0:T(8,128)(2,1)}) custom-call(s32[5]{0:T(128)} %stack.41.coords, bf16[2,2,4,24,2432]{4,3,2,1,0:T(8,128)(2,1)} %bitcast.59, ...), custom_call_target="tpu_custom_call" | custom-call | flops 933888000 | bytes 5603328000 | tf_op jit(solution)/shard_map/reduce_over_core/pallas_call | solution.py:127
  266.0 6.7 %collective-permute-done.27.refs_1_.refs_3_ = bf16[2,2,24,2432]{3,2,1,0:T(8,128)(2,1)S(1)} collective-permute-done((bf16[2,2,24,2432]{3,2,1,0:T(8,128)(2,1)}, bf16[2,2,24,2432]{3,2,1,0:T(8,128)(2,1)S(1)}, u32[]{:S(2)}, u32[]{:S(2)}) %collective-permute-start.27) | collective-permute-done | bytes 466976 | tf_op jit(solution)/shard_map/ppermute | solution.py:62
  274.7 3.2 %reduce_over_first_link.3 = (bf16[2,24,2432]{2,1,0:T(8,128)(2,1)}, bf16[2,24,2432]{2,1,0:T(8,128)(2,1)}, bf16[2,24,2432]{2,1,0:T(8,128)(2,1)}, bf16[2,24,2432]{2,1,0:T(8,128)(2,1)}) custom-call(s32[5]{0:T(128)} %stack.41.coords, bf16[2,2,24,2432]{3,2,1,0:T(8,128)(2,1)} %get-tuple-element.166.refs_0_.refs_2_, bf16[2,2,24,2432]{3,2,1,0:T(8,128)(2,1)} %copy-done, ...), custom_call_target="tpu_custom_call" | custom-call | flops 466944000 | bytes 2801664000 | tf_op jit(solution)/shard_map/reduce_over_first_link/pallas_call | solution.py:168
  282.6 4.0 %collective-permute-done.29.got_a = bf16[2,24,2432]{2,1,0:T(8,128)(2,1)S(1)} collective-permute-done((bf16[2,24,2432]{2,1,0:T(8,128)(2,1)}, bf16[2,24,2432]{2,1,0:T(8,128)(2,1)S(1)}, u32[]{:S(2)}, u32[]{:S(2)}) %collective-permute-start.29) | collective-permute-done | bytes 233504 | tf_op jit(solution)/shard_map/ppermute | solution.py:65
  291.9 5.2 %collective-permute-done.31.got = bf16[2,24,2432]{2,1,0:T(8,128)(2,1)S(1)} collective-permute-done((bf16[2,24,2432]{2,1,0:T(8,128)(2,1)}, bf16[2,24,2432]{2,1,0:T(8,128)(2,1)S(1)}, u32[]{:S(2)}, u32[]{:S(2)}) %collective-permute-start.31) | collective-permute-done | bytes 233504 | tf_op jit(solution)/shard_map/ppermute | solution.py:77
  301.5 5.0 %collective-permute-done.32 = bf16[24,2432]{1,0:T(8,128)(2,1)S(1)} collective-permute-done((bf16[24,2432]{1,0:T(8,128)(2,1)}, bf16[24,2432]{1,0:T(8,128)(2,1)S(1)}, u32[]{:S(2)}, u32[]{:S(2)}) %collective-permute-start.32) | collective-permute-done | bytes 116768 | tf_op jit(solution)/shard_map/ppermute | solution.py:77
  (170 shorter events, 69.9 us)
Async XLA Ops:
  7.2 98.1 %all-gather.4.cloned.1.call-start = ((), (), s32[]{:S(2)}) async-start(), calls=%async_computation | async-start | bytes 11354112 | tf_op jit(solution)/shard_map/all_gather | solution.py:1033
  11.2 251.3 %all-gather.6.cloned.1.call-start = ((), (), s32[]{:S(2)}) async-start(), calls=%async_computation.1 | async-start | bytes 2433024 | tf_op jit(solution)/shard_map/all_gather | solution.py:1066
  11.2 9.3 %collective-permute-start = (bf16[24,2432]{1,0:T(8,128)(2,1)}, bf16[24,2432]{1,0:T(8,128)(2,1)S(1)}, u32[]{:S(2)}, u32[]{:S(2)}) collective-permute-start(bf16[24,2432]{1,0:T(8,128)(2,1)} %get-tuple-element.102), channel_id=1, source_target_pairs={{0,2},{1,3},{2,4},{3,5},{4,6},{5,7},{6,0},{7,1},{8,10},{9,11},{10,... | collective-permute-start | bytes 350216 | tf_op jit(solution)/shard_map/ppermute | solution.py:73
  14.3 10.6 %collective-permute-start.5 = (bf16[24,2432]{1,0:T(8,128)(2,1)}, bf16[24,2432]{1,0:T(8,128)(2,1)S(1)}, u32[]{:S(2)}, u32[]{:S(2)}) collective-permute-start(bf16[24,2432]{1,0:T(8,128)(2,1)} %get-tuple-element.102), channel_id=1, source_target_pairs={{0,6},{1,7},{2,0},{3,1},{4,2},{5,3},{6,4},{7,5},{8,14},{9,15},{10,... | collective-permute-start | bytes 350216 | tf_op jit(solution)/shard_map/ppermute | solution.py:73
  16.4 11.3 %collective-permute-start.4 = (bf16[24,2432]{1,0:T(8,128)(2,1)}, bf16[24,2432]{1,0:T(8,128)(2,1)S(1)}, u32[]{:S(2)}, u32[]{:S(2)}) collective-permute-start(bf16[24,2432]{1,0:T(8,128)(2,1)} %get-tuple-element.102), channel_id=1, source_target_pairs={{0,4},{1,5},{2,6},{3,7},{4,0},{5,1},{6,2},{7,3},{8,12},{9,13},{10,... | collective-permute-start | bytes 350216 | tf_op jit(solution)/shard_map/ppermute | solution.py:73
  21.6 11.0 %collective-permute-start.2 = (bf16[2,24,2432]{2,1,0:T(8,128)(2,1)S(1)}, bf16[2,24,2432]{2,1,0:T(8,128)(2,1)S(1)}, u32[]{:S(2)}, u32[]{:S(2)}) collective-permute-start(bf16[2,24,2432]{2,1,0:T(8,128)(2,1)S(1)} %pad_maximum_fusion.refs_0_), channel_id=1, source_target_pairs={{0,16},{8,24},{16,0},{24,8},{1,17},{9,25},{17,1},{25,9},{2,18},{10... | collective-permute-start | bytes 700424 | tf_op jit(solution)/shard_map/ppermute | solution.py:65
  23.3 10.0 %collective-permute-start.1 = (bf16[2,24,2432]{2,1,0:T(8,128)(2,1)S(1)}, bf16[2,24,2432]{2,1,0:T(8,128)(2,1)S(1)}, u32[]{:S(2)}, u32[]{:S(2)}) collective-permute-start(bf16[2,24,2432]{2,1,0:T(8,128)(2,1)S(1)} %pad_maximum_fusion.refs_0_), channel_id=1, source_target_pairs={{0,8},{8,0},{16,24},{24,16},{1,9},{9,1},{17,25},{25,17},{2,10},{10... | collective-permute-start | bytes 700424 | tf_op jit(solution)/shard_map/ppermute | solution.py:62
  27.7 9.9 %collective-permute-start.7 = (bf16[2,24,2432]{2,1,0:T(8,128)(2,1)S(1)}, bf16[2,24,2432]{2,1,0:T(8,128)(2,1)S(1)}, u32[]{:S(2)}, u32[]{:S(2)}) collective-permute-start(bf16[2,24,2432]{2,1,0:T(8,128)(2,1)S(1)} %pad_maximum_fusion.1.refs_4_), channel_id=1, source_target_pairs={{0,16},{8,24},{16,0},{24,8},{1,17},{9,25},{17,1},{25,9},{2,18},{10... | collective-permute-start | bytes 700424 | tf_op jit(solution)/shard_map/ppermute | solution.py:65
  29.4 11.4 %collective-permute-start.13 = (bf16[2,24,2432]{2,1,0:T(8,128)(2,1)S(1)}, bf16[2,24,2432]{2,1,0:T(8,128)(2,1)S(1)}, u32[]{:S(2)}, u32[]{:S(2)}) collective-permute-start(bf16[2,24,2432]{2,1,0:T(8,128)(2,1)S(1)} %pad_maximum_fusion.1.refs_4_), channel_id=1, source_target_pairs={{0,1},{1,0},{2,3},{3,2},{4,5},{5,4},{6,7},{7,6},{8,9},{9,8},{10,11... | collective-permute-start | bytes 700424 | tf_op jit(solution)/shard_map/ppermute | solution.py:68
  29.4 11.4 %collective-permute-start.6 = (bf16[2,24,2432]{2,1,0:T(8,128)(2,1)S(1)}, bf16[2,24,2432]{2,1,0:T(8,128)(2,1)S(1)}, u32[]{:S(2)}, u32[]{:S(2)}) collective-permute-start(bf16[2,24,2432]{2,1,0:T(8,128)(2,1)S(1)} %pad_maximum_fusion.1.refs_4_), channel_id=1, source_target_pairs={{0,8},{8,0},{16,24},{24,16},{1,9},{9,1},{17,25},{25,17},{2,10},{10... | collective-permute-start | bytes 700424 | tf_op jit(solution)/shard_map/ppermute | solution.py:62
  32.6 8.8 %collective-permute-start.11 = (bf16[2,24,2432]{2,1,0:T(8,128)(2,1)S(1)}, bf16[2,24,2432]{2,1,0:T(8,128)(2,1)S(1)}, u32[]{:S(2)}, u32[]{:S(2)}) collective-permute-start(bf16[2,24,2432]{2,1,0:T(8,128)(2,1)S(1)} %collective-permute-done.2.refs_2_), channel_id=1, source_target_pairs={{0,1},{1,0},{2,3},{3,2},{4,5},{5,4},{6,7},{7,6},{8,9},{9,8},{10,11... | collective-permute-start | bytes 700424 | tf_op jit(solution)/shard_map/ppermute | solution.py:68
  153.9 12.1 %collective-permute-start.17 = (bf16[16,24,3072]{2,1,0:T(8,128)(2,1)}, bf16[16,24,3072]{2,1,0:T(8,128)(2,1)}, u32[]{:S(2)}, u32[]{:S(2)}) collective-permute-start(bf16[16,24,3072]{2,1,0:T(8,128)(2,1)} %get-tuple-element.120), channel_id=1, source_target_pairs={{0,1},{1,0},{2,3},{3,2},{4,5},{5,4},{6,7},{7,6},{8,9},{9,8},{10,11... | collective-permute-start | bytes 7077896 | tf_op jit(solution)/shard_map/ppermute | solution.py:68
  165.7 20.4 %collective-permute-start.20 = (bf16[16,24,3840]{2,1,0:T(8,128)(2,1)}, bf16[16,24,3840]{2,1,0:T(8,128)(2,1)}, u32[]{:S(2)}, u32[]{:S(2)}) collective-permute-start(bf16[16,24,3840]{2,1,0:T(8,128)(2,1)} %get-tuple-element.130), channel_id=1, source_target_pairs={{0,1},{1,0},{2,3},{3,2},{4,5},{5,4},{6,7},{7,6},{8,9},{9,8},{10,11... | collective-permute-start | bytes 8847368 | tf_op jit(solution)/shard_map/ppermute | solution.py:68
  170.3 36.6 %collective-permute-start.18 = (bf16[2,2,24,3072]{3,2,1,0:T(8,128)(2,1)}, bf16[2,2,24,3072]{3,2,1,0:T(8,128)(2,1)}, u32[]{:S(2)}, u32[]{:S(2)}) collective-permute-start(bf16[2,2,24,3072]{3,2,1,0:T(8,128)(2,1)} %get-tuple-element.122), channel_id=1, source_target_pairs={{0,8},{8,0},{16,24},{24,16},{1,9},{9,1},{17,25},{25,17},{2,10},{10... | collective-permute-start | bytes 1769480 | tf_op jit(solution)/shard_map/ppermute | solution.py:62
  171.8 35.1 %collective-permute-start.19 = (bf16[2,2,24,3072]{3,2,1,0:T(8,128)(2,1)}, bf16[2,2,24,3072]{3,2,1,0:T(8,128)(2,1)}, u32[]{:S(2)}, u32[]{:S(2)}) collective-permute-start(bf16[2,2,24,3072]{3,2,1,0:T(8,128)(2,1)} %get-tuple-element.124), channel_id=1, source_target_pairs={{0,16},{8,24},{16,0},{24,8},{1,17},{9,25},{17,1},{25,9},{2,18},{10... | collective-permute-start | bytes 1769480 | tf_op jit(solution)/shard_map/ppermute | solution.py:65
  190.9 18.5 %collective-permute-start.21 = (bf16[2,2,24,3840]{3,2,1,0:T(8,128)(2,1)}, bf16[2,2,24,3840]{3,2,1,0:T(8,128)(2,1)}, u32[]{:S(2)}, u32[]{:S(2)}) collective-permute-start(bf16[2,2,24,3840]{3,2,1,0:T(8,128)(2,1)} %get-tuple-element.139), channel_id=1, source_target_pairs={{0,8},{8,0},{16,24},{24,16},{1,9},{9,1},{17,25},{25,17},{2,10},{10... | collective-permute-start | bytes 2211848 | tf_op jit(solution)/shard_map/ppermute | solution.py:62
  192.5 18.1 %collective-permute-start.22 = (bf16[2,2,24,3840]{3,2,1,0:T(8,128)(2,1)}, bf16[2,2,24,3840]{3,2,1,0:T(8,128)(2,1)}, u32[]{:S(2)}, u32[]{:S(2)}) collective-permute-start(bf16[2,2,24,3840]{3,2,1,0:T(8,128)(2,1)} %get-tuple-element.141), channel_id=1, source_target_pairs={{0,16},{8,24},{16,0},{24,8},{1,17},{9,25},{17,1},{25,9},{2,18},{10... | collective-permute-start | bytes 2211848 | tf_op jit(solution)/shard_map/ppermute | solution.py:65
  215.5 15.7 %collective-permute-start.23 = (bf16[2,24,6912]{2,1,0:T(8,128)(2,1)}, bf16[2,24,6912]{2,1,0:T(8,128)(2,1)}, u32[]{:S(2)}, u32[]{:S(2)}) collective-permute-start(bf16[2,24,6912]{2,1,0:T(8,128)(2,1)} %get-tuple-element.143), channel_id=1, source_target_pairs={{0,16},{8,24},{16,0},{24,8},{1,17},{9,25},{17,1},{25,9},{2,18},{10... | collective-permute-start | bytes 1990664 | tf_op jit(solution)/shard_map/ppermute | solution.py:65
  216.0 15.4 %collective-permute-start.24 = (bf16[2,24,6912]{2,1,0:T(8,128)(2,1)}, bf16[2,24,6912]{2,1,0:T(8,128)(2,1)}, u32[]{:S(2)}, u32[]{:S(2)}) collective-permute-start(bf16[2,24,6912]{2,1,0:T(8,128)(2,1)} %get-tuple-element.145), channel_id=1, source_target_pairs={{0,8},{8,0},{16,24},{24,16},{1,9},{9,1},{17,25},{25,17},{2,10},{10... | collective-permute-start | bytes 1990664 | tf_op jit(solution)/shard_map/ppermute | solution.py:62
  234.4 18.7 %collective-permute-start.25 = (bf16[2,24,6912]{2,1,0:T(8,128)(2,1)}, bf16[2,24,6912]{2,1,0:T(8,128)(2,1)}, u32[]{:S(2)}, u32[]{:S(2)}) collective-permute-start(bf16[2,24,6912]{2,1,0:T(8,128)(2,1)} %get-tuple-element.160), channel_id=1, source_target_pairs={{0,2},{1,3},{2,0},{3,1},{4,6},{5,7},{6,4},{7,5},{8,10},{9,11},{10,... | collective-permute-start | bytes 1990664 | tf_op jit(solution)/shard_map/ppermute | solution.py:77
  244.4 10.9 %collective-permute-start.26 = (bf16[16,24,2432]{2,1,0:T(8,128)(2,1)}, bf16[16,24,2432]{2,1,0:T(8,128)(2,1)}, u32[]{:S(2)}, u32[]{:S(2)}) collective-permute-start(bf16[16,24,2432]{2,1,0:T(8,128)(2,1)} %get-tuple-element.165), channel_id=1, source_target_pairs={{0,1},{1,0},{2,3},{3,2},{4,5},{5,4},{6,7},{7,6},{8,9},{9,8},{10,11... | collective-permute-start | bytes 5603336 | tf_op jit(solution)/shard_map/ppermute | solution.py:68
  259.4 13.3 %collective-permute-start.27 = (bf16[2,2,24,2432]{3,2,1,0:T(8,128)(2,1)}, bf16[2,2,24,2432]{3,2,1,0:T(8,128)(2,1)S(1)}, u32[]{:S(2)}, u32[]{:S(2)}) collective-permute-start(bf16[2,2,24,2432]{3,2,1,0:T(8,128)(2,1)} %get-tuple-element.167), channel_id=1, source_target_pairs={{0,8},{8,0},{16,24},{24,16},{1,9},{9,1},{17,25},{25,17},{2,10},{10... | collective-permute-start | bytes 1400840 | tf_op jit(solution)/shard_map/ppermute | solution.py:62
  260.9 13.0 %collective-permute-start.28 = (bf16[2,2,24,2432]{3,2,1,0:T(8,128)(2,1)}, bf16[2,2,24,2432]{3,2,1,0:T(8,128)(2,1)S(1)}, u32[]{:S(2)}, u32[]{:S(2)}) collective-permute-start(bf16[2,2,24,2432]{3,2,1,0:T(8,128)(2,1)} %get-tuple-element.169), channel_id=1, source_target_pairs={{0,16},{8,24},{16,0},{24,8},{1,17},{9,25},{17,1},{25,9},{2,18},{10... | collective-permute-start | bytes 1400840 | tf_op jit(solution)/shard_map/ppermute | solution.py:65
  261.5 17.6 %collective-permute-start.33 = (bf16[24,6912]{1,0:T(8,128)(2,1)S(1)}, bf16[24,6912]{1,0:T(8,128)(2,1)S(1)}, u32[]{:S(2)}, u32[]{:S(2)}) collective-permute-start(bf16[24,6912]{1,0:T(8,128)(2,1)S(1)} %copy-done.22), channel_id=1, source_target_pairs={{0,4},{1,5},{2,6},{3,7},{4,0},{5,1},{6,2},{7,3},{8,12},{9,13},{10,... | collective-permute-start | bytes 995336 | tf_op jit(solution)/shard_map/ppermute | solution.py:77
  (50 other events, 455.6 us)
Sparse Core Ops, SparseCore 0:
  11.6 93.6 all-gather.3
  144.1 55.8 all-gather.5

commit v3 on v2

--- a/solution.py
+++ b/solution.py
@@ -9,6 +9,8 @@
 
 HEADS = 12
 STEP = 10
+LONG = 780
+SHORT = 150
 MOST_VALID = 900
 
 MASKED = 1e30
@@ -134,7 +136,7 @@
         ),
         out_shape=[struct((2, half, rows, columns), BF)] * 4,
         compiler_params=params(),
-        cost_estimate=cost(mine.size, 6 * mine.size),
+        cost_estimate=cost(mine.size, 6 * mine.size, times=10**6),
         name="reduce_over_core",
     )(place.coords, *([mine, got] * 4))
 
@@ -175,7 +177,9 @@
         ),
         out_shape=[struct(shape, BF)] * 4,
         compiler_params=params(),
-        cost_estimate=cost(4 * half * rows * shape[2], 24 * half * rows * shape[2]),
+        cost_estimate=cost(
+            4 * half * rows * shape[2], 24 * half * rows * shape[2], times=10**6
+        ),
         name="reduce_over_first_link",
     )(place.coords, *ins)
 
@@ -187,21 +191,31 @@
         out[1] = rounded_sum(keep_b[which], got_b[which])
 
 
+def spread_add_kernel(coords, keep_a, got_a, keep_b, got_b, *outs):
+    half = keep_a.shape[0]
+    for step, out in enumerate(outs):
+        target = lax.rem(coords[2] + step, 2 * half)
+        inner = lax.rem(target, half)
+        near = keep_a[inner].astype(F32) + got_a[inner].astype(F32)
+        far = keep_b[inner].astype(F32) + got_b[inner].astype(F32)
+        out[...] = jnp.where(target < half, near, far).astype(BF)
+
+
 def fourth_add_kernel(coords, keep, got, keep_out, send):
     own = lax.div(coords[2], 2)
     keep_out[...] = rounded_sum(keep[own], got[own])
     send[...] = rounded_sum(keep[1 - own], got[1 - own])
 
 
-def small_add(place, kernel, ins, shape, name):
+def small_add(place, kernel, ins, shape, name, times=10**6, outs=2):
     inside = pl.BlockSpec(memory_space=pltpu.VMEM)
     return pl.pallas_call(
         kernel,
         in_specs=[pl.BlockSpec(memory_space=pltpu.SMEM)] + [inside] * len(ins),
-        out_specs=[inside] * 2,
-        out_shape=[struct(shape, BF)] * 2,
+        out_specs=[inside] * outs,
+        out_shape=[struct(shape, BF)] * outs,
         compiler_params=params(),
-        cost_estimate=cost(2 * ins[0].size, 6 * ins[0].size),
+        cost_estimate=cost(2 * ins[0].size, 6 * ins[0].size, times=times),
         name=name,
     )(place.coords, *ins)
 
@@ -223,24 +237,38 @@
         self.sums = (keep_a, place.swap_y(send_a), keep_b, place.swap_x(send_b))
         return keep_a
 
-    def third(self):
+    def third(self, times=10**6):
         place = self.place
         keep, send = small_add(
-            place, third_add_kernel, self.sums, self.sums[0].shape, "reduce_over_second_link"
+            place, third_add_kernel, self.sums, self.sums[0].shape, "reduce_over_second_link", times
         )
         self.sums = (keep, place.swap_z(send, 1))
         return keep
 
-    def fourth(self):
+    def fourth(self, times=10**6):
         place = self.place
         keep, send = small_add(
-            place, fourth_add_kernel, self.sums, self.sums[0].shape[1:], "reduce_over_z"
+            place, fourth_add_kernel, self.sums, self.sums[0].shape[1:], "reduce_over_z", times
         )
         self.sums = (keep, place.swap_z(send, 2))
         return keep
 
+    def spread(self):
+        place = self.place
+        blocks = small_add(
+            place, spread_add_kernel, self.sums, self.sums[0].shape[1:],
+            "reduce_over_second_link", outs=place.depth,
+        )
+        self.sums = (blocks[0],) + tuple(
+            place.shift_z(blocks[step], step) for step in range(1, place.depth)
+        )
+        return blocks[0]
+
     def result(self):
-        return self.sums[0].astype(F32) + self.sums[1].astype(F32)
+        total = self.sums[0].astype(F32)
+        for part in self.sums[1:]:
+            total = total + part.astype(F32)
+        return total
 
 
 def pack_kernel(coords, qkv, out, up, down, vector, qkv_wire, wire, line):
@@ -279,53 +307,41 @@
 
 def qkv_kernel(depth, coords, frames, *refs):
     blocks = refs[:16]
-    q_ref, k_ref, v_ref, vector_out, w_out, raw, weights, entries, sems, out_sem = refs[16:]
+    q_ref, k_ref, v_ref, vector_out, w_out, weights, windows, entries, sem = refs[16:]
     half = depth // 2
-    chips = 4 * depth
-    rows = raw.shape[1]
+    rows = blocks[0].shape[1]
     width = weights.shape[2]
     outs = (q_ref, k_ref, v_ref)
+    copy = pltpu.make_async_copy(weights, w_out, sem)
 
     @pl.when(pl.program_id(0) == 0)
-    def load():
-        copies = []
-        for number, block in enumerate(blocks):
-            core = number // 8
-            far = (number // 4) % 2
-            dy = (number // 2) % 2
-            dx = number % 2
-            y = (coords[0] + dy) % 2
-            x = (coords[1] + dx) % 2
-            other = (coords[3] + core) % 2
+    def assemble():
+        first_core = coords[3] == 0
+        for number in range(8):
+            far = number // 4
+            y = (coords[0] + (number // 2) % 2) % 2
+            x = (coords[1] + number % 2) % 2
             for j in range(half):
                 z = (coords[2] + depth - (far * half + j)) % depth
-                device = ((y * 2 + x) * depth + z) * 2 + other
-                copies.append(
-                    pltpu.make_async_copy(block.at[j], raw.at[device], sems.at[number, j])
-                )
-        for copy in copies:
-            copy.start()
+                chip = (y * 2 + x) * depth + z
+                start = pl.multiple_of(chip * 2 * rows, 16)
+                for which in range(3):
+                    part = slice(which * width, (which + 1) * width)
+                    own = blocks[number][j, :, part].astype(F32)
+                    other = blocks[number + 8][j, :, part].astype(F32)
+                    low = jnp.where(first_core, own, other)
+                    high = jnp.where(first_core, other, own)
+                    weights[which, pl.ds(start, 2 * rows), :] = jnp.concatenate(
+                        [low, high], axis=0
+                    ).astype(BF)
+                part = slice(3 * width, 3 * width + 128)
+                windows[chip * 2 + coords[3]] = blocks[number][j, :, part].astype(F32)[0:8]
+                windows[chip * 2 + 1 - coords[3]] = blocks[number + 8][j, :, part].astype(F32)[0:8]
+        copy.start()
         entries[...] = jnp.zeros_like(entries)
-        for copy in copies:
-            copy.wait()
-
-        def place_rows(chip, carry):
-            start = pl.multiple_of(chip * 2 * rows, 16)
-            for which in range(3):
-                part = slice(which * width, (which + 1) * width)
-                pair = jnp.concatenate(
-                    [raw[2 * chip, :, part].astype(F32), raw[2 * chip + 1, :, part].astype(F32)],
-                    axis=0,
-                )
-                weights[which, pl.ds(start, 2 * rows), :] = pair.astype(BF)
-            return carry
-
-        lax.fori_loop(0, chips, place_rows, 0)
-        pltpu.make_async_copy(weights, w_out, out_sem).start()
-        for device in range(2 * chips):
+        for device in range(windows.shape[0]):
             first = 9 * (device // 4) + 2 * (device % 4)
-            window = raw[device, :, 3 * width : 3 * width + 128].astype(F32)
-            entries[first : first + 4, :] += window[0:4, :]
+            entries[first : first + 4, :] += windows[device, 0:4, :]
         vector_out[...] = jnp.zeros_like(vector_out)
         pieces = width // 128
         for row in range(12):
@@ -344,26 +360,26 @@
 
     @pl.when(pl.program_id(0) == pl.num_programs(0) - 1)
     def finish():
-        pltpu.make_async_copy(weights, w_out, out_sem).wait()
+        copy.wait()
 
 
 def project_qkv(place, frames, blocks, tile=256):
     count, width = frames.shape
-    rows, wire_width = blocks[0].shape[1:]
     low = struct((count, width), BF)
     row_tile = pl.BlockSpec((tile, width), lambda i: (i, 0))
     anywhere = pl.BlockSpec(memory_space=pl.ANY)
     return pl.pallas_call(
         partial(qkv_kernel, place.depth),
         grid=(count // tile,),
-        in_specs=[pl.BlockSpec(memory_space=pltpu.SMEM), row_tile] + [anywhere] * 16,
-        out_specs=[row_tile] * 3 + [pl.BlockSpec((16, width), lambda i: (0, 0)), anywhere],
+        in_specs=[pl.BlockSpec(memory_space=pltpu.SMEM), row_tile]
+        + [pl.BlockSpec(block.shape, lambda i: (0, 0, 0)) for block in blocks],
+        out_specs=[row_tile] * 3
+        + [pl.BlockSpec((16, width), lambda i: (0, 0)), anywhere],
         out_shape=[low, low, low, struct((16, width), F32), struct((3, width, width), BF)],
         scratch_shapes=[
-            pltpu.VMEM((place.count, rows, wire_width), BF),
             pltpu.VMEM((3, width, width), BF),
+            pltpu.VMEM((place.count, 8, 128), F32),
             pltpu.VMEM((80, 128), F32),
-            pltpu.SemaphoreType.DMA((16, place.depth // 2)),
             pltpu.SemaphoreType.DMA,
         ],
         compiler_params=params(),
@@ -372,8 +388,9 @@
     )(place.coords, frames, *blocks)
 
 
-def attention_forward_kernel(q_ref, k_ref, v_ref, q_mark, k_mark, out_ref, log_ref):
+def attention_forward_kernel(q_ref, k_ref, v_ref, q_mark, k_mark, out_ref, weights_ref):
     count = q_ref.shape[0]
+    valid = weights_ref.shape[2]
     values = v_ref[...].T
     lane = lax.broadcasted_iota(jnp.int32, (count, 128), 1)
     outs = []
@@ -386,13 +403,13 @@
         raised = jnp.exp(scores - maximum)
         total = jnp.sum(raised, axis=0, keepdims=True)
         weights = (raised * (1.0 / total)).astype(BF)
-        log_ref[0, head : head + 1, :] = maximum + jnp.log(total)
+        weights_ref[0, head] = weights[0:valid, :]
         rows = values[64 * head : 64 * head + 64, :]
         outs.append(jnp.dot(rows, weights, preferred_element_type=F32))
     out_ref[...] = jnp.concatenate(outs, axis=0).T.astype(BF)
 
 
-def attention_forward(q, k, v, q_mark, k_mark):
+def attention_forward(q, k, v, q_mark, k_mark, valid):
     count, width = q.shape
     pairs = width // 128
     column = pl.BlockSpec((count, 128), lambda i: (0, i))
@@ -401,8 +418,8 @@
         attention_forward_kernel,
         grid=(pairs,),
         in_specs=[column] * 3 + [whole] * 2,
-        out_specs=(column, pl.BlockSpec((1, 8, count), lambda i: (i, 0, 0))),
-        out_shape=(struct((count, width), BF), struct((pairs, 8, count), F32)),
+        out_specs=(column, pl.BlockSpec((1, 2, valid, count), lambda i: (i, 0, 0, 0))),
+        out_shape=(struct((count, width), BF), struct((pairs, 2, valid, count), BF)),
         compiler_params=params(),
         cost_estimate=cost(
             16 * count * count * width, 8 * count * width, 12 * count * count, times=1
@@ -412,80 +429,115 @@
 
 
 def attention_backward_kernel(
-    valid, q_ref, k_ref, v_ref, g_ref, q_mark, k_mark, log_ref, grads_ref, sum_ref, p_scr, ds_scr
+    valid, long_clip, lead_ref, q_ref, k_ref, v_ref, g_ref, weights_ref, grads_ref, sum_ref,
+    dk_scr, dv_scr,
 ):
     count = q_ref.shape[0]
-    keys_turned = k_ref[0:valid, :].T
-    lane = lax.broadcasted_iota(jnp.int32, (count, 128), 1)
-    lane_valid = lax.broadcasted_iota(jnp.int32, (valid, 128), 1)
-    turned = []
-    dk = jnp.zeros((valid, 128), F32)
-    dv = jnp.zeros((valid, 128), F32)
-    for head in (0, 1):
-        own = (lane < 64) == (head == 0)
-        scaled = q_ref[...] * BF(SCORE_SCALE)
-        keys = jnp.where((lane_valid < 64) == (head == 0), k_ref[0:valid, :], k_mark[0:valid, :])
-        queries = jnp.where(own, scaled, q_mark[...])
-        grads = jnp.where(own, g_ref[...], BF(0))
-        scores = lax.dot_general(keys, queries, NT, preferred_element_type=F32)
-        weights = jnp.exp(scores - log_ref[0, head : head + 1, :])
-        slopes = lax.dot_general(v_ref[0:valid, :], grads, NT, preferred_element_type=F32)
-        inner = jnp.sum(weights * slopes, axis=0, keepdims=True)
-        ds_scr[head] = (weights * (slopes - inner)).astype(BF)
-        p_scr[head] = weights.astype(BF)
-        turned.append(
-            jnp.dot(
-                keys_turned[64 * head : 64 * head + 64, :],
-                ds_scr[head],
-                preferred_element_type=F32,
+
+    def gradients(tiles, key_rows, query_rows):
+        lane = lax.broadcasted_iota(jnp.int32, (count, 128), 1)
+        keys_turned = k_ref[0:key_rows, :].T
+        single = len(tiles) == 1
+        if not single:
+            dk_scr[...] = jnp.zeros_like(dk_scr)
+            dv_scr[...] = jnp.zeros_like(dv_scr)
+        masked = []
+        for head in (0, 1):
+            own = (lane < 64) == (head == 0)
+            masked.append(
+                (
+                    jnp.where(own, q_ref[...] * BF(SCORE_SCALE), BF(0)),
+                    jnp.where(own, g_ref[...], BF(0)),
+                )
             )
-            * SCORE_SCALE
-        )
-        dk = dk + jnp.dot(
-            ds_scr[head], jnp.where(own, scaled, BF(0)), preferred_element_type=F32
-        )
-        dv = dv + jnp.dot(p_scr[head], grads, preferred_element_type=F32)
-    dq = jnp.concatenate(turned, axis=0).T.astype(BF)
-    grads_ref[0] = dq
-    grads_ref[1, 0:valid, :] = dk.astype(BF)
-    dv = dv.astype(BF)
-    grads_ref[2, 0:valid, :] = dv
-    if valid < count:
-        grads_ref[1, valid:count, :] = jnp.zeros((count - valid, 128), BF)
-        grads_ref[2, valid:count, :] = jnp.zeros((count - valid, 128), BF)
-    sum_ref[0:1, :] = jnp.sum(dq.astype(F32), axis=0, keepdims=True)
-    sum_ref[1:2, :] = jnp.sum(dv.astype(F32), axis=0, keepdims=True)
-    sum_ref[2:8, :] = jnp.zeros((6, 128), F32)
-
-
-def attention_backward(q, k, v, grads, q_mark, k_mark, logs, valid, first, pairs, earlier=()):
+        for queries, keys in tiles:
+            turned = []
+            dk = None
+            for head in (0, 1):
+                grads = masked[head][1][queries]
+                weights_low = weights_ref[0, head, keys, queries]
+                slopes = lax.dot_general(v_ref[keys, :], grads, NT, preferred_element_type=F32)
+                weights = weights_low.astype(F32)
+                inner = jnp.sum(weights * slopes, axis=0, keepdims=True)
+                ds = (weights * (slopes - inner)).astype(BF)
+                turned.append(
+                    jnp.dot(
+                        keys_turned[64 * head : 64 * head + 64, keys],
+                        ds,
+                        preferred_element_type=F32,
+                    )
+                    * SCORE_SCALE
+                )
+                dk_part = jnp.dot(ds, masked[head][0][queries], preferred_element_type=F32)
+                dv_part = jnp.dot(weights_low, grads, preferred_element_type=F32)
+                dk = dk_part if dk is None else dk + dk_part
+                dv = dv_part if head == 0 else dv + dv_part
+            dq = jnp.concatenate(turned, axis=0).T.astype(BF)
+            grads_ref[0, queries, :] = dq
+            sum_ref[0:1, :] += jnp.sum(dq.astype(F32), axis=0, keepdims=True)
+            if not single:
+                dk_scr[keys, :] += dk
+                dv_scr[keys, :] += dv
+        if not single:
+            dk = dk_scr[0:key_rows, :]
+            dv = dv_scr[0:key_rows, :]
+        grads_ref[1, 0:key_rows, :] = dk.astype(BF)
+        dv = dv.astype(BF)
+        grads_ref[2, 0:key_rows, :] = dv
+        sum_ref[1:2, :] += jnp.sum(dv.astype(F32), axis=0, keepdims=True)
+        rest = jnp.zeros((count - key_rows, 128), BF)
+        if key_rows < count:
+            grads_ref[1, key_rows:count, :] = rest
+            grads_ref[2, key_rows:count, :] = rest
+        if query_rows < count:
+            grads_ref[0, query_rows:count, :] = jnp.zeros((count - query_rows, 128), BF)
+
+    sum_ref[...] = jnp.zeros_like(sum_ref)
+
+    @pl.when(lead_ref[0] > 0)
+    def one_long_clip():
+        keys = -(-long_clip // 16) * 16
+        queries = -(-long_clip // 128) * 128
+        gradients([(slice(0, queries), slice(0, keys))], keys, queries)
+
+    @pl.when(lead_ref[0] == 0)
+    def short_clips():
+        tiles = []
+        for start in range(0, valid, 512):
+            first = start // SHORT * SHORT // 128 * 128
+            last = min(-(-(start + 512) // SHORT) * SHORT, valid)
+            keys = slice(first, min(-(-last // 16) * 16, valid))
+            tiles.append((slice(start, start + 512), keys))
+        gradients(tiles, valid, count)
+
+
+def attention_backward(lead, q, k, v, grads, weights, valid, first, pairs, earlier=()):
     count, width = q.shape
     column = pl.BlockSpec((count, 128), lambda i: (0, first + i))
-    whole = pl.BlockSpec((count, 128), lambda i: (0, 0))
 
     def kernel(*refs):
-        attention_backward_kernel(valid, *refs[:7], *refs[7 + len(earlier) :])
+        attention_backward_kernel(valid, LONG, *refs[:6], *refs[6 + len(earlier) :])
 
     return pl.pallas_call(
         kernel,
         grid=(pairs,),
-        in_specs=[column] * 4
-        + [whole] * 2
-        + [pl.BlockSpec((1, 8, count), lambda i: (first + i, 0, 0))]
+        in_specs=[pl.BlockSpec(memory_space=pltpu.SMEM)]
+        + [column] * 4
+        + [pl.BlockSpec((1, 2, valid, count), lambda i: (first + i, 0, 0, 0))]
         + [pl.BlockSpec(memory_space=pl.ANY)] * len(earlier),
         out_specs=(
             pl.BlockSpec((3, count, 128), lambda i: (0, 0, first + i)),
             pl.BlockSpec((8, 128), lambda i: (0, first + i)),
         ),
         out_shape=(struct((3, count, width), BF), struct((8, width), F32)),
-        scratch_shapes=[pltpu.VMEM((2, valid, count), BF)] * 2,
-        input_output_aliases={7 + i: i for i in range(len(earlier))},
+        scratch_shapes=[pltpu.VMEM((valid, 128), F32)] * 2,
+        input_output_aliases={6 + i: i for i in range(len(earlier))},
         compiler_params=params(),
         cost_estimate=cost(
-            40 * count * count * 128 * pairs, 14 * count * 128 * pairs, 2 * count * count * pairs
+            32 * count * count * 128 * pairs, 14 * count * 128 * pairs, 2 * count * count * pairs
         ),
         name="attention_backward",
-    )(q, k, v, grads, q_mark, k_mark, logs, *earlier)
+    )(lead, q, k, v, grads, weights, *earlier)
 
 
 def gelu_parts(value):
@@ -525,18 +577,17 @@
                 works.remove(work)
 
 
-def middle_kernel(packed, last_rows, chunk, total_ref, frames, context, cotangent, vector, *refs):
+def middle_kernel(packed, last_rows, total_ref, frames, context, cotangent, vector, *refs):
     weight_refs = refs[: 1 if packed else 3]
     (
         result, normed_out, activated_out, down_g_out, up_g_out, first_g_out, attended_g_out,
         context_g_out, sums, up_w, down_w, out_w, raw_up, raw_out, slopes, first_hats,
-        second_hats, inverses, sems,
+        second_hats, inverses, down_total, grad_total, sems,
     ) = refs[len(weight_refs) :]
     step = pl.program_id(0)
     tiles = pl.num_programs(0) - 1
     tile, width = frames.shape
     hidden = up_w.shape[1]
-    parts = [slice(j * chunk, (j + 1) * chunk) for j in range(hidden // chunk)]
 
     if packed:
         wire = weight_refs[0]
@@ -579,82 +630,71 @@
         position = number * tile + lax.broadcasted_iota(jnp.int32, (rows, 1), 0)
         return (position < total_ref[0]).astype(F32)
 
-    def forward():
-        slot = step % 2
-        valid = valid_rows(step, tile)
-        attended = jnp.dot(context[...], out_w[...], preferred_element_type=F32)
-        yield
-        attended = attended + vector[2:3, :]
+    def forward_start():
+        attended = jnp.dot(context[...], out_w[...], preferred_element_type=F32) + vector[2:3, :]
         first_sum = frames[...].astype(F32) + attended
         first_hat, first_inverse = normalize(first_sum)
-        normed = (first_hat * vector[4:5, :] + vector[5:6, :]).astype(BF)
-        normed_out[...] = normed
+        normed_out[...] = (first_hat * vector[4:5, :] + vector[5:6, :]).astype(BF)
         first_hats[slot] = first_hat
         inverses[slot, 0] = jnp.broadcast_to(first_inverse, (tile, 128))
+        valid = valid_rows(step, tile)
         add_sum(12, column_sums(valid * attended * attended))
         add_sum(13, column_sums(valid * first_sum * first_sum))
         add_sum(16, jnp.broadcast_to(column_sums(valid), (1, width)))
+        down_total[...] = jnp.broadcast_to(vector[3:4, :], (tile, width))
+
+    def forward_chunk(part, row):
+        pre = jnp.dot(normed_out[...], up_w[:, part], preferred_element_type=F32)
         yield
-        down_out = jnp.broadcast_to(vector[3:4, :], (tile, width))
-        pre = jnp.dot(normed, up_w[:, parts[0]], preferred_element_type=F32)
+        activated, slope = gelu_parts(pre + vector[pl.ds(row, 1), :])
+        slopes[slot, :, part] = slope
+        activated = activated.astype(BF)
+        activated_out[:, part] = activated
         yield
-        for j, part in enumerate(parts):
-            if j + 1 < len(parts):
-                later = jnp.dot(normed, up_w[:, parts[j + 1]], preferred_element_type=F32)
-            row = 8 + part.start // width
-            bias = vector[row : row + 1, part.start % width : part.start % width + chunk]
-            activated, slope = gelu_parts(pre + bias)
-            slopes[slot, :, part] = slope
-            activated = activated.astype(BF)
-            activated_out[:, part] = activated
-            yield
-            down_out = down_out + jnp.dot(activated, down_w[part, :], preferred_element_type=F32)
-            pre = later
-            yield
-        second_sum = normed.astype(F32) + down_out
+        down_total[...] += jnp.dot(activated, down_w[part, :], preferred_element_type=F32)
+
+    def forward_end():
+        down_out = down_total[...]
+        second_sum = normed_out[...].astype(F32) + down_out
         second_hat, second_inverse = normalize(second_sum)
         result[...] = (second_hat * vector[6:7, :] + vector[7:8, :]).astype(BF)
         second_hats[slot] = second_hat
         inverses[slot, 1] = jnp.broadcast_to(second_inverse, (tile, 128))
+        valid = valid_rows(step, tile)
         add_sum(14, column_sums(valid * down_out * down_out))
         add_sum(15, column_sums(valid * second_sum * second_sum))
 
-    def backward(rows):
-        slot = (step + 1) % 2
-        valid = valid_rows(step - 1, rows)
-        out_g = cotangent[0:rows, :].astype(F32) * valid
-        second_hat = second_hats[slot, 0:rows, :]
+    def backward_start(rows):
+        out_g = cotangent[0:rows, :].astype(F32) * valid_rows(step - 1, rows)
+        second_hat = second_hats[other, 0:rows, :]
         grad_second = norm_backward(
-            out_g, second_hat, inverses[slot, 1, 0:rows, 0:1], vector[6:7, :]
+            out_g, second_hat, inverses[other, 1, 0:rows, 0:1], vector[6:7, :]
         )
         add_sum(6, column_sums(out_g * second_hat))
         add_sum(7, column_sums(out_g))
         down_g = grad_second.astype(BF)
         down_g_out[0:rows, :] = down_g
         add_sum(3, column_sums(down_g.astype(F32)))
+        grad_total[0:rows, :] = grad_second
+
+    def backward_chunk(rows, part, row):
+        grad = lax.dot_general(
+            down_g_out[0:rows, :], down_w[part, :], NT, preferred_element_type=F32
+        )
         yield
-        grad_normed = grad_second
-        grad = lax.dot_general(down_g, down_w[parts[0], :], NT, preferred_element_type=F32)
+        up_g = (grad * slopes[other, 0:rows, part]).astype(BF)
+        up_g_out[0:rows, part] = up_g
+        sums[pl.ds(row, 1), :] += column_sums(up_g.astype(F32))
         yield
-        for j, part in enumerate(parts):
-            if j + 1 < len(parts):
-                later = lax.dot_general(
-                    down_g, down_w[parts[j + 1], :], NT, preferred_element_type=F32
-                )
-            up_g = (grad * slopes[slot, 0:rows, part]).astype(BF)
-            up_g_out[0:rows, part] = up_g
-            row = 8 + part.start // width
-            lanes = slice(part.start % width, part.start % width + chunk)
-            sums[row : row + 1, lanes] += column_sums(up_g.astype(F32))
-            yield
-            grad_normed = grad_normed + lax.dot_general(
-                up_g, up_w[:, part], NT, preferred_element_type=F32
-            )
-            grad = later
-            yield
-        first_hat = first_hats[slot, 0:rows, :]
+        grad_total[0:rows, :] += lax.dot_general(
+            up_g, up_w[:, part], NT, preferred_element_type=F32
+        )
+
+    def backward_end(rows):
+        grad_normed = grad_total[0:rows, :]
+        first_hat = first_hats[other, 0:rows, :]
         grad_first = norm_backward(
-            grad_normed, first_hat, inverses[slot, 0, 0:rows, 0:1], vector[4:5, :]
+            grad_normed, first_hat, inverses[other, 0, 0:rows, 0:1], vector[4:5, :]
         )
         add_sum(4, column_sums(grad_normed * first_hat))
         add_sum(5, column_sums(grad_normed))
@@ -662,10 +702,19 @@
         attended_g = grad_first.astype(BF)
         attended_g_out[0:rows, :] = attended_g
         add_sum(2, column_sums(attended_g.astype(F32)))
-        yield
         context_g_out[0:rows, :] = lax.dot_general(
             attended_g, out_w[...], NT, preferred_element_type=F32
         ).astype(BF)
+
+    def chunks(work, unroll):
+        def body(j, carry):
+            work(pl.ds(pl.multiple_of(j * width, width), width), 8 + j)
+            return carry
+
+        lax.fori_loop(0, hidden // width, body, 0, unroll=unroll)
+
+    slot = lax.rem(step, 2)
+    other = 1 - slot
 
     @pl.when(step == 0)
     def first_step():
@@ -675,25 +724,38 @@
         copies[0].wait()
         if packed:
             unpack(raw_out, out_w, 256, 3)
+        forward_start()
         copies[1].wait()
         if packed:
             unpack(raw_up, up_w, width, 4)
         copies[2].wait()
-        interleave(forward())
+        chunks(lambda part, row: interleave(forward_chunk(part, row)), 2)
+        forward_end()
 
     @pl.when((step > 0) & (step < tiles))
     def middle_step():
-        interleave(forward(), backward(tile))
+        forward_start()
+        backward_start(tile)
+        chunks(
+            lambda part, row: interleave(
+                backward_chunk(tile, part, row), forward_chunk(part, row)
+            ),
+            4,
+        )
+        forward_end()
+        backward_end(tile)
 
     @pl.when(step == tiles)
     def last_step():
-        interleave(backward(last_rows))
+        backward_start(last_rows)
+        chunks(lambda part, row: interleave(backward_chunk(last_rows, part, row)), 2)
+        backward_end(last_rows)
         if last_rows < tile:
             for ref in (down_g_out, up_g_out, first_g_out, attended_g_out, context_g_out):
                 ref[last_rows:tile, :] = jnp.zeros((tile - last_rows, ref.shape[1]), ref.dtype)
 
 
-def middle(frames, context, cotangent, vector, total, weights, hidden, valid, tile=256, chunk=768):
+def middle(frames, context, cotangent, vector, total, weights, hidden, valid, tile=256):
     count, width = frames.shape
     packed = len(weights) == 1
     tiles = count // tile
@@ -710,7 +772,7 @@
     wide = struct((count, hidden), BF)
     raw = hidden if packed else 16
     return pl.pallas_call(
-        partial(middle_kernel, packed, last_rows, chunk),
+        partial(middle_kernel, packed, last_rows),
         grid=(tiles + 1,),
         in_specs=[
             pl.BlockSpec(memory_space=pltpu.SMEM),
@@ -738,6 +800,8 @@
             pltpu.VMEM((2, tile, width), F32),
             pltpu.VMEM((2, tile, width), F32),
             pltpu.VMEM((2, 2, tile, 128), F32),
+            pltpu.VMEM((tile, width), F32),
+            pltpu.VMEM((tile, width), F32),
             pltpu.SemaphoreType.DMA((3,)),
         ],
         compiler_params=params(),
@@ -1046,14 +1110,14 @@
             for w in (out_master, up_master, down_master)
         )
 
-    context, logs = attention_forward(queries, keys, values, q_mark, k_mark)
+    context, attention = attention_forward(queries, keys, values, q_mark, k_mark, valid)
     (
         result, normed, activated, down_g, up_g, first_g, attended_g, context_g, sums,
     ) = middle(frames, context, cotangent, vector, total, weights, hidden, valid)
 
     def attention_part(first, pairs, start, earlier=()):
         return attention_backward(
-            start, keys, values, context_g, q_mark, k_mark, logs, valid, first, pairs, earlier
+            lengths[0, 0:1], start, keys, values, context_g, attention, valid, first, pairs, earlier
         )
 
     if fast:
@@ -1066,25 +1130,26 @@
         all_sums = lax.all_gather(sums, AXES, axis=0)
         most = Reduction(place)
         done = most.first(after(down_mine, up_mine), down_got)
-        grads = attention_part(0, 2, after(queries, done))
+        grads = attention_part(0, 3, after(queries, done))
         done = most.first(after(up_mine, grads[1]), up_got)
-        grads = attention_part(2, 2, after(queries, done), grads)
-        most.parts[0] = after(most.parts[0], grads[1])
+        qkv_g, bias_sums = attention_part(3, 3, after(queries, done), grads)
+        most.parts[0], all_sums = after((most.parts[0], all_sums), bias_sums)
         done = most.second()
-        qkv_g, bias_sums = attention_part(4, 2, after(queries, done), grads)
-        most.sums = after(most.sums, bias_sums)
+        mine, theirs = qkv_grad(
+            place, after(frames, (done, all_sums)), qkv_g, sums, bias_sums, valid
+        )
+        got = place.swap_core(theirs)
+        most.sums = after(most.sums, mine)
         done = most.third()
-        mine, theirs = qkv_grad(place, after(frames, done), qkv_g, sums, bias_sums, valid)
-        got = place.swap_core(theirs)
-        frames_grad = frames_gradient(after(first_g, mine), qkv_g, qkv_full)
+        last = Reduction(place)
+        done = last.first(after(mine, done), got)
+        frames_grad = frames_gradient(after(first_g, done), qkv_g, qkv_full)
         most.sums = after(most.sums, frames_grad)
-        done = most.fourth()
-        last = Reduction(place)
-        last.first(after(mine, done), got)
-        done = last.second()
-        most.sums = after(most.sums, done)
-        last.third()
-        last.fourth()
+        done = most.fourth(0)
+        last.parts[0] = after(last.parts[0], done)
+        last.second()
+        done = last.spread()
+        most.sums, all_sums = after((most.sums, all_sums), done)
         grad_most = most.result()
         grad_qkv = last.result()
         grad_down = grad_most[:, : 4 * width].reshape(rows, 4, width)

time: 322 us -> 302 us (0.938)
  Pallas kernels: 183 us -> 172 us
  waiting for transfers between devices: 69.1 us -> 59.6 us
    pallas_call x4 -> x3, Pallas kernels: 80 us -> 68.1 us  [the longest x1 38.4 us: middle(): pl.pallas_call(partial(middle_kernel, packed, last_rows), grid=(tiles + 1...]
    ppermute x8, waiting for transfers between devices: 13.6 us -> 6.06 us  [swap_x(): return lax.ppermute(value, 'dp', [(i, i ^ 1) for i in range(self.n_dp)])]
    ppermute x4 -> x2, waiting for transfers between devices: 11.4 us -> 5.37 us  [swap_z(): return lax.ppermute(value, 'fsdp', pairs)]
    ppermute x8, waiting for transfers between devices: 11.6 us -> 15.7 us  [swap_y(): return lax.ppermute(value, 'dp', [(i, i ^ 2) for i in range(self.n_dp)])]
    ppermute x3 -> x6, starting transfers between devices: 6.11 us -> 9.94 us  [shift_z(): return lax.ppermute(value, 'fsdp', pairs)]
    ppermute x3 -> x6, waiting for transfers between devices: 6.03 us -> 7.94 us  [shift_z(): return lax.ppermute(value, 'fsdp', pairs)]
    pallas_call x4 -> x3, Pallas kernels: 9.17 us -> 7.51 us  [small_add(): pl.pallas_call(kernel, in_specs=[pl.BlockSpec(memory_space=pltpu.SMEM)] +...]
  transfers between devices with their start and end apart: 36 -> 37, of which waited for: 19 -> 17; matrix products, arithmetic and copies ran while one was open for 3% -> 3% of each run, Pallas kernels for 44% -> 42%
where the time goes in v3:
time: 302 us; the launch traced here: 296 us
  Pallas kernels  172 us (57%)
  waiting for transfers between devices  59.6 us (20%)
  starting transfers between devices  33.6 us (11%)
  between operations  14.8 us (5%)
  other arithmetic  11.5 us (4%)
  local copies, waits for them, and re-layouts  5.15 us (2%)
    pallas_call x1, Pallas kernels, middle(): pl.pallas_call(partial(middle_kernel, packed, last_rows), grid=(tiles + 1...  38.4 us
    pallas_call x2, Pallas kernels, attention_backward(): pl.pallas_call(kernel, grid=(pairs,), in_specs=[pl.BlockSpec(memory_space...  29.7 us
    pallas_call x1, Pallas kernels, attention_forward(): pl.pallas_call(attention_forward_kernel, grid=(pairs,), in_specs=[column]...  25.2 us
    all_gather x1, waiting for transfers between devices, shards(): wire = lax.all_gather(wire_low, AXES, axis=0, tiled=True)  24 us
    ppermute x8, waiting for transfers between devices, swap_y(): return lax.ppermute(value, 'dp', [(i, i ^ 2) for i in range(self.n_dp)])  15.7 us
    pallas_call x3, Pallas kernels, first_add(): pl.pallas_call(first_add_kernel, grid_spec=pltpu.PrefetchScalarGridSpec(n...  13.1 us
    pallas_call x1, Pallas kernels, up_grad(): pl.pallas_call(partial(up_grad_kernel, valid, rows), grid_spec=pltpu.Pref...  11.6 us
    ppermute x8, starting transfers between devices, swap_x(): return lax.ppermute(value, 'dp', [(i, i ^ 1) for i in range(self.n_dp)])  11.5 us
  transfers between devices with their start and end apart: 37, of which 17 were waited for; matrix products, arithmetic and copies ran while one was open for 3% of the time, Pallas kernels for 42%

profile of v3, /device:TPU:0, one launch (start us, length us, event | category | flops | bytes accessed | tf_op | source)
XLA Modules:
  0.0 296.4 jit_solution(2638582724379896492)
XLA Ops:
  11.2 3.1 %collective-permute-start = (bf16[24,2432]{1,0:T(8,128)(2,1)}, bf16[24,2432]{1,0:T(8,128)(2,1)S(1)}, u32[]{:S(2)}, u32[]{:S(2)}) collective-permute-start(bf16[24,2432]{1,0:T(8,128)(2,1)} %get-tuple-element.105), channel_id=1, source_target_pairs={{0,2},{1,3},{2,4},{3,5},{4,6},{5,7},{6,0},{7,1},{8,10},{9,11},{10,... | collective-permute-start | bytes 350216 | tf_op jit(solution)/shard_map/ppermute | solution.py:75
  17.3 3.2 %collective-permute-done = bf16[24,2432]{1,0:T(8,128)(2,1)S(1)} collective-permute-done((bf16[24,2432]{1,0:T(8,128)(2,1)}, bf16[24,2432]{1,0:T(8,128)(2,1)S(1)}, u32[]{:S(2)}, u32[]{:S(2)}) %collective-permute-start) | collective-permute-done | bytes 116768 | tf_op jit(solution)/shard_map/ppermute | solution.py:75
  24.8 2.8 collective-permute-done.4
  34.5 3.1 %collective-permute-done.7.refs_6_ = bf16[2,24,2432]{2,1,0:T(8,128)(2,1)S(1)} collective-permute-done((bf16[2,24,2432]{2,1,0:T(8,128)(2,1)S(1)}, bf16[2,24,2432]{2,1,0:T(8,128)(2,1)S(1)}, u32[]{:S(2)}, u32[]{:S(2)}) %collective-permute-start.7) | collective-permute-done | bytes 233504 | tf_op jit(solution)/shard_map/ppermute | solution.py:67
  47.2 8.8 %project_qkv.1 = (bf16[1024,768]{1,0:T(8,128)(2,1)}, bf16[1024,768]{1,0:T(8,128)(2,1)}, bf16[1024,768]{1,0:T(8,128)(2,1)}, f32[16,768]{1,0:T(8,128)}, bf16[3,768,768]{2,1,0:T(8,128)(2,1)}) custom-call(s32[5]{0:T(128)} %stack.41.coords, bf16[1024,768]{1,0:T(8,128)(2,1)} %left, bf16[2,24,2432]{2,1,0:T(8,128)(2,1)} %copy-done.9, ...), custom_call_target="tpu_custom_call" | custom-call | flops 3623878656 | bytes 7864320 | tf_op jit(solution)/shard_map/project_qkv/pallas_call | solution.py:371
  56.0 25.2 %attention_forward.1 = (bf16[1024,768]{1,0:T(8,128)(2,1)}, bf16[6,2,912,1024]{3,2,1,0:T(8,128)(2,1)}) custom-call(bf16[1024,768]{1,0:T(8,128)(2,1)} %get-tuple-element.136.q_ref.refs_1_, bf16[1024,768]{1,0:T(8,128)(2,1)} %get-tuple-element.107.k_ref.refs_2_, bf16[1024,768]{1,0:T(8,128)(2,1)} %get-tuple-element.108.v_ref.refs_3_, ...), custom_call_target="tpu_custom_call" | custom-call | flops 12884901888 | bytes 6291456 | tf_op jit(solution)/shard_map/attention_forward/pallas_call | solution.py:417
  81.2 24.0 %all-gather.4.cloned.1.call-done.refs_0_ = bf16[3072,1792]{1,0:T(8,128)(2,1)} async-done(((bf16[96,1792]{1,0:T(8,128)(2,1)}), bf16[3072,1792]{1,0:T(8,128)(2,1)}) %all-gather.4.cloned.1.call-update) | async-done | bytes 11010064 | tf_op jit(solution)/shard_map/all_gather | solution.py:1097
  105.2 38.4 %feed_forward.1 = (bf16[1024,768]{1,0:T(8,128)(2,1)}, bf16[1024,768]{1,0:T(8,128)(2,1)}, bf16[1024,3072]{1,0:T(8,128)(2,1)}, bf16[1024,768]{1,0:T(8,128)(2,1)}, ...) custom-call(s32[1]{0:T(128)} %bitcast.1.total_ref, ...), custom_call_target="tpu_custom_call" | custom-call | flops 21743271936000 | bytes 33030144000 | tf_op jit(solution)/shard_map/feed_forward/pallas_call | solution.py:774
  143.6 10.1 %grad_down.1 = (bf16[16,24,3072]{2,1,0:T(8,128)(2,1)}, bf16[16,24,3072]{2,1,0:T(8,128)(2,1)}) custom-call(s32[5]{0:T(128)} %stack.41.coords, bf16[1024,3072]{1,0:T(8,128)(2,1)} %get-tuple-element.114.left, bf16[1024,768]{1,0:T(8,128)(2,1)} %get-tuple-element.115.right), custom_call_target="tpu_custom_call" | custom-call | flops 4831838208000 | bytes 7864320000 | tf_op jit(solution)/shard_map/grad_down/pallas_call | solution.py:848
  154.0 11.6 %grad_up_and_out.1 = (bf16[16,24,3840]{2,1,0:T(8,128)(2,1)}, bf16[16,24,3840]{2,1,0:T(8,128)(2,1)}) custom-call(s32[5]{0:T(128)} %stack.41.coords, bf16[1024,768]{1,0:T(8,128)(2,1)} %get-tuple-element.118.left, bf16[1024,3072]{1,0:T(8,128)(2,1)} %get-tuple-element.119.right, bf16[1024,768]{1,0:T(8,128)(2,1)} %get-tuple-element.109.context.out_left, ...), custom_call_target="tpu_custom_call" | custom-call | flops 6039797760000 | bytes 16515072000 | tf_op jit(solution)/shard_map/grad_up_and_out/pallas_call | solution.py:905
  165.9 4.3 %reduce_over_core.3 = (bf16[2,2,24,3072]{3,2,1,0:T(8,128)(2,1)}, bf16[2,2,24,3072]{3,2,1,0:T(8,128)(2,1)}, bf16[2,2,24,3072]{3,2,1,0:T(8,128)(2,1)}, bf16[2,2,24,3072]{3,2,1,0:T(8,128)(2,1)}) custom-call(s32[5]{0:T(128)} %stack.41.coords, bf16[2,2,4,24,3072]{4,3,2,1,0:T(8,128)(2,1)} %bitcast.68, ...), custom_call_target="tpu_custom_call" | custom-call | flops 1179648000000 | bytes 7077888000000 | tf_op jit(solution)/shard_map/reduce_over_core/pallas_call | solution.py:129
  172.4 14.6 %attention_backward.2 = (bf16[3,1024,768]{2,1,0:T(8,128)(2,1)}, f32[8,768]{1,0:T(8,128)}) custom-call(s32[1]{0:T(128)} %bitcast.62, bf16[1024,768]{1,0:T(8,128)(2,1)} %get-tuple-element.136.q_ref.refs_1_, bf16[1024,768]{1,0:T(8,128)(2,1)} %get-tuple-element.107.k_ref.refs_2_, bf16[1024,768]{1,0:T(8,128)(2,1)} %get-tuple-element.108.v_ref.refs_3_, ...), custom_call_target="tpu_custom_call" | custom-call | flops 12884901888000 | bytes 5505024000 | tf_op jit(solution)/shard_map/attention_backward/pallas_call | solution.py:521
  187.0 4.8 %reduce_over_core.4 = (bf16[2,2,24,3840]{3,2,1,0:T(8,128)(2,1)}, bf16[2,2,24,3840]{3,2,1,0:T(8,128)(2,1)}, bf16[2,2,24,3840]{3,2,1,0:T(8,128)(2,1)}, bf16[2,2,24,3840]{3,2,1,0:T(8,128)(2,1)}) custom-call(s32[5]{0:T(128)} %stack.41.coords, bf16[2,2,4,24,3840]{4,3,2,1,0:T(8,128)(2,1)} %bitcast.64, ...), custom_call_target="tpu_custom_call" | custom-call | flops 1474560000000 | bytes 8847360000000 | tf_op jit(solution)/shard_map/reduce_over_core/pallas_call | solution.py:129
  193.9 15.1 %attention_backward.3 = (bf16[3,1024,768]{2,1,0:T(8,128)(2,1)}, f32[8,768]{1,0:T(8,128)}) custom-call(s32[1]{0:T(128)} %bitcast.63, bf16[1024,768]{1,0:T(8,128)(2,1)} %get-tuple-element.136.q_ref.refs_1_, bf16[1024,768]{1,0:T(8,128)(2,1)} %get-tuple-element.107.k_ref.refs_2_, ...), custom_call_target="tpu_custom_call", output_to_operand_aliasing={{0}: (6, {}), {1}: (7, {})} | custom-call | flops 12884901888000 | bytes 5505024000 | tf_op jit(solution)/shard_map/attention_backward/pallas_call | solution.py:521
  211.6 4.9 %reduce_over_first_link.2 = (bf16[2,24,6912]{2,1,0:T(8,128)(2,1)}, bf16[2,24,6912]{2,1,0:T(8,128)(2,1)}, bf16[2,24,6912]{2,1,0:T(8,128)(2,1)}, bf16[2,24,6912]{2,1,0:T(8,128)(2,1)}) custom-call(s32[5]{0:T(128)} %stack.41.coords, bf16[2,2,24,3072]{3,2,1,0:T(8,128)(2,1)} %get-tuple-element.139.refs_0_.refs_2_, ...), custom_call_target="tpu_custom_call" | custom-call | flops 1327104000000 | bytes 7962624000000 | tf_op jit(solution)/shard_map/reduce_over_first_link/pallas_call | solution.py:170
  218.4 8.5 %grad_qkv.1 = (bf16[16,24,2432]{2,1,0:T(8,128)(2,1)}, bf16[16,24,2432]{2,1,0:T(8,128)(2,1)}) custom-call(s32[5]{0:T(128)} %stack.41.coords, bf16[1024,768]{1,0:T(8,128)(2,1)} %left, bf16[3,1024,768]{2,1,0:T(8,128)(2,1)} %get-tuple-element.149.right.grads, f32[24,768]{1,0:T(8,128)} %get-tuple-element.128.sums, f32[8,768]{1,0:T(8,128)} %get-tuple-element.138.more), custom_call_target="tpu_custom_call" | custom-call | flops 3623878656000 | bytes 11010048000 | tf_op jit(solution)/shard_map/grad_qkv/pallas_call | solution.py:993
  227.0 5.1 %collective-permute-done.23.got_a = bf16[2,24,6912]{2,1,0:T(8,128)(2,1)} collective-permute-done((bf16[2,24,6912]{2,1,0:T(8,128)(2,1)}, bf16[2,24,6912]{2,1,0:T(8,128)(2,1)}, u32[]{:S(2)}, u32[]{:S(2)}) %collective-permute-start.23) | collective-permute-done | bytes 663584 | tf_op jit(solution)/shard_map/ppermute | solution.py:67
  232.3 3.0 %reduce_over_second_link.2 = (bf16[2,24,6912]{2,1,0:T(8,128)(2,1)}, bf16[2,24,6912]{2,1,0:T(8,128)(2,1)}) custom-call(s32[5]{0:T(128)} %stack.41.coords, bf16[2,24,6912]{2,1,0:T(8,128)(2,1)} %get-tuple-element.154.keep_a, bf16[2,24,6912]{2,1,0:T(8,128)(2,1)} %collective-permute-done.23.got_a, bf16[2,24,6912]{2,1,0:T(8,128)(2,1)} %get-tuple-element.156.keep_b, ...), custom_call_target="tpu_custom_call" | custom-call | flops 663552000000 | bytes 1990656000000 | tf_op jit(solution)/shard_map/reduce_over_second_link/pallas_call | solution.py:212
  237.8 3.9 %reduce_over_core.5 = (bf16[2,2,24,2432]{3,2,1,0:T(8,128)(2,1)}, bf16[2,2,24,2432]{3,2,1,0:T(8,128)(2,1)}, bf16[2,2,24,2432]{3,2,1,0:T(8,128)(2,1)}, bf16[2,2,24,2432]{3,2,1,0:T(8,128)(2,1)}) custom-call(s32[5]{0:T(128)} %stack.41.coords, bf16[2,2,4,24,2432]{4,3,2,1,0:T(8,128)(2,1)} %bitcast.72, ...), custom_call_target="tpu_custom_call" | custom-call | flops 933888000000 | bytes 5603328000000 | tf_op jit(solution)/shard_map/reduce_over_core/pallas_call | solution.py:129
  243.7 8.7 %frames_gradient.1 = bf16[1024,768]{1,0:T(8,128)(2,1)} custom-call(f32[1024,768]{1,0:T(8,128)} %get-tuple-element.162.first_g, bf16[3,1024,768]{2,1,0:T(8,128)(2,1)} %get-tuple-element.149.right.grads, bf16[3,768,768]{2,1,0:T(8,128)(2,1)} %get-tuple-element.163.weights), custom_call_target="tpu_custom_call" | custom-call | flops 3623878656000 | bytes 12976128000 | tf_op jit(solution)/shard_map/frames_gradient/pallas_call | solution.py:1031
  254.6 3.2 %reduce_over_first_link.3 = (bf16[2,24,2432]{2,1,0:T(8,128)(2,1)}, bf16[2,24,2432]{2,1,0:T(8,128)(2,1)}, bf16[2,24,2432]{2,1,0:T(8,128)(2,1)}, bf16[2,24,2432]{2,1,0:T(8,128)(2,1)}) custom-call(s32[5]{0:T(128)} %stack.41.coords, bf16[2,2,24,2432]{3,2,1,0:T(8,128)(2,1)} %get-tuple-element.172.refs_0_.refs_2_, ...), custom_call_target="tpu_custom_call" | custom-call | flops 466944000000 | bytes 2801664000000 | tf_op jit(solution)/shard_map/reduce_over_first_link/pallas_call | solution.py:170
  260.0 4.2 %collective-permute-done.30.got_a = bf16[2,24,2432]{2,1,0:T(8,128)(2,1)S(1)} collective-permute-done((bf16[2,24,2432]{2,1,0:T(8,128)(2,1)}, bf16[2,24,2432]{2,1,0:T(8,128)(2,1)S(1)}, u32[]{:S(2)}, u32[]{:S(2)}) %collective-permute-start.30) | collective-permute-done | bytes 233504 | tf_op jit(solution)/shard_map/ppermute | solution.py:67
  268.6 5.4 %collective-permute-done.27 = bf16[24,6912]{1,0:T(8,128)(2,1)} collective-permute-done((bf16[24,6912]{1,0:T(8,128)(2,1)}, bf16[24,6912]{1,0:T(8,128)(2,1)}, u32[]{:S(2)}, u32[]{:S(2)}) %collective-permute-start.27) | collective-permute-done | bytes 331808 | tf_op jit(solution)/shard_map/ppermute | solution.py:79
  277.6 2.5 collective-permute-start.34
  (164 shorter events, 63.0 us)
Async XLA Ops:
  7.2 98.0 %all-gather.4.cloned.1.call-start = ((), (), s32[]{:S(2)}) async-start(), calls=%async_computation | async-start | bytes 11354112 | tf_op jit(solution)/shard_map/all_gather | solution.py:1097
  11.2 197.9 %all-gather.6.cloned.1.call-start = ((), (), s32[]{:S(2)}) async-start(), calls=%async_computation.1 | async-start | bytes 2433024 | tf_op jit(solution)/shard_map/all_gather | solution.py:1130
  14.3 10.6 %collective-permute-start.5 = (bf16[24,2432]{1,0:T(8,128)(2,1)}, bf16[24,2432]{1,0:T(8,128)(2,1)S(1)}, u32[]{:S(2)}, u32[]{:S(2)}) collective-permute-start(bf16[24,2432]{1,0:T(8,128)(2,1)} %get-tuple-element.105), channel_id=1, source_target_pairs={{0,6},{1,7},{2,0},{3,1},{4,2},{5,3},{6,4},{7,5},{8,14},{9,15},{10,... | collective-permute-start | bytes 350216 | tf_op jit(solution)/shard_map/ppermute | solution.py:75
  16.4 11.3 %collective-permute-start.4 = (bf16[24,2432]{1,0:T(8,128)(2,1)}, bf16[24,2432]{1,0:T(8,128)(2,1)S(1)}, u32[]{:S(2)}, u32[]{:S(2)}) collective-permute-start(bf16[24,2432]{1,0:T(8,128)(2,1)} %get-tuple-element.105), channel_id=1, source_target_pairs={{0,4},{1,5},{2,6},{3,7},{4,0},{5,1},{6,2},{7,3},{8,12},{9,13},{10,... | collective-permute-start | bytes 350216 | tf_op jit(solution)/shard_map/ppermute | solution.py:75
  21.6 11.0 %collective-permute-start.2 = (bf16[2,24,2432]{2,1,0:T(8,128)(2,1)S(1)}, bf16[2,24,2432]{2,1,0:T(8,128)(2,1)S(1)}, u32[]{:S(2)}, u32[]{:S(2)}) collective-permute-start(bf16[2,24,2432]{2,1,0:T(8,128)(2,1)S(1)} %pad_maximum_fusion.refs_0_), channel_id=1, source_target_pairs={{0,16},{8,24},{16,0},{24,8},{1,17},{9,25},{17,1},{25,9},{2,18},{10... | collective-permute-start | bytes 700424 | tf_op jit(solution)/shard_map/ppermute | solution.py:67
  23.3 10.0 %collective-permute-start.1 = (bf16[2,24,2432]{2,1,0:T(8,128)(2,1)S(1)}, bf16[2,24,2432]{2,1,0:T(8,128)(2,1)S(1)}, u32[]{:S(2)}, u32[]{:S(2)}) collective-permute-start(bf16[2,24,2432]{2,1,0:T(8,128)(2,1)S(1)} %pad_maximum_fusion.refs_0_), channel_id=1, source_target_pairs={{0,8},{8,0},{16,24},{24,16},{1,9},{9,1},{17,25},{25,17},{2,10},{10... | collective-permute-start | bytes 700424 | tf_op jit(solution)/shard_map/ppermute | solution.py:64
  27.7 9.9 %collective-permute-start.7 = (bf16[2,24,2432]{2,1,0:T(8,128)(2,1)S(1)}, bf16[2,24,2432]{2,1,0:T(8,128)(2,1)S(1)}, u32[]{:S(2)}, u32[]{:S(2)}) collective-permute-start(bf16[2,24,2432]{2,1,0:T(8,128)(2,1)S(1)} %pad_maximum_fusion.1.refs_4_), channel_id=1, source_target_pairs={{0,16},{8,24},{16,0},{24,8},{1,17},{9,25},{17,1},{25,9},{2,18},{10... | collective-permute-start | bytes 700424 | tf_op jit(solution)/shard_map/ppermute | solution.py:67
  29.4 11.4 %collective-permute-start.13 = (bf16[2,24,2432]{2,1,0:T(8,128)(2,1)S(1)}, bf16[2,24,2432]{2,1,0:T(8,128)(2,1)S(1)}, u32[]{:S(2)}, u32[]{:S(2)}) collective-permute-start(bf16[2,24,2432]{2,1,0:T(8,128)(2,1)S(1)} %pad_maximum_fusion.1.refs_4_), channel_id=1, source_target_pairs={{0,1},{1,0},{2,3},{3,2},{4,5},{5,4},{6,7},{7,6},{8,9},{9,8},{10,11... | collective-permute-start | bytes 700424 | tf_op jit(solution)/shard_map/ppermute | solution.py:70
  29.4 11.4 %collective-permute-start.6 = (bf16[2,24,2432]{2,1,0:T(8,128)(2,1)S(1)}, bf16[2,24,2432]{2,1,0:T(8,128)(2,1)S(1)}, u32[]{:S(2)}, u32[]{:S(2)}) collective-permute-start(bf16[2,24,2432]{2,1,0:T(8,128)(2,1)S(1)} %pad_maximum_fusion.1.refs_4_), channel_id=1, source_target_pairs={{0,8},{8,0},{16,24},{24,16},{1,9},{9,1},{17,25},{25,17},{2,10},{10... | collective-permute-start | bytes 700424 | tf_op jit(solution)/shard_map/ppermute | solution.py:64
  153.8 12.2 %collective-permute-start.17 = (bf16[16,24,3072]{2,1,0:T(8,128)(2,1)}, bf16[16,24,3072]{2,1,0:T(8,128)(2,1)}, u32[]{:S(2)}, u32[]{:S(2)}) collective-permute-start(bf16[16,24,3072]{2,1,0:T(8,128)(2,1)} %get-tuple-element.123), channel_id=1, source_target_pairs={{0,1},{1,0},{2,3},{3,2},{4,5},{5,4},{6,7},{7,6},{8,9},{9,8},{10,11... | collective-permute-start | bytes 7077896 | tf_op jit(solution)/shard_map/ppermute | solution.py:70
  165.6 21.4 %collective-permute-start.20 = (bf16[16,24,3840]{2,1,0:T(8,128)(2,1)}, bf16[16,24,3840]{2,1,0:T(8,128)(2,1)}, u32[]{:S(2)}, u32[]{:S(2)}) collective-permute-start(bf16[16,24,3840]{2,1,0:T(8,128)(2,1)} %get-tuple-element.134), channel_id=1, source_target_pairs={{0,1},{1,0},{2,3},{3,2},{4,5},{5,4},{6,7},{7,6},{8,9},{9,8},{10,11... | collective-permute-start | bytes 8847368 | tf_op jit(solution)/shard_map/ppermute | solution.py:70
  170.3 38.7 %collective-permute-start.18 = (bf16[2,2,24,3072]{3,2,1,0:T(8,128)(2,1)}, bf16[2,2,24,3072]{3,2,1,0:T(8,128)(2,1)}, u32[]{:S(2)}, u32[]{:S(2)}) collective-permute-start(bf16[2,2,24,3072]{3,2,1,0:T(8,128)(2,1)} %get-tuple-element.125), channel_id=1, source_target_pairs={{0,8},{8,0},{16,24},{24,16},{1,9},{9,1},{17,25},{25,17},{2,10},{10... | collective-permute-start | bytes 1769480 | tf_op jit(solution)/shard_map/ppermute | solution.py:64
  171.8 37.2 %collective-permute-start.19 = (bf16[2,2,24,3072]{3,2,1,0:T(8,128)(2,1)}, bf16[2,2,24,3072]{3,2,1,0:T(8,128)(2,1)}, u32[]{:S(2)}, u32[]{:S(2)}) collective-permute-start(bf16[2,2,24,3072]{3,2,1,0:T(8,128)(2,1)} %get-tuple-element.127), channel_id=1, source_target_pairs={{0,16},{8,24},{16,0},{24,8},{1,17},{9,25},{17,1},{25,9},{2,18},{10... | collective-permute-start | bytes 1769480 | tf_op jit(solution)/shard_map/ppermute | solution.py:67
  191.9 18.5 %collective-permute-start.21 = (bf16[2,2,24,3840]{3,2,1,0:T(8,128)(2,1)}, bf16[2,2,24,3840]{3,2,1,0:T(8,128)(2,1)}, u32[]{:S(2)}, u32[]{:S(2)}) collective-permute-start(bf16[2,2,24,3840]{3,2,1,0:T(8,128)(2,1)} %get-tuple-element.143), channel_id=1, source_target_pairs={{0,8},{8,0},{16,24},{24,16},{1,9},{9,1},{17,25},{25,17},{2,10},{10... | collective-permute-start | bytes 2211848 | tf_op jit(solution)/shard_map/ppermute | solution.py:64
  193.4 18.2 %collective-permute-start.22 = (bf16[2,2,24,3840]{3,2,1,0:T(8,128)(2,1)}, bf16[2,2,24,3840]{3,2,1,0:T(8,128)(2,1)}, u32[]{:S(2)}, u32[]{:S(2)}) collective-permute-start(bf16[2,2,24,3840]{3,2,1,0:T(8,128)(2,1)} %get-tuple-element.145), channel_id=1, source_target_pairs={{0,16},{8,24},{16,0},{24,8},{1,17},{9,25},{17,1},{25,9},{2,18},{10... | collective-permute-start | bytes 2211848 | tf_op jit(solution)/shard_map/ppermute | solution.py:67
  216.4 15.7 %collective-permute-start.23 = (bf16[2,24,6912]{2,1,0:T(8,128)(2,1)}, bf16[2,24,6912]{2,1,0:T(8,128)(2,1)}, u32[]{:S(2)}, u32[]{:S(2)}) collective-permute-start(bf16[2,24,6912]{2,1,0:T(8,128)(2,1)} %get-tuple-element.151), channel_id=1, source_target_pairs={{0,16},{8,24},{16,0},{24,8},{1,17},{9,25},{17,1},{25,9},{2,18},{10... | collective-permute-start | bytes 1990664 | tf_op jit(solution)/shard_map/ppermute | solution.py:67
  216.9 15.4 %collective-permute-start.24 = (bf16[2,24,6912]{2,1,0:T(8,128)(2,1)}, bf16[2,24,6912]{2,1,0:T(8,128)(2,1)}, u32[]{:S(2)}, u32[]{:S(2)}) collective-permute-start(bf16[2,24,6912]{2,1,0:T(8,128)(2,1)} %get-tuple-element.153), channel_id=1, source_target_pairs={{0,8},{8,0},{16,24},{24,16},{1,9},{9,1},{17,25},{25,17},{2,10},{10... | collective-permute-start | bytes 1990664 | tf_op jit(solution)/shard_map/ppermute | solution.py:64
  226.9 10.9 %collective-permute-start.25 = (bf16[16,24,2432]{2,1,0:T(8,128)(2,1)}, bf16[16,24,2432]{2,1,0:T(8,128)(2,1)}, u32[]{:S(2)}, u32[]{:S(2)}) collective-permute-start(bf16[16,24,2432]{2,1,0:T(8,128)(2,1)} %get-tuple-element.160), channel_id=1, source_target_pairs={{0,1},{1,0},{2,3},{3,2},{4,5},{5,4},{6,7},{7,6},{8,9},{9,8},{10,11... | collective-permute-start | bytes 5603336 | tf_op jit(solution)/shard_map/ppermute | solution.py:70
  235.3 17.1 %collective-permute-start.26 = (bf16[2,24,6912]{2,1,0:T(8,128)(2,1)}, bf16[2,24,6912]{2,1,0:T(8,128)(2,1)}, u32[]{:S(2)}, u32[]{:S(2)}) collective-permute-start(bf16[2,24,6912]{2,1,0:T(8,128)(2,1)} %get-tuple-element.164), channel_id=1, source_target_pairs={{0,2},{1,3},{2,0},{3,1},{4,6},{5,7},{6,4},{7,5},{8,10},{9,11},{10,... | collective-permute-start | bytes 1990664 | tf_op jit(solution)/shard_map/ppermute | solution.py:79
  241.7 12.9 %collective-permute-start.28 = (bf16[2,2,24,2432]{3,2,1,0:T(8,128)(2,1)}, bf16[2,2,24,2432]{3,2,1,0:T(8,128)(2,1)}, u32[]{:S(2)}, u32[]{:S(2)}) collective-permute-start(bf16[2,2,24,2432]{3,2,1,0:T(8,128)(2,1)} %get-tuple-element.169), channel_id=1, source_target_pairs={{0,8},{8,0},{16,24},{24,16},{1,9},{9,1},{17,25},{25,17},{2,10},{10... | collective-permute-start | bytes 1400840 | tf_op jit(solution)/shard_map/ppermute | solution.py:64
  243.1 11.5 %collective-permute-start.29 = (bf16[2,2,24,2432]{3,2,1,0:T(8,128)(2,1)}, bf16[2,2,24,2432]{3,2,1,0:T(8,128)(2,1)}, u32[]{:S(2)}, u32[]{:S(2)}) collective-permute-start(bf16[2,2,24,2432]{3,2,1,0:T(8,128)(2,1)} %get-tuple-element.171), channel_id=1, source_target_pairs={{0,16},{8,24},{16,0},{24,8},{1,17},{9,25},{17,1},{25,9},{2,18},{10... | collective-permute-start | bytes 1400840 | tf_op jit(solution)/shard_map/ppermute | solution.py:67
  260.0 13.9 %collective-permute-start.27 = (bf16[24,6912]{1,0:T(8,128)(2,1)}, bf16[24,6912]{1,0:T(8,128)(2,1)}, u32[]{:S(2)}, u32[]{:S(2)}) collective-permute-start(bf16[24,6912]{1,0:T(8,128)(2,1)} %get-tuple-element.168), channel_id=1, source_target_pairs={{0,4},{1,5},{2,6},{3,7},{4,0},{5,1},{6,2},{7,3},{8,12},{9,13},{10,... | collective-permute-start | bytes 995336 | tf_op jit(solution)/shard_map/ppermute | solution.py:79
  276.3 11.3 %collective-permute-start.33 = (bf16[24,2432]{1,0:T(8,128)(2,1)}, bf16[24,2432]{1,0:T(8,128)(2,1)S(1)}, u32[]{:S(2)}, u32[]{:S(2)}) collective-permute-start(bf16[24,2432]{1,0:T(8,128)(2,1)} %get-tuple-element.183), channel_id=1, source_target_pairs={{0,4},{1,5},{2,6},{3,7},{4,0},{5,1},{6,2},{7,3},{8,12},{9,13},{10,... | collective-permute-start | bytes 350216 | tf_op jit(solution)/shard_map/ppermute | solution.py:75
  277.6 10.0 %collective-permute-start.34 = (bf16[24,2432]{1,0:T(8,128)(2,1)}, bf16[24,2432]{1,0:T(8,128)(2,1)S(1)}, u32[]{:S(2)}, u32[]{:S(2)}) collective-permute-start(bf16[24,2432]{1,0:T(8,128)(2,1)} %get-tuple-element.184), channel_id=1, source_target_pairs={{0,6},{1,7},{2,0},{3,1},{4,2},{5,3},{6,4},{7,5},{8,14},{9,15},{10,... | collective-permute-start | bytes 350216 | tf_op jit(solution)/shard_map/ppermute | solution.py:75
  (48 other events, 325.2 us)
Sparse Core Ops, SparseCore 0:
  11.6 93.5 all-gather.3
  143.8 55.9 all-gather.5

commit v4 on v3

--- a/solution.py
+++ b/solution.py
@@ -153,7 +153,7 @@
         start += width
 
 
-def second_add(place, parts):
+def second_add(place, parts, times):
     half, rows = parts[0][0].shape[1:3]
     widths = [part[0].shape[3] for part in parts]
     specs = []
@@ -178,7 +178,7 @@
         out_shape=[struct(shape, BF)] * 4,
         compiler_params=params(),
         cost_estimate=cost(
-            4 * half * rows * shape[2], 24 * half * rows * shape[2], times=10**6
+            4 * half * rows * shape[2], 24 * half * rows * shape[2], times=times
         ),
         name="reduce_over_first_link",
     )(place.coords, *ins)
@@ -231,9 +231,9 @@
         self.parts.append((keep_a, place.swap_x(send_a), keep_b, place.swap_y(send_b)))
         return keep_a
 
-    def second(self):
+    def second(self, times=10**6):
         place = self.place
-        keep_a, send_a, keep_b, send_b = second_add(place, self.parts)
+        keep_a, send_a, keep_b, send_b = second_add(place, self.parts, times)
         self.sums = (keep_a, place.swap_y(send_a), keep_b, place.swap_x(send_b))
         return keep_a
 
@@ -253,11 +253,11 @@
         self.sums = (keep, place.swap_z(send, 2))
         return keep
 
-    def spread(self):
+    def spread(self, times=10**6):
         place = self.place
         blocks = small_add(
             place, spread_add_kernel, self.sums, self.sums[0].shape[1:],
-            "reduce_over_second_link", outs=place.depth,
+            "reduce_over_second_link", times, outs=place.depth,
         )
         self.sums = (blocks[0],) + tuple(
             place.shift_z(blocks[step], step) for step in range(1, place.depth)
@@ -1130,9 +1130,9 @@
         all_sums = lax.all_gather(sums, AXES, axis=0)
         most = Reduction(place)
         done = most.first(after(down_mine, up_mine), down_got)
-        grads = attention_part(0, 3, after(queries, done))
+        grads = attention_part(0, 2, after(queries, done))
         done = most.first(after(up_mine, grads[1]), up_got)
-        qkv_g, bias_sums = attention_part(3, 3, after(queries, done), grads)
+        qkv_g, bias_sums = attention_part(2, 4, after(queries, done), grads)
         most.parts[0], all_sums = after((most.parts[0], all_sums), bias_sums)
         done = most.second()
         mine, theirs = qkv_grad(
@@ -1147,8 +1147,8 @@
         most.sums = after(most.sums, frames_grad)
         done = most.fourth(0)
         last.parts[0] = after(last.parts[0], done)
-        last.second()
-        done = last.spread()
+        last.second(1000)
+        done = last.spread(1000)
         most.sums, all_sums = after((most.sums, all_sums), done)
         grad_most = most.result()
         grad_qkv = last.result()

time: 302 us -> 301 us (level)
  waiting for transfers between devices: 59.6 us -> 64 us
  starting transfers between devices: 33.6 us -> 29.6 us
  transfers between devices with their start and end apart: 37 -> 37, of which waited for: 17 -> 16; matrix products, arithmetic and copies ran while one was open for 3% -> 3% of each run, Pallas kernels for 42% -> 43%
where the time goes in v4:
time: 301 us; the launch traced here: 296 us
  Pallas kernels  172 us (57%)
  waiting for transfers between devices  64 us (21%)
  starting transfers between devices  29.6 us (10%)
  between operations  14.8 us (5%)
  other arithmetic  10.5 us (3%)
  local copies, waits for them, and re-layouts  5.15 us (2%)
    pallas_call x1, Pallas kernels, middle(): pl.pallas_call(partial(middle_kernel, packed, last_rows), grid=(tiles + 1...  38.4 us
    pallas_call x2, Pallas kernels, attention_backward(): pl.pallas_call(kernel, grid=(pairs,), in_specs=[pl.BlockSpec(memory_space...  29.7 us
    pallas_call x1, Pallas kernels, attention_forward(): pl.pallas_call(attention_forward_kernel, grid=(pairs,), in_specs=[column]...  25.2 us
    all_gather x1, waiting for transfers between devices, shards(): wire = lax.all_gather(wire_low, AXES, axis=0, tiled=True)  24 us
    ppermute x8, waiting for transfers between devices, swap_y(): return lax.ppermute(value, 'dp', [(i, i ^ 2) for i in range(self.n_dp)])  18.6 us
    pallas_call x3, Pallas kernels, first_add(): pl.pallas_call(first_add_kernel, grid_spec=pltpu.PrefetchScalarGridSpec(n...  13.1 us
    pallas_call x1, Pallas kernels, up_grad(): pl.pallas_call(partial(up_grad_kernel, valid, rows), grid_spec=pltpu.Pref...  11.6 us
    pallas_call x1, Pallas kernels, down_grad(): pl.pallas_call(partial(down_grad_kernel, valid, rows), grid_spec=pltpu.Pr...  10.1 us
  transfers between devices with their start and end apart: 37, of which 16 were waited for; matrix products, arithmetic and copies ran while one was open for 3% of the time, Pallas kernels for 43%

profile of v4, /device:TPU:0, one launch (start us, length us, event | category | flops | bytes accessed | tf_op | source)
XLA Modules:
  0.0 295.9 jit_solution(2143242832587334315)
XLA Ops:
  11.2 3.1 %collective-permute-start = (bf16[24,2432]{1,0:T(8,128)(2,1)}, bf16[24,2432]{1,0:T(8,128)(2,1)S(1)}, u32[]{:S(2)}, u32[]{:S(2)}) collective-permute-start(bf16[24,2432]{1,0:T(8,128)(2,1)} %get-tuple-element.105), channel_id=1, source_target_pairs={{0,2},{1,3},{2,4},{3,5},{4,6},{5,7},{6,0},{7,1},{8,10},{9,11},{10,... | collective-permute-start | bytes 350216 | tf_op jit(solution)/shard_map/ppermute | solution.py:75
  17.3 3.2 %collective-permute-done = bf16[24,2432]{1,0:T(8,128)(2,1)S(1)} collective-permute-done((bf16[24,2432]{1,0:T(8,128)(2,1)}, bf16[24,2432]{1,0:T(8,128)(2,1)S(1)}, u32[]{:S(2)}, u32[]{:S(2)}) %collective-permute-start) | collective-permute-done | bytes 116768 | tf_op jit(solution)/shard_map/ppermute | solution.py:75
  34.5 3.1 %collective-permute-done.7.refs_6_ = bf16[2,24,2432]{2,1,0:T(8,128)(2,1)S(1)} collective-permute-done((bf16[2,24,2432]{2,1,0:T(8,128)(2,1)S(1)}, bf16[2,24,2432]{2,1,0:T(8,128)(2,1)S(1)}, u32[]{:S(2)}, u32[]{:S(2)}) %collective-permute-start.7) | collective-permute-done | bytes 233504 | tf_op jit(solution)/shard_map/ppermute | solution.py:67
  47.2 8.8 %project_qkv.1 = (bf16[1024,768]{1,0:T(8,128)(2,1)}, bf16[1024,768]{1,0:T(8,128)(2,1)}, bf16[1024,768]{1,0:T(8,128)(2,1)}, f32[16,768]{1,0:T(8,128)}, bf16[3,768,768]{2,1,0:T(8,128)(2,1)}) custom-call(s32[5]{0:T(128)} %stack.41.coords, bf16[1024,768]{1,0:T(8,128)(2,1)} %left, bf16[2,24,2432]{2,1,0:T(8,128)(2,1)} %copy-done.9, ...), custom_call_target="tpu_custom_call" | custom-call | flops 3623878656 | bytes 7864320 | tf_op jit(solution)/shard_map/project_qkv/pallas_call | solution.py:371
  56.0 25.2 %attention_forward.1 = (bf16[1024,768]{1,0:T(8,128)(2,1)}, bf16[6,2,912,1024]{3,2,1,0:T(8,128)(2,1)}) custom-call(bf16[1024,768]{1,0:T(8,128)(2,1)} %get-tuple-element.136.q_ref.refs_1_, bf16[1024,768]{1,0:T(8,128)(2,1)} %get-tuple-element.107.k_ref.refs_2_, bf16[1024,768]{1,0:T(8,128)(2,1)} %get-tuple-element.108.v_ref.refs_3_, ...), custom_call_target="tpu_custom_call" | custom-call | flops 12884901888 | bytes 6291456 | tf_op jit(solution)/shard_map/attention_forward/pallas_call | solution.py:417
  81.2 24.0 %all-gather.4.cloned.1.call-done.refs_0_ = bf16[3072,1792]{1,0:T(8,128)(2,1)} async-done(((bf16[96,1792]{1,0:T(8,128)(2,1)}), bf16[3072,1792]{1,0:T(8,128)(2,1)}) %all-gather.4.cloned.1.call-update) | async-done | bytes 11010064 | tf_op jit(solution)/shard_map/all_gather | solution.py:1097
  105.2 38.4 %feed_forward.1 = (bf16[1024,768]{1,0:T(8,128)(2,1)}, bf16[1024,768]{1,0:T(8,128)(2,1)}, bf16[1024,3072]{1,0:T(8,128)(2,1)}, bf16[1024,768]{1,0:T(8,128)(2,1)}, ...) custom-call(s32[1]{0:T(128)} %bitcast.1.total_ref, ...), custom_call_target="tpu_custom_call" | custom-call | flops 21743271936000 | bytes 33030144000 | tf_op jit(solution)/shard_map/feed_forward/pallas_call | solution.py:774
  143.6 10.1 %grad_down.1 = (bf16[16,24,3072]{2,1,0:T(8,128)(2,1)}, bf16[16,24,3072]{2,1,0:T(8,128)(2,1)}) custom-call(s32[5]{0:T(128)} %stack.41.coords, bf16[1024,3072]{1,0:T(8,128)(2,1)} %get-tuple-element.114.left, bf16[1024,768]{1,0:T(8,128)(2,1)} %get-tuple-element.115.right), custom_call_target="tpu_custom_call" | custom-call | flops 4831838208000 | bytes 7864320000 | tf_op jit(solution)/shard_map/grad_down/pallas_call | solution.py:848
  154.0 11.6 %grad_up_and_out.1 = (bf16[16,24,3840]{2,1,0:T(8,128)(2,1)}, bf16[16,24,3840]{2,1,0:T(8,128)(2,1)}) custom-call(s32[5]{0:T(128)} %stack.41.coords, bf16[1024,768]{1,0:T(8,128)(2,1)} %get-tuple-element.118.left, bf16[1024,3072]{1,0:T(8,128)(2,1)} %get-tuple-element.119.right, bf16[1024,768]{1,0:T(8,128)(2,1)} %get-tuple-element.109.context.out_left, ...), custom_call_target="tpu_custom_call" | custom-call | flops 6039797760000 | bytes 16515072000 | tf_op jit(solution)/shard_map/grad_up_and_out/pallas_call | solution.py:905
  165.9 4.3 %reduce_over_core.3 = (bf16[2,2,24,3072]{3,2,1,0:T(8,128)(2,1)}, bf16[2,2,24,3072]{3,2,1,0:T(8,128)(2,1)}, bf16[2,2,24,3072]{3,2,1,0:T(8,128)(2,1)}, bf16[2,2,24,3072]{3,2,1,0:T(8,128)(2,1)}) custom-call(s32[5]{0:T(128)} %stack.41.coords, bf16[2,2,4,24,3072]{4,3,2,1,0:T(8,128)(2,1)} %bitcast.68, ...), custom_call_target="tpu_custom_call" | custom-call | flops 1179648000000 | bytes 7077888000000 | tf_op jit(solution)/shard_map/reduce_over_core/pallas_call | solution.py:129
  172.4 11.0 %attention_backward.2 = (bf16[3,1024,768]{2,1,0:T(8,128)(2,1)}, f32[8,768]{1,0:T(8,128)}) custom-call(s32[1]{0:T(128)} %bitcast.62, bf16[1024,768]{1,0:T(8,128)(2,1)} %get-tuple-element.136.q_ref.refs_1_, bf16[1024,768]{1,0:T(8,128)(2,1)} %get-tuple-element.107.k_ref.refs_2_, bf16[1024,768]{1,0:T(8,128)(2,1)} %get-tuple-element.108.v_ref.refs_3_, ...), custom_call_target="tpu_custom_call" | custom-call | flops 8589934592000 | bytes 3670016000 | tf_op jit(solution)/shard_map/attention_backward/pallas_call | solution.py:521
  183.5 4.8 %reduce_over_core.4 = (bf16[2,2,24,3840]{3,2,1,0:T(8,128)(2,1)}, bf16[2,2,24,3840]{3,2,1,0:T(8,128)(2,1)}, bf16[2,2,24,3840]{3,2,1,0:T(8,128)(2,1)}, bf16[2,2,24,3840]{3,2,1,0:T(8,128)(2,1)}) custom-call(s32[5]{0:T(128)} %stack.41.coords, bf16[2,2,4,24,3840]{4,3,2,1,0:T(8,128)(2,1)} %bitcast.64, ...), custom_call_target="tpu_custom_call" | custom-call | flops 1474560000000 | bytes 8847360000000 | tf_op jit(solution)/shard_map/reduce_over_core/pallas_call | solution.py:129
  190.6 18.7 %attention_backward.3 = (bf16[3,1024,768]{2,1,0:T(8,128)(2,1)}, f32[8,768]{1,0:T(8,128)}) custom-call(s32[1]{0:T(128)} %bitcast.63, bf16[1024,768]{1,0:T(8,128)(2,1)} %get-tuple-element.136.q_ref.refs_1_, bf16[1024,768]{1,0:T(8,128)(2,1)} %get-tuple-element.107.k_ref.refs_2_, ...), custom_call_target="tpu_custom_call", output_to_operand_aliasing={{0}: (6, {}), {1}: (7, {})} | custom-call | flops 17179869184000 | bytes 7340032000 | tf_op jit(solution)/shard_map/attention_backward/pallas_call | solution.py:521
  209.4 4.9 %reduce_over_first_link.2 = (bf16[2,24,6912]{2,1,0:T(8,128)(2,1)}, bf16[2,24,6912]{2,1,0:T(8,128)(2,1)}, bf16[2,24,6912]{2,1,0:T(8,128)(2,1)}, bf16[2,24,6912]{2,1,0:T(8,128)(2,1)}) custom-call(s32[5]{0:T(128)} %stack.41.coords, bf16[2,2,24,3072]{3,2,1,0:T(8,128)(2,1)} %get-tuple-element.139.refs_0_.refs_2_, ...), custom_call_target="tpu_custom_call" | custom-call | flops 1327104000000 | bytes 7962624000000 | tf_op jit(solution)/shard_map/reduce_over_first_link/pallas_call | solution.py:170
  216.0 8.5 %grad_qkv.1 = (bf16[16,24,2432]{2,1,0:T(8,128)(2,1)}, bf16[16,24,2432]{2,1,0:T(8,128)(2,1)}) custom-call(s32[5]{0:T(128)} %stack.41.coords, bf16[1024,768]{1,0:T(8,128)(2,1)} %left, bf16[3,1024,768]{2,1,0:T(8,128)(2,1)} %get-tuple-element.149.right.grads, f32[24,768]{1,0:T(8,128)} %get-tuple-element.128.sums, f32[8,768]{1,0:T(8,128)} %get-tuple-element.138.more), custom_call_target="tpu_custom_call" | custom-call | flops 3623878656000 | bytes 11010048000 | tf_op jit(solution)/shard_map/grad_qkv/pallas_call | solution.py:993
  224.8 7.1 %collective-permute-done.23.got_a = bf16[2,24,6912]{2,1,0:T(8,128)(2,1)} collective-permute-done((bf16[2,24,6912]{2,1,0:T(8,128)(2,1)}, bf16[2,24,6912]{2,1,0:T(8,128)(2,1)}, u32[]{:S(2)}, u32[]{:S(2)}) %collective-permute-start.23) | collective-permute-done | bytes 663584 | tf_op jit(solution)/shard_map/ppermute | solution.py:67
  233.3 3.0 %reduce_over_second_link.2 = (bf16[2,24,6912]{2,1,0:T(8,128)(2,1)}, bf16[2,24,6912]{2,1,0:T(8,128)(2,1)}) custom-call(s32[5]{0:T(128)} %stack.41.coords, bf16[2,24,6912]{2,1,0:T(8,128)(2,1)} %get-tuple-element.154.keep_a, bf16[2,24,6912]{2,1,0:T(8,128)(2,1)} %collective-permute-done.23.got_a, bf16[2,24,6912]{2,1,0:T(8,128)(2,1)} %get-tuple-element.156.keep_b, ...), custom_call_target="tpu_custom_call" | custom-call | flops 663552000000 | bytes 1990656000000 | tf_op jit(solution)/shard_map/reduce_over_second_link/pallas_call | solution.py:212
  236.4 3.9 %reduce_over_core.5 = (bf16[2,2,24,2432]{3,2,1,0:T(8,128)(2,1)}, bf16[2,2,24,2432]{3,2,1,0:T(8,128)(2,1)}, bf16[2,2,24,2432]{3,2,1,0:T(8,128)(2,1)}, bf16[2,2,24,2432]{3,2,1,0:T(8,128)(2,1)}) custom-call(s32[5]{0:T(128)} %stack.41.coords, bf16[2,2,4,24,2432]{4,3,2,1,0:T(8,128)(2,1)} %bitcast.72, ...), custom_call_target="tpu_custom_call" | custom-call | flops 933888000000 | bytes 5603328000000 | tf_op jit(solution)/shard_map/reduce_over_core/pallas_call | solution.py:129
  242.0 8.7 %frames_gradient.1 = bf16[1024,768]{1,0:T(8,128)(2,1)} custom-call(f32[1024,768]{1,0:T(8,128)} %get-tuple-element.162.first_g, bf16[3,1024,768]{2,1,0:T(8,128)(2,1)} %get-tuple-element.149.right.grads, bf16[3,768,768]{2,1,0:T(8,128)(2,1)} %get-tuple-element.163.weights), custom_call_target="tpu_custom_call" | custom-call | flops 3623878656000 | bytes 12976128000 | tf_op jit(solution)/shard_map/frames_gradient/pallas_call | solution.py:1031
  255.6 3.3 %reduce_over_first_link.3 = (bf16[2,24,2432]{2,1,0:T(8,128)(2,1)}, bf16[2,24,2432]{2,1,0:T(8,128)(2,1)}, bf16[2,24,2432]{2,1,0:T(8,128)(2,1)}, bf16[2,24,2432]{2,1,0:T(8,128)(2,1)}) custom-call(s32[5]{0:T(128)} %stack.41.coords, bf16[2,2,24,2432]{3,2,1,0:T(8,128)(2,1)} %get-tuple-element.172.refs_0_.refs_2_, ...), custom_call_target="tpu_custom_call" | custom-call | flops 466944000 | bytes 2801664000 | tf_op jit(solution)/shard_map/reduce_over_first_link/pallas_call | solution.py:170
  259.5 6.4 %collective-permute-done.30.got_a = bf16[2,24,2432]{2,1,0:T(8,128)(2,1)S(1)} collective-permute-done((bf16[2,24,2432]{2,1,0:T(8,128)(2,1)}, bf16[2,24,2432]{2,1,0:T(8,128)(2,1)S(1)}, u32[]{:S(2)}, u32[]{:S(2)}) %collective-permute-start.30) | collective-permute-done | bytes 233504 | tf_op jit(solution)/shard_map/ppermute | solution.py:67
  269.0 3.5 %collective-permute-done.27 = bf16[24,6912]{1,0:T(8,128)(2,1)S(1)} collective-permute-done((bf16[24,6912]{1,0:T(8,128)(2,1)}, bf16[24,6912]{1,0:T(8,128)(2,1)S(1)}, u32[]{:S(2)}, u32[]{:S(2)}) %collective-permute-start.27) | collective-permute-done | bytes 331808 | tf_op jit(solution)/shard_map/ppermute | solution.py:79
  275.8 2.9 collective-permute-start.34
  283.3 3.7 %collective-permute-done.33 = bf16[24,2432]{1,0:T(8,128)(2,1)S(1)} collective-permute-done((bf16[24,2432]{1,0:T(8,128)(2,1)}, bf16[24,2432]{1,0:T(8,128)(2,1)S(1)}, u32[]{:S(2)}, u32[]{:S(2)}) %collective-permute-start.33) | collective-permute-done | bytes 116768 | tf_op jit(solution)/shard_map/ppermute | solution.py:75
  (164 shorter events, 58.6 us)
Async XLA Ops:
  7.2 98.0 %all-gather.4.cloned.1.call-start = ((), (), s32[]{:S(2)}) async-start(), calls=%async_computation | async-start | bytes 11354112 | tf_op jit(solution)/shard_map/all_gather | solution.py:1097
  11.2 198.2 %all-gather.6.cloned.1.call-start = ((), (), s32[]{:S(2)}) async-start(), calls=%async_computation.1 | async-start | bytes 2433024 | tf_op jit(solution)/shard_map/all_gather | solution.py:1130
  14.3 10.6 %collective-permute-start.5 = (bf16[24,2432]{1,0:T(8,128)(2,1)}, bf16[24,2432]{1,0:T(8,128)(2,1)S(1)}, u32[]{:S(2)}, u32[]{:S(2)}) collective-permute-start(bf16[24,2432]{1,0:T(8,128)(2,1)} %get-tuple-element.105), channel_id=1, source_target_pairs={{0,6},{1,7},{2,0},{3,1},{4,2},{5,3},{6,4},{7,5},{8,14},{9,15},{10,... | collective-permute-start | bytes 350216 | tf_op jit(solution)/shard_map/ppermute | solution.py:75
  16.4 11.3 %collective-permute-start.4 = (bf16[24,2432]{1,0:T(8,128)(2,1)}, bf16[24,2432]{1,0:T(8,128)(2,1)S(1)}, u32[]{:S(2)}, u32[]{:S(2)}) collective-permute-start(bf16[24,2432]{1,0:T(8,128)(2,1)} %get-tuple-element.105), channel_id=1, source_target_pairs={{0,4},{1,5},{2,6},{3,7},{4,0},{5,1},{6,2},{7,3},{8,12},{9,13},{10,... | collective-permute-start | bytes 350216 | tf_op jit(solution)/shard_map/ppermute | solution.py:75
  21.6 11.0 %collective-permute-start.2 = (bf16[2,24,2432]{2,1,0:T(8,128)(2,1)S(1)}, bf16[2,24,2432]{2,1,0:T(8,128)(2,1)S(1)}, u32[]{:S(2)}, u32[]{:S(2)}) collective-permute-start(bf16[2,24,2432]{2,1,0:T(8,128)(2,1)S(1)} %pad_maximum_fusion.refs_0_), channel_id=1, source_target_pairs={{0,16},{8,24},{16,0},{24,8},{1,17},{9,25},{17,1},{25,9},{2,18},{10... | collective-permute-start | bytes 700424 | tf_op jit(solution)/shard_map/ppermute | solution.py:67
  23.3 10.0 %collective-permute-start.1 = (bf16[2,24,2432]{2,1,0:T(8,128)(2,1)S(1)}, bf16[2,24,2432]{2,1,0:T(8,128)(2,1)S(1)}, u32[]{:S(2)}, u32[]{:S(2)}) collective-permute-start(bf16[2,24,2432]{2,1,0:T(8,128)(2,1)S(1)} %pad_maximum_fusion.refs_0_), channel_id=1, source_target_pairs={{0,8},{8,0},{16,24},{24,16},{1,9},{9,1},{17,25},{25,17},{2,10},{10... | collective-permute-start | bytes 700424 | tf_op jit(solution)/shard_map/ppermute | solution.py:64
  27.7 9.9 %collective-permute-start.7 = (bf16[2,24,2432]{2,1,0:T(8,128)(2,1)S(1)}, bf16[2,24,2432]{2,1,0:T(8,128)(2,1)S(1)}, u32[]{:S(2)}, u32[]{:S(2)}) collective-permute-start(bf16[2,24,2432]{2,1,0:T(8,128)(2,1)S(1)} %pad_maximum_fusion.1.refs_4_), channel_id=1, source_target_pairs={{0,16},{8,24},{16,0},{24,8},{1,17},{9,25},{17,1},{25,9},{2,18},{10... | collective-permute-start | bytes 700424 | tf_op jit(solution)/shard_map/ppermute | solution.py:67
  29.4 11.4 %collective-permute-start.13 = (bf16[2,24,2432]{2,1,0:T(8,128)(2,1)S(1)}, bf16[2,24,2432]{2,1,0:T(8,128)(2,1)S(1)}, u32[]{:S(2)}, u32[]{:S(2)}) collective-permute-start(bf16[2,24,2432]{2,1,0:T(8,128)(2,1)S(1)} %pad_maximum_fusion.1.refs_4_), channel_id=1, source_target_pairs={{0,1},{1,0},{2,3},{3,2},{4,5},{5,4},{6,7},{7,6},{8,9},{9,8},{10,11... | collective-permute-start | bytes 700424 | tf_op jit(solution)/shard_map/ppermute | solution.py:70
  29.4 11.4 %collective-permute-start.6 = (bf16[2,24,2432]{2,1,0:T(8,128)(2,1)S(1)}, bf16[2,24,2432]{2,1,0:T(8,128)(2,1)S(1)}, u32[]{:S(2)}, u32[]{:S(2)}) collective-permute-start(bf16[2,24,2432]{2,1,0:T(8,128)(2,1)S(1)} %pad_maximum_fusion.1.refs_4_), channel_id=1, source_target_pairs={{0,8},{8,0},{16,24},{24,16},{1,9},{9,1},{17,25},{25,17},{2,10},{10... | collective-permute-start | bytes 700424 | tf_op jit(solution)/shard_map/ppermute | solution.py:64
  153.8 12.2 %collective-permute-start.17 = (bf16[16,24,3072]{2,1,0:T(8,128)(2,1)}, bf16[16,24,3072]{2,1,0:T(8,128)(2,1)}, u32[]{:S(2)}, u32[]{:S(2)}) collective-permute-start(bf16[16,24,3072]{2,1,0:T(8,128)(2,1)} %get-tuple-element.123), channel_id=1, source_target_pairs={{0,1},{1,0},{2,3},{3,2},{4,5},{5,4},{6,7},{7,6},{8,9},{9,8},{10,11... | collective-permute-start | bytes 7077896 | tf_op jit(solution)/shard_map/ppermute | solution.py:70
  165.6 17.9 %collective-permute-start.20 = (bf16[16,24,3840]{2,1,0:T(8,128)(2,1)}, bf16[16,24,3840]{2,1,0:T(8,128)(2,1)}, u32[]{:S(2)}, u32[]{:S(2)}) collective-permute-start(bf16[16,24,3840]{2,1,0:T(8,128)(2,1)} %get-tuple-element.134), channel_id=1, source_target_pairs={{0,1},{1,0},{2,3},{3,2},{4,5},{5,4},{6,7},{7,6},{8,9},{9,8},{10,11... | collective-permute-start | bytes 8847368 | tf_op jit(solution)/shard_map/ppermute | solution.py:70
  170.3 39.0 %collective-permute-start.18 = (bf16[2,2,24,3072]{3,2,1,0:T(8,128)(2,1)}, bf16[2,2,24,3072]{3,2,1,0:T(8,128)(2,1)}, u32[]{:S(2)}, u32[]{:S(2)}) collective-permute-start(bf16[2,2,24,3072]{3,2,1,0:T(8,128)(2,1)} %get-tuple-element.125), channel_id=1, source_target_pairs={{0,8},{8,0},{16,24},{24,16},{1,9},{9,1},{17,25},{25,17},{2,10},{10... | collective-permute-start | bytes 1769480 | tf_op jit(solution)/shard_map/ppermute | solution.py:64
  171.8 37.5 %collective-permute-start.19 = (bf16[2,2,24,3072]{3,2,1,0:T(8,128)(2,1)}, bf16[2,2,24,3072]{3,2,1,0:T(8,128)(2,1)}, u32[]{:S(2)}, u32[]{:S(2)}) collective-permute-start(bf16[2,2,24,3072]{3,2,1,0:T(8,128)(2,1)} %get-tuple-element.127), channel_id=1, source_target_pairs={{0,16},{8,24},{16,0},{24,8},{1,17},{9,25},{17,1},{25,9},{2,18},{10... | collective-permute-start | bytes 1769480 | tf_op jit(solution)/shard_map/ppermute | solution.py:67
  188.3 21.1 %collective-permute-start.21 = (bf16[2,2,24,3840]{3,2,1,0:T(8,128)(2,1)}, bf16[2,2,24,3840]{3,2,1,0:T(8,128)(2,1)}, u32[]{:S(2)}, u32[]{:S(2)}) collective-permute-start(bf16[2,2,24,3840]{3,2,1,0:T(8,128)(2,1)} %get-tuple-element.143), channel_id=1, source_target_pairs={{0,8},{8,0},{16,24},{24,16},{1,9},{9,1},{17,25},{25,17},{2,10},{10... | collective-permute-start | bytes 2211848 | tf_op jit(solution)/shard_map/ppermute | solution.py:64
  189.8 19.5 %collective-permute-start.22 = (bf16[2,2,24,3840]{3,2,1,0:T(8,128)(2,1)}, bf16[2,2,24,3840]{3,2,1,0:T(8,128)(2,1)}, u32[]{:S(2)}, u32[]{:S(2)}) collective-permute-start(bf16[2,2,24,3840]{3,2,1,0:T(8,128)(2,1)} %get-tuple-element.145), channel_id=1, source_target_pairs={{0,16},{8,24},{16,0},{24,8},{1,17},{9,25},{17,1},{25,9},{2,18},{10... | collective-permute-start | bytes 2211848 | tf_op jit(solution)/shard_map/ppermute | solution.py:67
  214.3 17.6 %collective-permute-start.23 = (bf16[2,24,6912]{2,1,0:T(8,128)(2,1)}, bf16[2,24,6912]{2,1,0:T(8,128)(2,1)}, u32[]{:S(2)}, u32[]{:S(2)}) collective-permute-start(bf16[2,24,6912]{2,1,0:T(8,128)(2,1)} %get-tuple-element.151), channel_id=1, source_target_pairs={{0,16},{8,24},{16,0},{24,8},{1,17},{9,25},{17,1},{25,9},{2,18},{10... | collective-permute-start | bytes 1990664 | tf_op jit(solution)/shard_map/ppermute | solution.py:67
  215.5 17.9 %collective-permute-start.24 = (bf16[2,24,6912]{2,1,0:T(8,128)(2,1)}, bf16[2,24,6912]{2,1,0:T(8,128)(2,1)}, u32[]{:S(2)}, u32[]{:S(2)}) collective-permute-start(bf16[2,24,6912]{2,1,0:T(8,128)(2,1)} %get-tuple-element.153), channel_id=1, source_target_pairs={{0,8},{8,0},{16,24},{24,16},{1,9},{9,1},{17,25},{25,17},{2,10},{10... | collective-permute-start | bytes 1990664 | tf_op jit(solution)/shard_map/ppermute | solution.py:64
  224.5 11.9 %collective-permute-start.25 = (bf16[16,24,2432]{2,1,0:T(8,128)(2,1)}, bf16[16,24,2432]{2,1,0:T(8,128)(2,1)}, u32[]{:S(2)}, u32[]{:S(2)}) collective-permute-start(bf16[16,24,2432]{2,1,0:T(8,128)(2,1)} %get-tuple-element.160), channel_id=1, source_target_pairs={{0,1},{1,0},{2,3},{3,2},{4,5},{5,4},{6,7},{7,6},{8,9},{9,8},{10,11... | collective-permute-start | bytes 5603336 | tf_op jit(solution)/shard_map/ppermute | solution.py:70
  236.4 17.0 %collective-permute-start.26 = (bf16[2,24,6912]{2,1,0:T(8,128)(2,1)}, bf16[2,24,6912]{2,1,0:T(8,128)(2,1)}, u32[]{:S(2)}, u32[]{:S(2)}) collective-permute-start(bf16[2,24,6912]{2,1,0:T(8,128)(2,1)} %get-tuple-element.164), channel_id=1, source_target_pairs={{0,2},{1,3},{2,0},{3,1},{4,6},{5,7},{6,4},{7,5},{8,10},{9,11},{10,... | collective-permute-start | bytes 1990664 | tf_op jit(solution)/shard_map/ppermute | solution.py:79
  240.3 15.3 %collective-permute-start.28 = (bf16[2,2,24,2432]{3,2,1,0:T(8,128)(2,1)}, bf16[2,2,24,2432]{3,2,1,0:T(8,128)(2,1)}, u32[]{:S(2)}, u32[]{:S(2)}) collective-permute-start(bf16[2,2,24,2432]{3,2,1,0:T(8,128)(2,1)} %get-tuple-element.169), channel_id=1, source_target_pairs={{0,8},{8,0},{16,24},{24,16},{1,9},{9,1},{17,25},{25,17},{2,10},{10... | collective-permute-start | bytes 1400840 | tf_op jit(solution)/shard_map/ppermute | solution.py:64
  240.7 15.0 %collective-permute-start.29 = (bf16[2,2,24,2432]{3,2,1,0:T(8,128)(2,1)}, bf16[2,2,24,2432]{3,2,1,0:T(8,128)(2,1)}, u32[]{:S(2)}, u32[]{:S(2)}) collective-permute-start(bf16[2,2,24,2432]{3,2,1,0:T(8,128)(2,1)} %get-tuple-element.171), channel_id=1, source_target_pairs={{0,16},{8,24},{16,0},{24,8},{1,17},{9,25},{17,1},{25,9},{2,18},{10... | collective-permute-start | bytes 1400840 | tf_op jit(solution)/shard_map/ppermute | solution.py:67
  255.6 16.9 %collective-permute-start.27 = (bf16[24,6912]{1,0:T(8,128)(2,1)}, bf16[24,6912]{1,0:T(8,128)(2,1)S(1)}, u32[]{:S(2)}, u32[]{:S(2)}) collective-permute-start(bf16[24,6912]{1,0:T(8,128)(2,1)} %get-tuple-element.168), channel_id=1, source_target_pairs={{0,4},{1,5},{2,6},{3,7},{4,0},{5,1},{6,2},{7,3},{8,12},{9,13},{10,... | collective-permute-start | bytes 995336 | tf_op jit(solution)/shard_map/ppermute | solution.py:79
  274.9 12.2 %collective-permute-start.33 = (bf16[24,2432]{1,0:T(8,128)(2,1)}, bf16[24,2432]{1,0:T(8,128)(2,1)S(1)}, u32[]{:S(2)}, u32[]{:S(2)}) collective-permute-start(bf16[24,2432]{1,0:T(8,128)(2,1)} %get-tuple-element.183), channel_id=1, source_target_pairs={{0,4},{1,5},{2,6},{3,7},{4,0},{5,1},{6,2},{7,3},{8,12},{9,13},{10,... | collective-permute-start | bytes 350216 | tf_op jit(solution)/shard_map/ppermute | solution.py:75
  275.8 11.3 %collective-permute-start.34 = (bf16[24,2432]{1,0:T(8,128)(2,1)}, bf16[24,2432]{1,0:T(8,128)(2,1)S(1)}, u32[]{:S(2)}, u32[]{:S(2)}) collective-permute-start(bf16[24,2432]{1,0:T(8,128)(2,1)} %get-tuple-element.184), channel_id=1, source_target_pairs={{0,6},{1,7},{2,0},{3,1},{4,2},{5,3},{6,4},{7,5},{8,14},{9,15},{10,... | collective-permute-start | bytes 350216 | tf_op jit(solution)/shard_map/ppermute | solution.py:75
  (48 other events, 358.5 us)
Sparse Core Ops, SparseCore 0:
  11.6 93.5 all-gather.3
  143.8 55.8 all-gather.5

commit v5 on v4

--- a/solution.py
+++ b/solution.py
@@ -1139,7 +1139,9 @@
             place, after(frames, (done, all_sums)), qkv_g, sums, bias_sums, valid
         )
         got = place.swap_core(theirs)
-        most.sums = after(most.sums, mine)
+        squares = jnp.sum(after(all_sums, mine)[:, 12:17], axis=(0, 2))
+        layer_rms = jnp.sqrt(squares[0:4] / squares[4])
+        most.sums = after(most.sums, (mine, layer_rms))
         done = most.third()
         last = Reduction(place)
         done = last.first(after(mine, done), got)
@@ -1149,7 +1151,7 @@
         last.parts[0] = after(last.parts[0], done)
         last.second(1000)
         done = last.spread(1000)
-        most.sums, all_sums = after((most.sums, all_sums), done)
+        most.sums = after(most.sums, done)
         grad_most = most.result()
         grad_qkv = last.result()
         grad_down = grad_most[:, : 4 * width].reshape(rows, 4, width)
@@ -1161,8 +1163,6 @@
             window, (32 * (place.index % 4),), (vector_master.shape[0],)
         )
         grad_qkv = grad_qkv[:, : 3 * width].reshape(rows, 3, width).transpose(1, 0, 2)
-        squares = jnp.sum(all_sums[:, 12:17], axis=(0, 2))
-        layer_rms = jnp.sqrt(squares[0:4] / squares[4])
     else:
         def scatter(value, dimension):
             return lax.psum_scatter(value, AXES, scatter_dimension=dimension, tiled=True)

time: 301 us -> 298 us (0.990)
  waiting for transfers between devices: 64 us -> 57.9 us
    ppermute x8, waiting for transfers between devices: 18.6 us -> 13.4 us  [swap_y(): return lax.ppermute(value, 'dp', [(i, i ^ 2) for i in range(self.n_dp)])]
  transfers between devices with their start and end apart: 37 -> 37, of which waited for: 16 -> 17; matrix products, arithmetic and copies ran while one was open for 3% -> 3% of each run, Pallas kernels for 43% -> 43%
where the time goes in v5:
time: 298 us; the launch traced here: 293 us
  Pallas kernels  172 us (58%)
  waiting for transfers between devices  57.9 us (19%)
  starting transfers between devices  32.3 us (11%)
  between operations  14.8 us (5%)
  other arithmetic  10.5 us (4%)
  local copies, waits for them, and re-layouts  5.14 us (2%)
    pallas_call x1, Pallas kernels, middle(): pl.pallas_call(partial(middle_kernel, packed, last_rows), grid=(tiles + 1...  38.4 us
    pallas_call x2, Pallas kernels, attention_backward(): pl.pallas_call(kernel, grid=(pairs,), in_specs=[pl.BlockSpec(memory_space...  29.7 us
    pallas_call x1, Pallas kernels, attention_forward(): pl.pallas_call(attention_forward_kernel, grid=(pairs,), in_specs=[column]...  25.2 us
    all_gather x1, waiting for transfers between devices, shards(): wire = lax.all_gather(wire_low, AXES, axis=0, tiled=True)  24 us
    ppermute x8, waiting for transfers between devices, swap_y(): return lax.ppermute(value, 'dp', [(i, i ^ 2) for i in range(self.n_dp)])  13.4 us
    pallas_call x3, Pallas kernels, first_add(): pl.pallas_call(first_add_kernel, grid_spec=pltpu.PrefetchScalarGridSpec(n...  13.1 us
    pallas_call x1, Pallas kernels, up_grad(): pl.pallas_call(partial(up_grad_kernel, valid, rows), grid_spec=pltpu.Pref...  11.6 us
    ppermute x6, waiting for transfers between devices, shift_z(): return lax.ppermute(value, 'fsdp', pairs)  10.2 us
  transfers between devices with their start and end apart: 37, of which 17 were waited for; matrix products, arithmetic and copies ran while one was open for 3% of the time, Pallas kernels for 43%

profile of v5, /device:TPU:0, one launch (start us, length us, event | category | flops | bytes accessed | tf_op | source)
XLA Modules:
  0.0 292.6 jit_solution(15243416130534906843)
XLA Ops:
  11.2 3.1 %collective-permute-start = (bf16[24,2432]{1,0:T(8,128)(2,1)}, bf16[24,2432]{1,0:T(8,128)(2,1)S(1)}, u32[]{:S(2)}, u32[]{:S(2)}) collective-permute-start(bf16[24,2432]{1,0:T(8,128)(2,1)} %get-tuple-element.105), channel_id=1, source_target_pairs={{0,2},{1,3},{2,4},{3,5},{4,6},{5,7},{6,0},{7,1},{8,10},{9,11},{10,... | collective-permute-start | bytes 350216 | tf_op jit(solution)/shard_map/ppermute | solution.py:75
  17.3 3.2 %collective-permute-done = bf16[24,2432]{1,0:T(8,128)(2,1)S(1)} collective-permute-done((bf16[24,2432]{1,0:T(8,128)(2,1)}, bf16[24,2432]{1,0:T(8,128)(2,1)S(1)}, u32[]{:S(2)}, u32[]{:S(2)}) %collective-permute-start) | collective-permute-done | bytes 116768 | tf_op jit(solution)/shard_map/ppermute | solution.py:75
  24.8 2.8 collective-permute-done.4
  34.5 3.1 %collective-permute-done.7.refs_6_ = bf16[2,24,2432]{2,1,0:T(8,128)(2,1)S(1)} collective-permute-done((bf16[2,24,2432]{2,1,0:T(8,128)(2,1)S(1)}, bf16[2,24,2432]{2,1,0:T(8,128)(2,1)S(1)}, u32[]{:S(2)}, u32[]{:S(2)}) %collective-permute-start.7) | collective-permute-done | bytes 233504 | tf_op jit(solution)/shard_map/ppermute | solution.py:67
  47.2 8.8 %project_qkv.1 = (bf16[1024,768]{1,0:T(8,128)(2,1)}, bf16[1024,768]{1,0:T(8,128)(2,1)}, bf16[1024,768]{1,0:T(8,128)(2,1)}, f32[16,768]{1,0:T(8,128)}, bf16[3,768,768]{2,1,0:T(8,128)(2,1)}) custom-call(s32[5]{0:T(128)} %stack.41.coords, bf16[1024,768]{1,0:T(8,128)(2,1)} %left, bf16[2,24,2432]{2,1,0:T(8,128)(2,1)} %copy-done.9, ...), custom_call_target="tpu_custom_call" | custom-call | flops 3623878656 | bytes 7864320 | tf_op jit(solution)/shard_map/project_qkv/pallas_call | solution.py:371
  56.0 25.2 %attention_forward.1 = (bf16[1024,768]{1,0:T(8,128)(2,1)}, bf16[6,2,912,1024]{3,2,1,0:T(8,128)(2,1)}) custom-call(bf16[1024,768]{1,0:T(8,128)(2,1)} %get-tuple-element.136.q_ref.refs_1_, bf16[1024,768]{1,0:T(8,128)(2,1)} %get-tuple-element.107.k_ref.refs_2_, bf16[1024,768]{1,0:T(8,128)(2,1)} %get-tuple-element.108.v_ref.refs_3_, ...), custom_call_target="tpu_custom_call" | custom-call | flops 12884901888 | bytes 6291456 | tf_op jit(solution)/shard_map/attention_forward/pallas_call | solution.py:417
  81.2 24.0 %all-gather.4.cloned.1.call-done.refs_0_ = bf16[3072,1792]{1,0:T(8,128)(2,1)} async-done(((bf16[96,1792]{1,0:T(8,128)(2,1)}), bf16[3072,1792]{1,0:T(8,128)(2,1)}) %all-gather.4.cloned.1.call-update) | async-done | bytes 11010064 | tf_op jit(solution)/shard_map/all_gather | solution.py:1097
  105.2 38.4 %feed_forward.1 = (bf16[1024,768]{1,0:T(8,128)(2,1)}, bf16[1024,768]{1,0:T(8,128)(2,1)}, bf16[1024,3072]{1,0:T(8,128)(2,1)}, bf16[1024,768]{1,0:T(8,128)(2,1)}, ...) custom-call(s32[1]{0:T(128)} %bitcast.1.total_ref, ...), custom_call_target="tpu_custom_call" | custom-call | flops 21743271936000 | bytes 33030144000 | tf_op jit(solution)/shard_map/feed_forward/pallas_call | solution.py:774
  143.6 10.1 %grad_down.1 = (bf16[16,24,3072]{2,1,0:T(8,128)(2,1)}, bf16[16,24,3072]{2,1,0:T(8,128)(2,1)}) custom-call(s32[5]{0:T(128)} %stack.41.coords, bf16[1024,3072]{1,0:T(8,128)(2,1)} %get-tuple-element.114.left, bf16[1024,768]{1,0:T(8,128)(2,1)} %get-tuple-element.115.right), custom_call_target="tpu_custom_call" | custom-call | flops 4831838208000 | bytes 7864320000 | tf_op jit(solution)/shard_map/grad_down/pallas_call | solution.py:848
  154.0 11.6 %grad_up_and_out.1 = (bf16[16,24,3840]{2,1,0:T(8,128)(2,1)}, bf16[16,24,3840]{2,1,0:T(8,128)(2,1)}) custom-call(s32[5]{0:T(128)} %stack.41.coords, bf16[1024,768]{1,0:T(8,128)(2,1)} %get-tuple-element.118.left, bf16[1024,3072]{1,0:T(8,128)(2,1)} %get-tuple-element.119.right, bf16[1024,768]{1,0:T(8,128)(2,1)} %get-tuple-element.109.context.out_left, ...), custom_call_target="tpu_custom_call" | custom-call | flops 6039797760000 | bytes 16515072000 | tf_op jit(solution)/shard_map/grad_up_and_out/pallas_call | solution.py:905
  165.9 4.3 %reduce_over_core.3 = (bf16[2,2,24,3072]{3,2,1,0:T(8,128)(2,1)}, bf16[2,2,24,3072]{3,2,1,0:T(8,128)(2,1)}, bf16[2,2,24,3072]{3,2,1,0:T(8,128)(2,1)}, bf16[2,2,24,3072]{3,2,1,0:T(8,128)(2,1)}) custom-call(s32[5]{0:T(128)} %stack.41.coords, bf16[2,2,4,24,3072]{4,3,2,1,0:T(8,128)(2,1)} %bitcast.68, ...), custom_call_target="tpu_custom_call" | custom-call | flops 1179648000000 | bytes 7077888000000 | tf_op jit(solution)/shard_map/reduce_over_core/pallas_call | solution.py:129
  172.4 11.0 %attention_backward.2 = (bf16[3,1024,768]{2,1,0:T(8,128)(2,1)}, f32[8,768]{1,0:T(8,128)}) custom-call(s32[1]{0:T(128)} %bitcast.62, bf16[1024,768]{1,0:T(8,128)(2,1)} %get-tuple-element.136.q_ref.refs_1_, bf16[1024,768]{1,0:T(8,128)(2,1)} %get-tuple-element.107.k_ref.refs_2_, bf16[1024,768]{1,0:T(8,128)(2,1)} %get-tuple-element.108.v_ref.refs_3_, ...), custom_call_target="tpu_custom_call" | custom-call | flops 8589934592000 | bytes 3670016000 | tf_op jit(solution)/shard_map/attention_backward/pallas_call | solution.py:521
  183.5 4.8 %reduce_over_core.4 = (bf16[2,2,24,3840]{3,2,1,0:T(8,128)(2,1)}, bf16[2,2,24,3840]{3,2,1,0:T(8,128)(2,1)}, bf16[2,2,24,3840]{3,2,1,0:T(8,128)(2,1)}, bf16[2,2,24,3840]{3,2,1,0:T(8,128)(2,1)}) custom-call(s32[5]{0:T(128)} %stack.41.coords, bf16[2,2,4,24,3840]{4,3,2,1,0:T(8,128)(2,1)} %bitcast.64, ...), custom_call_target="tpu_custom_call" | custom-call | flops 1474560000000 | bytes 8847360000000 | tf_op jit(solution)/shard_map/reduce_over_core/pallas_call | solution.py:129
  190.6 18.7 %attention_backward.3 = (bf16[3,1024,768]{2,1,0:T(8,128)(2,1)}, f32[8,768]{1,0:T(8,128)}) custom-call(s32[1]{0:T(128)} %bitcast.63, bf16[1024,768]{1,0:T(8,128)(2,1)} %get-tuple-element.136.q_ref.refs_1_, bf16[1024,768]{1,0:T(8,128)(2,1)} %get-tuple-element.107.k_ref.refs_2_, ...), custom_call_target="tpu_custom_call", output_to_operand_aliasing={{0}: (6, {}), {1}: (7, {})} | custom-call | flops 17179869184000 | bytes 7340032000 | tf_op jit(solution)/shard_map/attention_backward/pallas_call | solution.py:521
  209.4 4.9 %reduce_over_first_link.2 = (bf16[2,24,6912]{2,1,0:T(8,128)(2,1)}, bf16[2,24,6912]{2,1,0:T(8,128)(2,1)}, bf16[2,24,6912]{2,1,0:T(8,128)(2,1)}, bf16[2,24,6912]{2,1,0:T(8,128)(2,1)}) custom-call(s32[5]{0:T(128)} %stack.41.coords, bf16[2,2,24,3072]{3,2,1,0:T(8,128)(2,1)} %get-tuple-element.139.refs_0_.refs_2_, ...), custom_call_target="tpu_custom_call" | custom-call | flops 1327104000000 | bytes 7962624000000 | tf_op jit(solution)/shard_map/reduce_over_first_link/pallas_call | solution.py:170
  216.0 8.5 %grad_qkv.1 = (bf16[16,24,2432]{2,1,0:T(8,128)(2,1)}, bf16[16,24,2432]{2,1,0:T(8,128)(2,1)}) custom-call(s32[5]{0:T(128)} %stack.41.coords, bf16[1024,768]{1,0:T(8,128)(2,1)} %left, bf16[3,1024,768]{2,1,0:T(8,128)(2,1)} %get-tuple-element.149.right.grads, f32[24,768]{1,0:T(8,128)} %get-tuple-element.128.sums, f32[8,768]{1,0:T(8,128)} %get-tuple-element.138.more), custom_call_target="tpu_custom_call" | custom-call | flops 3623878656000 | bytes 11010048000 | tf_op jit(solution)/shard_map/grad_qkv/pallas_call | solution.py:993
  231.7 3.0 %reduce_over_second_link.2 = (bf16[2,24,6912]{2,1,0:T(8,128)(2,1)}, bf16[2,24,6912]{2,1,0:T(8,128)(2,1)}) custom-call(s32[5]{0:T(128)} %stack.41.coords, bf16[2,24,6912]{2,1,0:T(8,128)(2,1)} %get-tuple-element.155.keep_a, bf16[2,24,6912]{2,1,0:T(8,128)(2,1)} %collective-permute-done.23.got_a, bf16[2,24,6912]{2,1,0:T(8,128)(2,1)} %get-tuple-element.157.keep_b, ...), custom_call_target="tpu_custom_call" | custom-call | flops 663552000000 | bytes 1990656000000 | tf_op jit(solution)/shard_map/reduce_over_second_link/pallas_call | solution.py:212
  234.8 2.8 collective-permute-start.28
  237.6 3.9 %reduce_over_core.5 = (bf16[2,2,24,2432]{3,2,1,0:T(8,128)(2,1)}, bf16[2,2,24,2432]{3,2,1,0:T(8,128)(2,1)}, bf16[2,2,24,2432]{3,2,1,0:T(8,128)(2,1)}, bf16[2,2,24,2432]{3,2,1,0:T(8,128)(2,1)}) custom-call(s32[5]{0:T(128)} %stack.41.coords, bf16[2,2,4,24,2432]{4,3,2,1,0:T(8,128)(2,1)} %bitcast.72, ...), custom_call_target="tpu_custom_call" | custom-call | flops 933888000000 | bytes 5603328000000 | tf_op jit(solution)/shard_map/reduce_over_core/pallas_call | solution.py:129
  242.4 8.7 %frames_gradient.1 = bf16[1024,768]{1,0:T(8,128)(2,1)} custom-call(f32[1024,768]{1,0:T(8,128)} %get-tuple-element.163.first_g, bf16[3,1024,768]{2,1,0:T(8,128)(2,1)} %get-tuple-element.149.right.grads, bf16[3,768,768]{2,1,0:T(8,128)(2,1)} %get-tuple-element.164.weights), custom_call_target="tpu_custom_call" | custom-call | flops 3623878656000 | bytes 12976128000 | tf_op jit(solution)/shard_map/frames_gradient/pallas_call | solution.py:1031
  255.2 3.3 %reduce_over_first_link.3 = (bf16[2,24,2432]{2,1,0:T(8,128)(2,1)}, bf16[2,24,2432]{2,1,0:T(8,128)(2,1)}, bf16[2,24,2432]{2,1,0:T(8,128)(2,1)}, bf16[2,24,2432]{2,1,0:T(8,128)(2,1)}) custom-call(s32[5]{0:T(128)} %stack.41.coords, bf16[2,2,24,2432]{3,2,1,0:T(8,128)(2,1)} %get-tuple-element.172.refs_0_.refs_2_, ...), custom_call_target="tpu_custom_call" | custom-call | flops 466944000 | bytes 2801664000 | tf_op jit(solution)/shard_map/reduce_over_first_link/pallas_call | solution.py:170
  260.0 5.6 %collective-permute-done.29.got_a = bf16[2,24,2432]{2,1,0:T(8,128)(2,1)S(1)} collective-permute-done((bf16[2,24,2432]{2,1,0:T(8,128)(2,1)}, bf16[2,24,2432]{2,1,0:T(8,128)(2,1)S(1)}, u32[]{:S(2)}, u32[]{:S(2)}) %collective-permute-start.29) | collective-permute-done | bytes 233504 | tf_op jit(solution)/shard_map/ppermute | solution.py:67
  269.0 3.3 %collective-permute-done.34 = bf16[24,6912]{1,0:T(8,128)(2,1)S(1)} collective-permute-done((bf16[24,6912]{1,0:T(8,128)(2,1)}, bf16[24,6912]{1,0:T(8,128)(2,1)S(1)}, u32[]{:S(2)}, u32[]{:S(2)}) %collective-permute-start.34) | collective-permute-done | bytes 331808 | tf_op jit(solution)/shard_map/ppermute | solution.py:79
  280.5 3.2 %collective-permute-done.32 = bf16[24,2432]{1,0:T(8,128)(2,1)S(1)} collective-permute-done((bf16[24,2432]{1,0:T(8,128)(2,1)}, bf16[24,2432]{1,0:T(8,128)(2,1)S(1)}, u32[]{:S(2)}, u32[]{:S(2)}) %collective-permute-start.32) | collective-permute-done | bytes 116768 | tf_op jit(solution)/shard_map/ppermute | solution.py:75
  (164 shorter events, 61.1 us)
Async XLA Ops:
  7.2 98.0 %all-gather.4.cloned.1.call-start = ((), (), s32[]{:S(2)}) async-start(), calls=%async_computation | async-start | bytes 11354112 | tf_op jit(solution)/shard_map/all_gather | solution.py:1097
  11.2 198.2 %all-gather.6.cloned.1.call-start = ((), (), s32[]{:S(2)}) async-start(), calls=%async_computation.1 | async-start | bytes 2433024 | tf_op jit(solution)/shard_map/all_gather | solution.py:1130
  14.3 10.6 %collective-permute-start.5 = (bf16[24,2432]{1,0:T(8,128)(2,1)}, bf16[24,2432]{1,0:T(8,128)(2,1)S(1)}, u32[]{:S(2)}, u32[]{:S(2)}) collective-permute-start(bf16[24,2432]{1,0:T(8,128)(2,1)} %get-tuple-element.105), channel_id=1, source_target_pairs={{0,6},{1,7},{2,0},{3,1},{4,2},{5,3},{6,4},{7,5},{8,14},{9,15},{10,... | collective-permute-start | bytes 350216 | tf_op jit(solution)/shard_map/ppermute | solution.py:75
  16.4 11.3 %collective-permute-start.4 = (bf16[24,2432]{1,0:T(8,128)(2,1)}, bf16[24,2432]{1,0:T(8,128)(2,1)S(1)}, u32[]{:S(2)}, u32[]{:S(2)}) collective-permute-start(bf16[24,2432]{1,0:T(8,128)(2,1)} %get-tuple-element.105), channel_id=1, source_target_pairs={{0,4},{1,5},{2,6},{3,7},{4,0},{5,1},{6,2},{7,3},{8,12},{9,13},{10,... | collective-permute-start | bytes 350216 | tf_op jit(solution)/shard_map/ppermute | solution.py:75
  21.6 11.0 %collective-permute-start.2 = (bf16[2,24,2432]{2,1,0:T(8,128)(2,1)S(1)}, bf16[2,24,2432]{2,1,0:T(8,128)(2,1)S(1)}, u32[]{:S(2)}, u32[]{:S(2)}) collective-permute-start(bf16[2,24,2432]{2,1,0:T(8,128)(2,1)S(1)} %pad_maximum_fusion.refs_0_), channel_id=1, source_target_pairs={{0,16},{8,24},{16,0},{24,8},{1,17},{9,25},{17,1},{25,9},{2,18},{10... | collective-permute-start | bytes 700424 | tf_op jit(solution)/shard_map/ppermute | solution.py:67
  23.3 10.0 %collective-permute-start.1 = (bf16[2,24,2432]{2,1,0:T(8,128)(2,1)S(1)}, bf16[2,24,2432]{2,1,0:T(8,128)(2,1)S(1)}, u32[]{:S(2)}, u32[]{:S(2)}) collective-permute-start(bf16[2,24,2432]{2,1,0:T(8,128)(2,1)S(1)} %pad_maximum_fusion.refs_0_), channel_id=1, source_target_pairs={{0,8},{8,0},{16,24},{24,16},{1,9},{9,1},{17,25},{25,17},{2,10},{10... | collective-permute-start | bytes 700424 | tf_op jit(solution)/shard_map/ppermute | solution.py:64
  27.7 9.9 %collective-permute-start.7 = (bf16[2,24,2432]{2,1,0:T(8,128)(2,1)S(1)}, bf16[2,24,2432]{2,1,0:T(8,128)(2,1)S(1)}, u32[]{:S(2)}, u32[]{:S(2)}) collective-permute-start(bf16[2,24,2432]{2,1,0:T(8,128)(2,1)S(1)} %pad_maximum_fusion.1.refs_4_), channel_id=1, source_target_pairs={{0,16},{8,24},{16,0},{24,8},{1,17},{9,25},{17,1},{25,9},{2,18},{10... | collective-permute-start | bytes 700424 | tf_op jit(solution)/shard_map/ppermute | solution.py:67
  29.4 11.4 %collective-permute-start.13 = (bf16[2,24,2432]{2,1,0:T(8,128)(2,1)S(1)}, bf16[2,24,2432]{2,1,0:T(8,128)(2,1)S(1)}, u32[]{:S(2)}, u32[]{:S(2)}) collective-permute-start(bf16[2,24,2432]{2,1,0:T(8,128)(2,1)S(1)} %pad_maximum_fusion.1.refs_4_), channel_id=1, source_target_pairs={{0,1},{1,0},{2,3},{3,2},{4,5},{5,4},{6,7},{7,6},{8,9},{9,8},{10,11... | collective-permute-start | bytes 700424 | tf_op jit(solution)/shard_map/ppermute | solution.py:70
  29.4 11.4 %collective-permute-start.6 = (bf16[2,24,2432]{2,1,0:T(8,128)(2,1)S(1)}, bf16[2,24,2432]{2,1,0:T(8,128)(2,1)S(1)}, u32[]{:S(2)}, u32[]{:S(2)}) collective-permute-start(bf16[2,24,2432]{2,1,0:T(8,128)(2,1)S(1)} %pad_maximum_fusion.1.refs_4_), channel_id=1, source_target_pairs={{0,8},{8,0},{16,24},{24,16},{1,9},{9,1},{17,25},{25,17},{2,10},{10... | collective-permute-start | bytes 700424 | tf_op jit(solution)/shard_map/ppermute | solution.py:64
  153.8 12.2 %collective-permute-start.17 = (bf16[16,24,3072]{2,1,0:T(8,128)(2,1)}, bf16[16,24,3072]{2,1,0:T(8,128)(2,1)}, u32[]{:S(2)}, u32[]{:S(2)}) collective-permute-start(bf16[16,24,3072]{2,1,0:T(8,128)(2,1)} %get-tuple-element.123), channel_id=1, source_target_pairs={{0,1},{1,0},{2,3},{3,2},{4,5},{5,4},{6,7},{7,6},{8,9},{9,8},{10,11... | collective-permute-start | bytes 7077896 | tf_op jit(solution)/shard_map/ppermute | solution.py:70
  165.6 17.9 %collective-permute-start.20 = (bf16[16,24,3840]{2,1,0:T(8,128)(2,1)}, bf16[16,24,3840]{2,1,0:T(8,128)(2,1)}, u32[]{:S(2)}, u32[]{:S(2)}) collective-permute-start(bf16[16,24,3840]{2,1,0:T(8,128)(2,1)} %get-tuple-element.134), channel_id=1, source_target_pairs={{0,1},{1,0},{2,3},{3,2},{4,5},{5,4},{6,7},{7,6},{8,9},{9,8},{10,11... | collective-permute-start | bytes 8847368 | tf_op jit(solution)/shard_map/ppermute | solution.py:70
  170.3 39.0 %collective-permute-start.18 = (bf16[2,2,24,3072]{3,2,1,0:T(8,128)(2,1)}, bf16[2,2,24,3072]{3,2,1,0:T(8,128)(2,1)}, u32[]{:S(2)}, u32[]{:S(2)}) collective-permute-start(bf16[2,2,24,3072]{3,2,1,0:T(8,128)(2,1)} %get-tuple-element.125), channel_id=1, source_target_pairs={{0,8},{8,0},{16,24},{24,16},{1,9},{9,1},{17,25},{25,17},{2,10},{10... | collective-permute-start | bytes 1769480 | tf_op jit(solution)/shard_map/ppermute | solution.py:64
  171.8 37.5 %collective-permute-start.19 = (bf16[2,2,24,3072]{3,2,1,0:T(8,128)(2,1)}, bf16[2,2,24,3072]{3,2,1,0:T(8,128)(2,1)}, u32[]{:S(2)}, u32[]{:S(2)}) collective-permute-start(bf16[2,2,24,3072]{3,2,1,0:T(8,128)(2,1)} %get-tuple-element.127), channel_id=1, source_target_pairs={{0,16},{8,24},{16,0},{24,8},{1,17},{9,25},{17,1},{25,9},{2,18},{10... | collective-permute-start | bytes 1769480 | tf_op jit(solution)/shard_map/ppermute | solution.py:67
  188.3 21.1 %collective-permute-start.21 = (bf16[2,2,24,3840]{3,2,1,0:T(8,128)(2,1)}, bf16[2,2,24,3840]{3,2,1,0:T(8,128)(2,1)}, u32[]{:S(2)}, u32[]{:S(2)}) collective-permute-start(bf16[2,2,24,3840]{3,2,1,0:T(8,128)(2,1)} %get-tuple-element.143), channel_id=1, source_target_pairs={{0,8},{8,0},{16,24},{24,16},{1,9},{9,1},{17,25},{25,17},{2,10},{10... | collective-permute-start | bytes 2211848 | tf_op jit(solution)/shard_map/ppermute | solution.py:64
  189.8 19.5 %collective-permute-start.22 = (bf16[2,2,24,3840]{3,2,1,0:T(8,128)(2,1)}, bf16[2,2,24,3840]{3,2,1,0:T(8,128)(2,1)}, u32[]{:S(2)}, u32[]{:S(2)}) collective-permute-start(bf16[2,2,24,3840]{3,2,1,0:T(8,128)(2,1)} %get-tuple-element.145), channel_id=1, source_target_pairs={{0,16},{8,24},{16,0},{24,8},{1,17},{9,25},{17,1},{25,9},{2,18},{10... | collective-permute-start | bytes 2211848 | tf_op jit(solution)/shard_map/ppermute | solution.py:67
  214.3 16.4 %collective-permute-start.23 = (bf16[2,24,6912]{2,1,0:T(8,128)(2,1)}, bf16[2,24,6912]{2,1,0:T(8,128)(2,1)}, u32[]{:S(2)}, u32[]{:S(2)}) collective-permute-start(bf16[2,24,6912]{2,1,0:T(8,128)(2,1)} %get-tuple-element.151), channel_id=1, source_target_pairs={{0,16},{8,24},{16,0},{24,8},{1,17},{9,25},{17,1},{25,9},{2,18},{10... | collective-permute-start | bytes 1990664 | tf_op jit(solution)/shard_map/ppermute | solution.py:67
  215.5 16.3 %collective-permute-start.24 = (bf16[2,24,6912]{2,1,0:T(8,128)(2,1)}, bf16[2,24,6912]{2,1,0:T(8,128)(2,1)}, u32[]{:S(2)}, u32[]{:S(2)}) collective-permute-start(bf16[2,24,6912]{2,1,0:T(8,128)(2,1)} %get-tuple-element.153), channel_id=1, source_target_pairs={{0,8},{8,0},{16,24},{24,16},{1,9},{9,1},{17,25},{25,17},{2,10},{10... | collective-permute-start | bytes 1990664 | tf_op jit(solution)/shard_map/ppermute | solution.py:64
  226.8 10.8 %collective-permute-start.25 = (bf16[16,24,2432]{2,1,0:T(8,128)(2,1)}, bf16[16,24,2432]{2,1,0:T(8,128)(2,1)}, u32[]{:S(2)}, u32[]{:S(2)}) collective-permute-start(bf16[16,24,2432]{2,1,0:T(8,128)(2,1)} %get-tuple-element.161), channel_id=1, source_target_pairs={{0,1},{1,0},{2,3},{3,2},{4,5},{5,4},{6,7},{7,6},{8,9},{9,8},{10,11... | collective-permute-start | bytes 5603336 | tf_op jit(solution)/shard_map/ppermute | solution.py:70
  234.8 18.1 %collective-permute-start.28 = (bf16[2,24,6912]{2,1,0:T(8,128)(2,1)}, bf16[2,24,6912]{2,1,0:T(8,128)(2,1)}, u32[]{:S(2)}, u32[]{:S(2)}) collective-permute-start(bf16[2,24,6912]{2,1,0:T(8,128)(2,1)} %get-tuple-element.168), channel_id=1, source_target_pairs={{0,2},{1,3},{2,0},{3,1},{4,6},{5,7},{6,4},{7,5},{8,10},{9,11},{10,... | collective-permute-start | bytes 1990664 | tf_op jit(solution)/shard_map/ppermute | solution.py:79
  241.5 13.6 %collective-permute-start.26 = (bf16[2,2,24,2432]{3,2,1,0:T(8,128)(2,1)}, bf16[2,2,24,2432]{3,2,1,0:T(8,128)(2,1)}, u32[]{:S(2)}, u32[]{:S(2)}) collective-permute-start(bf16[2,2,24,2432]{3,2,1,0:T(8,128)(2,1)} %get-tuple-element.165), channel_id=1, source_target_pairs={{0,8},{8,0},{16,24},{24,16},{1,9},{9,1},{17,25},{25,17},{2,10},{10... | collective-permute-start | bytes 1400840 | tf_op jit(solution)/shard_map/ppermute | solution.py:64
  241.9 13.3 %collective-permute-start.27 = (bf16[2,2,24,2432]{3,2,1,0:T(8,128)(2,1)}, bf16[2,2,24,2432]{3,2,1,0:T(8,128)(2,1)}, u32[]{:S(2)}, u32[]{:S(2)}) collective-permute-start(bf16[2,2,24,2432]{3,2,1,0:T(8,128)(2,1)} %get-tuple-element.167), channel_id=1, source_target_pairs={{0,16},{8,24},{16,0},{24,8},{1,17},{9,25},{17,1},{25,9},{2,18},{10... | collective-permute-start | bytes 1400840 | tf_op jit(solution)/shard_map/ppermute | solution.py:67
  255.1 17.3 %collective-permute-start.34 = (bf16[24,6912]{1,0:T(8,128)(2,1)}, bf16[24,6912]{1,0:T(8,128)(2,1)S(1)}, u32[]{:S(2)}, u32[]{:S(2)}) collective-permute-start(bf16[24,6912]{1,0:T(8,128)(2,1)} %get-tuple-element.184), channel_id=1, source_target_pairs={{0,4},{1,5},{2,6},{3,7},{4,0},{5,1},{6,2},{7,3},{8,12},{9,13},{10,... | collective-permute-start | bytes 995336 | tf_op jit(solution)/shard_map/ppermute | solution.py:79
  272.3 11.4 %collective-permute-start.32 = (bf16[24,2432]{1,0:T(8,128)(2,1)}, bf16[24,2432]{1,0:T(8,128)(2,1)S(1)}, u32[]{:S(2)}, u32[]{:S(2)}) collective-permute-start(bf16[24,2432]{1,0:T(8,128)(2,1)} %get-tuple-element.182), channel_id=1, source_target_pairs={{0,4},{1,5},{2,6},{3,7},{4,0},{5,1},{6,2},{7,3},{8,12},{9,13},{10,... | collective-permute-start | bytes 350216 | tf_op jit(solution)/shard_map/ppermute | solution.py:75
  274.0 9.7 %collective-permute-start.33 = (bf16[24,2432]{1,0:T(8,128)(2,1)}, bf16[24,2432]{1,0:T(8,128)(2,1)S(1)}, u32[]{:S(2)}, u32[]{:S(2)}) collective-permute-start(bf16[24,2432]{1,0:T(8,128)(2,1)} %get-tuple-element.183), channel_id=1, source_target_pairs={{0,6},{1,7},{2,0},{3,1},{4,2},{5,3},{6,4},{7,5},{8,14},{9,15},{10,... | collective-permute-start | bytes 350216 | tf_op jit(solution)/shard_map/ppermute | solution.py:75
  (48 other events, 364.1 us)
Sparse Core Ops, SparseCore 0:
  11.6 93.5 all-gather.3
  143.8 55.8 all-gather.5

commit v6 on v5

--- a/solution.py
+++ b/solution.py
@@ -1132,16 +1132,13 @@
         done = most.first(after(down_mine, up_mine), down_got)
         grads = attention_part(0, 2, after(queries, done))
         done = most.first(after(up_mine, grads[1]), up_got)
-        qkv_g, bias_sums = attention_part(2, 4, after(queries, done), grads)
-        most.parts[0], all_sums = after((most.parts[0], all_sums), bias_sums)
+        grads = attention_part(2, 3, after(queries, done), grads)
+        most.parts[0] = after(most.parts[0], grads[1])
         done = most.second()
-        mine, theirs = qkv_grad(
-            place, after(frames, (done, all_sums)), qkv_g, sums, bias_sums, valid
-        )
+        qkv_g, bias_sums = attention_part(5, 1, after(queries, done), grads)
+        mine, theirs = qkv_grad(place, frames, qkv_g, sums, bias_sums, valid)
         got = place.swap_core(theirs)
-        squares = jnp.sum(after(all_sums, mine)[:, 12:17], axis=(0, 2))
-        layer_rms = jnp.sqrt(squares[0:4] / squares[4])
-        most.sums = after(most.sums, (mine, layer_rms))
+        most.sums, all_sums = after((most.sums, all_sums), mine)
         done = most.third()
         last = Reduction(place)
         done = last.first(after(mine, done), got)
@@ -1149,7 +1146,10 @@
         most.sums = after(most.sums, frames_grad)
         done = most.fourth(0)
         last.parts[0] = after(last.parts[0], done)
-        last.second(1000)
+        done = last.second(1000)
+        squares = jnp.sum(after(all_sums, done)[:, 12:17], axis=(0, 2))
+        layer_rms = jnp.sqrt(squares[0:4] / squares[4])
+        last.sums = after(last.sums, layer_rms)
         done = last.spread(1000)
         most.sums = after(most.sums, done)
         grad_most = most.result()

time: 298 us -> 299 us (level)
  waiting for transfers between devices: 57.9 us -> 51.6 us
  Pallas kernels: 172 us -> 178 us
    pallas_call x2 -> x3, Pallas kernels: 29.7 us -> 36.1 us  [attention_backward(): pl.pallas_call(kernel, grid=(pairs,), in_specs=[pl.BlockSpec(memory_space...]
    ppermute x8, waiting for transfers between devices: 13.4 us -> 8.21 us  [swap_y(): return lax.ppermute(value, 'dp', [(i, i ^ 2) for i in range(self.n_dp)])]
  transfers between devices with their start and end apart: 37 -> 37, of which waited for: 17 -> 18; matrix products, arithmetic and copies ran while one was open for 3% -> 3% of each run, Pallas kernels for 43% -> 47%
where the time goes in v6:
time: 299 us; the launch traced here: 294 us
  Pallas kernels  178 us (60%)
  waiting for transfers between devices  51.6 us (17%)
  starting transfers between devices  33.3 us (11%)
  between operations  15 us (5%)
  other arithmetic  10.5 us (4%)
  local copies, waits for them, and re-layouts  5.16 us (2%)
    pallas_call x1, Pallas kernels, middle(): pl.pallas_call(partial(middle_kernel, packed, last_rows), grid=(tiles + 1...  38.7 us
    pallas_call x3, Pallas kernels, attention_backward(): pl.pallas_call(kernel, grid=(pairs,), in_specs=[pl.BlockSpec(memory_space...  36.1 us
    pallas_call x1, Pallas kernels, attention_forward(): pl.pallas_call(attention_forward_kernel, grid=(pairs,), in_specs=[column]...  25.2 us
    all_gather x1, waiting for transfers between devices, shards(): wire = lax.all_gather(wire_low, AXES, axis=0, tiled=True)  24 us
    pallas_call x3, Pallas kernels, first_add(): pl.pallas_call(first_add_kernel, grid_spec=pltpu.PrefetchScalarGridSpec(n...  13.1 us
    pallas_call x1, Pallas kernels, up_grad(): pl.pallas_call(partial(up_grad_kernel, valid, rows), grid_spec=pltpu.Pref...  11.5 us
    ppermute x6, waiting for transfers between devices, shift_z(): return lax.ppermute(value, 'fsdp', pairs)  10.8 us
    ppermute x8, starting transfers between devices, swap_x(): return lax.ppermute(value, 'dp', [(i, i ^ 1) for i in range(self.n_dp)])  10.7 us
  transfers between devices with their start and end apart: 37, of which 18 were waited for; matrix products, arithmetic and copies ran while one was open for 3% of the time, Pallas kernels for 47%

profile of v6, /device:TPU:0, one launch (start us, length us, event | category | flops | bytes accessed | tf_op | source)
XLA Modules:
  0.0 293.7 jit_solution(14152584492116036627)
XLA Ops:
  11.2 3.1 %collective-permute-start = (bf16[24,2432]{1,0:T(8,128)(2,1)}, bf16[24,2432]{1,0:T(8,128)(2,1)S(1)}, u32[]{:S(2)}, u32[]{:S(2)}) collective-permute-start(bf16[24,2432]{1,0:T(8,128)(2,1)} %get-tuple-element.111), channel_id=1, source_target_pairs={{0,2},{1,3},{2,4},{3,5},{4,6},{5,7},{6,0},{7,1},{8,10},{9,11},{10,... | collective-permute-start | bytes 350216 | tf_op jit(solution)/shard_map/ppermute | solution.py:75
  17.3 3.2 %collective-permute-done = bf16[24,2432]{1,0:T(8,128)(2,1)S(1)} collective-permute-done((bf16[24,2432]{1,0:T(8,128)(2,1)}, bf16[24,2432]{1,0:T(8,128)(2,1)S(1)}, u32[]{:S(2)}, u32[]{:S(2)}) %collective-permute-start) | collective-permute-done | bytes 116768 | tf_op jit(solution)/shard_map/ppermute | solution.py:75
  24.8 2.8 collective-permute-done.4
  34.5 3.1 %collective-permute-done.7.refs_6_ = bf16[2,24,2432]{2,1,0:T(8,128)(2,1)S(1)} collective-permute-done((bf16[2,24,2432]{2,1,0:T(8,128)(2,1)S(1)}, bf16[2,24,2432]{2,1,0:T(8,128)(2,1)S(1)}, u32[]{:S(2)}, u32[]{:S(2)}) %collective-permute-start.7) | collective-permute-done | bytes 233504 | tf_op jit(solution)/shard_map/ppermute | solution.py:67
  42.1 2.4 collective-permute-done.8.refs_7_
  47.2 8.8 %project_qkv.1 = (bf16[1024,768]{1,0:T(8,128)(2,1)}, bf16[1024,768]{1,0:T(8,128)(2,1)}, bf16[1024,768]{1,0:T(8,128)(2,1)}, f32[16,768]{1,0:T(8,128)}, bf16[3,768,768]{2,1,0:T(8,128)(2,1)}) custom-call(s32[5]{0:T(128)} %stack.41.coords, bf16[1024,768]{1,0:T(8,128)(2,1)} %left.1, bf16[2,24,2432]{2,1,0:T(8,128)(2,1)} %copy-done.9, ...), custom_call_target="tpu_custom_call" | custom-call | flops 3623878656 | bytes 7864320 | tf_op jit(solution)/shard_map/project_qkv/pallas_call | solution.py:371
  56.0 25.2 %attention_forward.1 = (bf16[1024,768]{1,0:T(8,128)(2,1)}, bf16[6,2,912,1024]{3,2,1,0:T(8,128)(2,1)}) custom-call(bf16[1024,768]{1,0:T(8,128)(2,1)} %get-tuple-element.152.q_ref.refs_1_, bf16[1024,768]{1,0:T(8,128)(2,1)} %get-tuple-element.113.k_ref.refs_2_, bf16[1024,768]{1,0:T(8,128)(2,1)} %get-tuple-element.114.v_ref.refs_3_, ...), custom_call_target="tpu_custom_call" | custom-call | flops 12884901888 | bytes 6291456 | tf_op jit(solution)/shard_map/attention_forward/pallas_call | solution.py:417
  81.2 24.0 %all-gather.4.cloned.1.call-done.refs_0_ = bf16[3072,1792]{1,0:T(8,128)(2,1)} async-done(((bf16[96,1792]{1,0:T(8,128)(2,1)}), bf16[3072,1792]{1,0:T(8,128)(2,1)}) %all-gather.4.cloned.1.call-update) | async-done | bytes 11010064 | tf_op jit(solution)/shard_map/all_gather | solution.py:1097
  105.2 38.7 %feed_forward.1 = (bf16[1024,768]{1,0:T(8,128)(2,1)}, bf16[1024,768]{1,0:T(8,128)(2,1)}, bf16[1024,3072]{1,0:T(8,128)(2,1)}, bf16[1024,768]{1,0:T(8,128)(2,1)}, ...) custom-call(s32[1]{0:T(128)} %bitcast.1.total_ref, ...), custom_call_target="tpu_custom_call" | custom-call | flops 21743271936000 | bytes 33030144000 | tf_op jit(solution)/shard_map/feed_forward/pallas_call | solution.py:774
  143.9 10.1 %grad_down.1 = (bf16[16,24,3072]{2,1,0:T(8,128)(2,1)}, bf16[16,24,3072]{2,1,0:T(8,128)(2,1)}) custom-call(s32[5]{0:T(128)} %stack.41.coords, bf16[1024,3072]{1,0:T(8,128)(2,1)} %get-tuple-element.120.left, bf16[1024,768]{1,0:T(8,128)(2,1)} %get-tuple-element.121.right), custom_call_target="tpu_custom_call" | custom-call | flops 4831838208000 | bytes 7864320000 | tf_op jit(solution)/shard_map/grad_down/pallas_call | solution.py:848
  154.3 11.5 %grad_up_and_out.1 = (bf16[16,24,3840]{2,1,0:T(8,128)(2,1)}, bf16[16,24,3840]{2,1,0:T(8,128)(2,1)}) custom-call(s32[5]{0:T(128)} %stack.41.coords, bf16[1024,768]{1,0:T(8,128)(2,1)} %get-tuple-element.124.left, bf16[1024,3072]{1,0:T(8,128)(2,1)} %get-tuple-element.125.right, bf16[1024,768]{1,0:T(8,128)(2,1)} %get-tuple-element.115.context.out_left, ...), custom_call_target="tpu_custom_call" | custom-call | flops 6039797760000 | bytes 16515072000 | tf_op jit(solution)/shard_map/grad_up_and_out/pallas_call | solution.py:905
  166.1 4.3 %reduce_over_core.3 = (bf16[2,2,24,3072]{3,2,1,0:T(8,128)(2,1)}, bf16[2,2,24,3072]{3,2,1,0:T(8,128)(2,1)}, bf16[2,2,24,3072]{3,2,1,0:T(8,128)(2,1)}, bf16[2,2,24,3072]{3,2,1,0:T(8,128)(2,1)}) custom-call(s32[5]{0:T(128)} %stack.41.coords, bf16[2,2,4,24,3072]{4,3,2,1,0:T(8,128)(2,1)} %bitcast.69, ...), custom_call_target="tpu_custom_call" | custom-call | flops 1179648000000 | bytes 7077888000000 | tf_op jit(solution)/shard_map/reduce_over_core/pallas_call | solution.py:129
  172.6 11.9 %attention_backward.3 = (bf16[3,1024,768]{2,1,0:T(8,128)(2,1)}, f32[8,768]{1,0:T(8,128)}) custom-call(s32[1]{0:T(128)} %bitcast.62, bf16[1024,768]{1,0:T(8,128)(2,1)} %get-tuple-element.152.q_ref.refs_1_, bf16[1024,768]{1,0:T(8,128)(2,1)} %get-tuple-element.113.k_ref.refs_2_, bf16[1024,768]{1,0:T(8,128)(2,1)} %get-tuple-element.114.v_ref.refs_3_, ...), custom_call_target="tpu_custom_call" | custom-call | flops 8589934592000 | bytes 3670016000 | tf_op jit(solution)/shard_map/attention_backward/pallas_call | solution.py:521
  184.5 4.8 %reduce_over_core.4 = (bf16[2,2,24,3840]{3,2,1,0:T(8,128)(2,1)}, bf16[2,2,24,3840]{3,2,1,0:T(8,128)(2,1)}, bf16[2,2,24,3840]{3,2,1,0:T(8,128)(2,1)}, bf16[2,2,24,3840]{3,2,1,0:T(8,128)(2,1)}) custom-call(s32[5]{0:T(128)} %stack.41.coords, bf16[2,2,4,24,3840]{4,3,2,1,0:T(8,128)(2,1)} %bitcast.65, ...), custom_call_target="tpu_custom_call" | custom-call | flops 1474560000000 | bytes 8847360000000 | tf_op jit(solution)/shard_map/reduce_over_core/pallas_call | solution.py:129
  190.9 16.1 %attention_backward.4 = (bf16[3,1024,768]{2,1,0:T(8,128)(2,1)}, f32[8,768]{1,0:T(8,128)}) custom-call(s32[1]{0:T(128)} %bitcast.63, bf16[1024,768]{1,0:T(8,128)(2,1)} %get-tuple-element.152.q_ref.refs_1_, bf16[1024,768]{1,0:T(8,128)(2,1)} %get-tuple-element.113.k_ref.refs_2_, ...), custom_call_target="tpu_custom_call", output_to_operand_aliasing={{0}: (6, {}), {1}: (7, {})} | custom-call | flops 12884901888000 | bytes 5505024000 | tf_op jit(solution)/shard_map/attention_backward/pallas_call | solution.py:521
  208.5 4.9 %reduce_over_first_link.2 = (bf16[2,24,6912]{2,1,0:T(8,128)(2,1)}, bf16[2,24,6912]{2,1,0:T(8,128)(2,1)}, bf16[2,24,6912]{2,1,0:T(8,128)(2,1)}, bf16[2,24,6912]{2,1,0:T(8,128)(2,1)}) custom-call(s32[5]{0:T(128)} %stack.41.coords, bf16[2,2,24,3072]{3,2,1,0:T(8,128)(2,1)} %get-tuple-element.144.refs_0_.refs_2_, ...), custom_call_target="tpu_custom_call" | custom-call | flops 1327104000000 | bytes 7962624000000 | tf_op jit(solution)/shard_map/reduce_over_first_link/pallas_call | solution.py:170
  215.4 8.1 %attention_backward.5 = (bf16[3,1024,768]{2,1,0:T(8,128)(2,1)}, f32[8,768]{1,0:T(8,128)}) custom-call(s32[1]{0:T(128)} %bitcast.64, bf16[1024,768]{1,0:T(8,128)(2,1)} %get-tuple-element.152.q_ref.refs_1_, bf16[1024,768]{1,0:T(8,128)(2,1)} %get-tuple-element.113.k_ref.refs_2_, ...), custom_call_target="tpu_custom_call", output_to_operand_aliasing={{0}: (6, {}), {1}: (7, {})} | custom-call | flops 4294967296000 | bytes 1835008000 | tf_op jit(solution)/shard_map/attention_backward/pallas_call | solution.py:521
  223.5 8.6 %grad_qkv.1 = (bf16[16,24,2432]{2,1,0:T(8,128)(2,1)}, bf16[16,24,2432]{2,1,0:T(8,128)(2,1)}) custom-call(s32[5]{0:T(128)} %stack.41.coords, bf16[1024,768]{1,0:T(8,128)(2,1)} %left.1, bf16[3,1024,768]{2,1,0:T(8,128)(2,1)} %get-tuple-element.154.right.grads, f32[24,768]{1,0:T(8,128)} %get-tuple-element.155.sums, f32[8,768]{1,0:T(8,128)} %get-tuple-element.156.more), custom_call_target="tpu_custom_call" | custom-call | flops 3623878656000 | bytes 11010048000 | tf_op jit(solution)/shard_map/grad_qkv/pallas_call | solution.py:993
  232.2 3.0 %reduce_over_second_link.2 = (bf16[2,24,6912]{2,1,0:T(8,128)(2,1)}, bf16[2,24,6912]{2,1,0:T(8,128)(2,1)}) custom-call(s32[5]{0:T(128)} %stack.41.coords, bf16[2,24,6912]{2,1,0:T(8,128)(2,1)} %get-tuple-element.161.keep_a, bf16[2,24,6912]{2,1,0:T(8,128)(2,1)} %collective-permute-done.23.got_a, bf16[2,24,6912]{2,1,0:T(8,128)(2,1)} %get-tuple-element.163.keep_b, ...), custom_call_target="tpu_custom_call" | custom-call | flops 663552000000 | bytes 1990656000000 | tf_op jit(solution)/shard_map/reduce_over_second_link/pallas_call | solution.py:212
  236.3 3.9 %reduce_over_core.5 = (bf16[2,2,24,2432]{3,2,1,0:T(8,128)(2,1)}, bf16[2,2,24,2432]{3,2,1,0:T(8,128)(2,1)}, bf16[2,2,24,2432]{3,2,1,0:T(8,128)(2,1)}, bf16[2,2,24,2432]{3,2,1,0:T(8,128)(2,1)}) custom-call(s32[5]{0:T(128)} %stack.41.coords, bf16[2,2,4,24,2432]{4,3,2,1,0:T(8,128)(2,1)} %bitcast.73, ...), custom_call_target="tpu_custom_call" | custom-call | flops 933888000000 | bytes 5603328000000 | tf_op jit(solution)/shard_map/reduce_over_core/pallas_call | solution.py:129
  242.5 8.5 %frames_gradient.1 = bf16[1024,768]{1,0:T(8,128)(2,1)} custom-call(f32[1024,768]{1,0:T(8,128)} %get-tuple-element.169.first_g, bf16[3,1024,768]{2,1,0:T(8,128)(2,1)} %get-tuple-element.154.right.grads, bf16[3,768,768]{2,1,0:T(8,128)(2,1)} %get-tuple-element.170.weights), custom_call_target="tpu_custom_call" | custom-call | flops 3623878656000 | bytes 12976128000 | tf_op jit(solution)/shard_map/frames_gradient/pallas_call | solution.py:1031
  256.4 3.2 %reduce_over_first_link.3 = (bf16[2,24,2432]{2,1,0:T(8,128)(2,1)}, bf16[2,24,2432]{2,1,0:T(8,128)(2,1)}, bf16[2,24,2432]{2,1,0:T(8,128)(2,1)}, bf16[2,24,2432]{2,1,0:T(8,128)(2,1)}) custom-call(s32[5]{0:T(128)} %stack.41.coords, bf16[2,2,24,2432]{3,2,1,0:T(8,128)(2,1)} %get-tuple-element.179.refs_0_.refs_2_, ...), custom_call_target="tpu_custom_call" | custom-call | flops 466944000 | bytes 2801664000 | tf_op jit(solution)/shard_map/reduce_over_first_link/pallas_call | solution.py:170
  270.1 2.6 collective-permute-done.34
  280.8 3.8 %collective-permute-done.32 = bf16[24,2432]{1,0:T(8,128)(2,1)S(1)} collective-permute-done((bf16[24,2432]{1,0:T(8,128)(2,1)}, bf16[24,2432]{1,0:T(8,128)(2,1)S(1)}, u32[]{:S(2)}, u32[]{:S(2)}) %collective-permute-start.32) | collective-permute-done | bytes 116768 | tf_op jit(solution)/shard_map/ppermute | solution.py:75
  (165 shorter events, 62.1 us)
Async XLA Ops:
  7.2 98.0 %all-gather.4.cloned.1.call-start = ((), (), s32[]{:S(2)}) async-start(), calls=%async_computation | async-start | bytes 11354112 | tf_op jit(solution)/shard_map/all_gather | solution.py:1097
  11.2 221.0 %all-gather.6.cloned.1.call-start = ((), (), s32[]{:S(2)}) async-start(), calls=%async_computation.1 | async-start | bytes 2433024 | tf_op jit(solution)/shard_map/all_gather | solution.py:1130
  11.2 9.3 %collective-permute-start = (bf16[24,2432]{1,0:T(8,128)(2,1)}, bf16[24,2432]{1,0:T(8,128)(2,1)S(1)}, u32[]{:S(2)}, u32[]{:S(2)}) collective-permute-start(bf16[24,2432]{1,0:T(8,128)(2,1)} %get-tuple-element.111), channel_id=1, source_target_pairs={{0,2},{1,3},{2,4},{3,5},{4,6},{5,7},{6,0},{7,1},{8,10},{9,11},{10,... | collective-permute-start | bytes 350216 | tf_op jit(solution)/shard_map/ppermute | solution.py:75
  14.3 10.6 %collective-permute-start.5 = (bf16[24,2432]{1,0:T(8,128)(2,1)}, bf16[24,2432]{1,0:T(8,128)(2,1)S(1)}, u32[]{:S(2)}, u32[]{:S(2)}) collective-permute-start(bf16[24,2432]{1,0:T(8,128)(2,1)} %get-tuple-element.111), channel_id=1, source_target_pairs={{0,6},{1,7},{2,0},{3,1},{4,2},{5,3},{6,4},{7,5},{8,14},{9,15},{10,... | collective-permute-start | bytes 350216 | tf_op jit(solution)/shard_map/ppermute | solution.py:75
  16.4 11.3 %collective-permute-start.4 = (bf16[24,2432]{1,0:T(8,128)(2,1)}, bf16[24,2432]{1,0:T(8,128)(2,1)S(1)}, u32[]{:S(2)}, u32[]{:S(2)}) collective-permute-start(bf16[24,2432]{1,0:T(8,128)(2,1)} %get-tuple-element.111), channel_id=1, source_target_pairs={{0,4},{1,5},{2,6},{3,7},{4,0},{5,1},{6,2},{7,3},{8,12},{9,13},{10,... | collective-permute-start | bytes 350216 | tf_op jit(solution)/shard_map/ppermute | solution.py:75
  21.6 11.0 %collective-permute-start.2 = (bf16[2,24,2432]{2,1,0:T(8,128)(2,1)S(1)}, bf16[2,24,2432]{2,1,0:T(8,128)(2,1)S(1)}, u32[]{:S(2)}, u32[]{:S(2)}) collective-permute-start(bf16[2,24,2432]{2,1,0:T(8,128)(2,1)S(1)} %pad_maximum_fusion.refs_0_), channel_id=1, source_target_pairs={{0,16},{8,24},{16,0},{24,8},{1,17},{9,25},{17,1},{25,9},{2,18},{10... | collective-permute-start | bytes 700424 | tf_op jit(solution)/shard_map/ppermute | solution.py:67
  23.3 10.0 %collective-permute-start.1 = (bf16[2,24,2432]{2,1,0:T(8,128)(2,1)S(1)}, bf16[2,24,2432]{2,1,0:T(8,128)(2,1)S(1)}, u32[]{:S(2)}, u32[]{:S(2)}) collective-permute-start(bf16[2,24,2432]{2,1,0:T(8,128)(2,1)S(1)} %pad_maximum_fusion.refs_0_), channel_id=1, source_target_pairs={{0,8},{8,0},{16,24},{24,16},{1,9},{9,1},{17,25},{25,17},{2,10},{10... | collective-permute-start | bytes 700424 | tf_op jit(solution)/shard_map/ppermute | solution.py:64
  27.7 9.9 %collective-permute-start.7 = (bf16[2,24,2432]{2,1,0:T(8,128)(2,1)S(1)}, bf16[2,24,2432]{2,1,0:T(8,128)(2,1)S(1)}, u32[]{:S(2)}, u32[]{:S(2)}) collective-permute-start(bf16[2,24,2432]{2,1,0:T(8,128)(2,1)S(1)} %pad_maximum_fusion.1.refs_4_), channel_id=1, source_target_pairs={{0,16},{8,24},{16,0},{24,8},{1,17},{9,25},{17,1},{25,9},{2,18},{10... | collective-permute-start | bytes 700424 | tf_op jit(solution)/shard_map/ppermute | solution.py:67
  29.4 11.4 %collective-permute-start.13 = (bf16[2,24,2432]{2,1,0:T(8,128)(2,1)S(1)}, bf16[2,24,2432]{2,1,0:T(8,128)(2,1)S(1)}, u32[]{:S(2)}, u32[]{:S(2)}) collective-permute-start(bf16[2,24,2432]{2,1,0:T(8,128)(2,1)S(1)} %pad_maximum_fusion.1.refs_4_), channel_id=1, source_target_pairs={{0,1},{1,0},{2,3},{3,2},{4,5},{5,4},{6,7},{7,6},{8,9},{9,8},{10,11... | collective-permute-start | bytes 700424 | tf_op jit(solution)/shard_map/ppermute | solution.py:70
  29.4 11.4 %collective-permute-start.6 = (bf16[2,24,2432]{2,1,0:T(8,128)(2,1)S(1)}, bf16[2,24,2432]{2,1,0:T(8,128)(2,1)S(1)}, u32[]{:S(2)}, u32[]{:S(2)}) collective-permute-start(bf16[2,24,2432]{2,1,0:T(8,128)(2,1)S(1)} %pad_maximum_fusion.1.refs_4_), channel_id=1, source_target_pairs={{0,8},{8,0},{16,24},{24,16},{1,9},{9,1},{17,25},{25,17},{2,10},{10... | collective-permute-start | bytes 700424 | tf_op jit(solution)/shard_map/ppermute | solution.py:64
  154.0 12.1 %collective-permute-start.17 = (bf16[16,24,3072]{2,1,0:T(8,128)(2,1)}, bf16[16,24,3072]{2,1,0:T(8,128)(2,1)}, u32[]{:S(2)}, u32[]{:S(2)}) collective-permute-start(bf16[16,24,3072]{2,1,0:T(8,128)(2,1)} %get-tuple-element.129), channel_id=1, source_target_pairs={{0,1},{1,0},{2,3},{3,2},{4,5},{5,4},{6,7},{7,6},{8,9},{9,8},{10,11... | collective-permute-start | bytes 7077896 | tf_op jit(solution)/shard_map/ppermute | solution.py:70
  165.8 18.7 %collective-permute-start.20 = (bf16[16,24,3840]{2,1,0:T(8,128)(2,1)}, bf16[16,24,3840]{2,1,0:T(8,128)(2,1)}, u32[]{:S(2)}, u32[]{:S(2)}) collective-permute-start(bf16[16,24,3840]{2,1,0:T(8,128)(2,1)} %get-tuple-element.139), channel_id=1, source_target_pairs={{0,1},{1,0},{2,3},{3,2},{4,5},{5,4},{6,7},{7,6},{8,9},{9,8},{10,11... | collective-permute-start | bytes 8847368 | tf_op jit(solution)/shard_map/ppermute | solution.py:70
  170.5 36.5 %collective-permute-start.18 = (bf16[2,2,24,3072]{3,2,1,0:T(8,128)(2,1)}, bf16[2,2,24,3072]{3,2,1,0:T(8,128)(2,1)}, u32[]{:S(2)}, u32[]{:S(2)}) collective-permute-start(bf16[2,2,24,3072]{3,2,1,0:T(8,128)(2,1)} %get-tuple-element.131), channel_id=1, source_target_pairs={{0,8},{8,0},{16,24},{24,16},{1,9},{9,1},{17,25},{25,17},{2,10},{10... | collective-permute-start | bytes 1769480 | tf_op jit(solution)/shard_map/ppermute | solution.py:64
  172.0 35.0 %collective-permute-start.19 = (bf16[2,2,24,3072]{3,2,1,0:T(8,128)(2,1)}, bf16[2,2,24,3072]{3,2,1,0:T(8,128)(2,1)}, u32[]{:S(2)}, u32[]{:S(2)}) collective-permute-start(bf16[2,2,24,3072]{3,2,1,0:T(8,128)(2,1)} %get-tuple-element.133), channel_id=1, source_target_pairs={{0,16},{8,24},{16,0},{24,8},{1,17},{9,25},{17,1},{25,9},{2,18},{10... | collective-permute-start | bytes 1769480 | tf_op jit(solution)/shard_map/ppermute | solution.py:67
  189.3 17.8 %collective-permute-start.21 = (bf16[2,2,24,3840]{3,2,1,0:T(8,128)(2,1)}, bf16[2,2,24,3840]{3,2,1,0:T(8,128)(2,1)}, u32[]{:S(2)}, u32[]{:S(2)}) collective-permute-start(bf16[2,2,24,3840]{3,2,1,0:T(8,128)(2,1)} %get-tuple-element.148), channel_id=1, source_target_pairs={{0,8},{8,0},{16,24},{24,16},{1,9},{9,1},{17,25},{25,17},{2,10},{10... | collective-permute-start | bytes 2211848 | tf_op jit(solution)/shard_map/ppermute | solution.py:64
  190.1 18.4 %collective-permute-start.22 = (bf16[2,2,24,3840]{3,2,1,0:T(8,128)(2,1)}, bf16[2,2,24,3840]{3,2,1,0:T(8,128)(2,1)}, u32[]{:S(2)}, u32[]{:S(2)}) collective-permute-start(bf16[2,2,24,3840]{3,2,1,0:T(8,128)(2,1)} %get-tuple-element.150), channel_id=1, source_target_pairs={{0,16},{8,24},{16,0},{24,8},{1,17},{9,25},{17,1},{25,9},{2,18},{10... | collective-permute-start | bytes 2211848 | tf_op jit(solution)/shard_map/ppermute | solution.py:67
  213.4 18.8 %collective-permute-start.23 = (bf16[2,24,6912]{2,1,0:T(8,128)(2,1)}, bf16[2,24,6912]{2,1,0:T(8,128)(2,1)}, u32[]{:S(2)}, u32[]{:S(2)}) collective-permute-start(bf16[2,24,6912]{2,1,0:T(8,128)(2,1)} %get-tuple-element.158), channel_id=1, source_target_pairs={{0,16},{8,24},{16,0},{24,8},{1,17},{9,25},{17,1},{25,9},{2,18},{10... | collective-permute-start | bytes 1990664 | tf_op jit(solution)/shard_map/ppermute | solution.py:67
  214.0 18.2 %collective-permute-start.24 = (bf16[2,24,6912]{2,1,0:T(8,128)(2,1)}, bf16[2,24,6912]{2,1,0:T(8,128)(2,1)}, u32[]{:S(2)}, u32[]{:S(2)}) collective-permute-start(bf16[2,24,6912]{2,1,0:T(8,128)(2,1)} %get-tuple-element.160), channel_id=1, source_target_pairs={{0,8},{8,0},{16,24},{24,16},{1,9},{9,1},{17,25},{25,17},{2,10},{10... | collective-permute-start | bytes 1990664 | tf_op jit(solution)/shard_map/ppermute | solution.py:64
  235.2 17.6 %collective-permute-start.28 = (bf16[2,24,6912]{2,1,0:T(8,128)(2,1)}, bf16[2,24,6912]{2,1,0:T(8,128)(2,1)}, u32[]{:S(2)}, u32[]{:S(2)}) collective-permute-start(bf16[2,24,6912]{2,1,0:T(8,128)(2,1)} %get-tuple-element.175), channel_id=1, source_target_pairs={{0,2},{1,3},{2,0},{3,1},{4,6},{5,7},{6,4},{7,5},{8,10},{9,11},{10,... | collective-permute-start | bytes 1990664 | tf_op jit(solution)/shard_map/ppermute | solution.py:79
  240.2 16.2 %collective-permute-start.26 = (bf16[2,2,24,2432]{3,2,1,0:T(8,128)(2,1)}, bf16[2,2,24,2432]{3,2,1,0:T(8,128)(2,1)}, u32[]{:S(2)}, u32[]{:S(2)}) collective-permute-start(bf16[2,2,24,2432]{3,2,1,0:T(8,128)(2,1)} %get-tuple-element.172), channel_id=1, source_target_pairs={{0,8},{8,0},{16,24},{24,16},{1,9},{9,1},{17,25},{25,17},{2,10},{10... | collective-permute-start | bytes 1400840 | tf_op jit(solution)/shard_map/ppermute | solution.py:64
  240.8 15.6 %collective-permute-start.27 = (bf16[2,2,24,2432]{3,2,1,0:T(8,128)(2,1)}, bf16[2,2,24,2432]{3,2,1,0:T(8,128)(2,1)}, u32[]{:S(2)}, u32[]{:S(2)}) collective-permute-start(bf16[2,2,24,2432]{3,2,1,0:T(8,128)(2,1)} %get-tuple-element.174), channel_id=1, source_target_pairs={{0,16},{8,24},{16,0},{24,8},{1,17},{9,25},{17,1},{25,9},{2,18},{10... | collective-permute-start | bytes 1400840 | tf_op jit(solution)/shard_map/ppermute | solution.py:67
  255.1 17.6 %collective-permute-start.34 = (bf16[24,6912]{1,0:T(8,128)(2,1)}, bf16[24,6912]{1,0:T(8,128)(2,1)S(1)}, u32[]{:S(2)}, u32[]{:S(2)}) collective-permute-start(bf16[24,6912]{1,0:T(8,128)(2,1)} %get-tuple-element.196), channel_id=1, source_target_pairs={{0,4},{1,5},{2,6},{3,7},{4,0},{5,1},{6,2},{7,3},{8,12},{9,13},{10,... | collective-permute-start | bytes 995336 | tf_op jit(solution)/shard_map/ppermute | solution.py:79
  272.7 11.9 %collective-permute-start.32 = (bf16[24,2432]{1,0:T(8,128)(2,1)}, bf16[24,2432]{1,0:T(8,128)(2,1)S(1)}, u32[]{:S(2)}, u32[]{:S(2)}) collective-permute-start(bf16[24,2432]{1,0:T(8,128)(2,1)} %get-tuple-element.194), channel_id=1, source_target_pairs={{0,4},{1,5},{2,6},{3,7},{4,0},{5,1},{6,2},{7,3},{8,12},{9,13},{10,... | collective-permute-start | bytes 350216 | tf_op jit(solution)/shard_map/ppermute | solution.py:75
  274.3 10.3 %collective-permute-start.33 = (bf16[24,2432]{1,0:T(8,128)(2,1)}, bf16[24,2432]{1,0:T(8,128)(2,1)S(1)}, u32[]{:S(2)}, u32[]{:S(2)}) collective-permute-start(bf16[24,2432]{1,0:T(8,128)(2,1)} %get-tuple-element.195), channel_id=1, source_target_pairs={{0,6},{1,7},{2,0},{3,1},{4,2},{5,3},{6,4},{7,5},{8,14},{9,15},{10,... | collective-permute-start | bytes 350216 | tf_op jit(solution)/shard_map/ppermute | solution.py:75
  (48 other events, 348.2 us)
Sparse Core Ops, SparseCore 0:
  11.6 93.5 all-gather.3
  144.0 55.9 all-gather.5
